TPU v7x, 128 devices: a whole 4x4x4 slice. The times are simulated.
128 devices in a mesh: pos: 64 (over z, y, x), head: 2 (over core).
Axes of the slice: x: 4, y: 4, z: 4, core: 2. Of those that a mesh axis runs over, the one named last changes fastest.
Arguments:
- queries: bfloat16 [2, 8192, 4096], P(None, 'pos', 'head'), may hold values from -40 to 40
- keys_values: bfloat16 [2, 2, 8192, 512], P(None, None, 'pos', 'head'), may hold values from -10 to 10
- d_out: bfloat16 [2, 8192, 4096], P(None, 'pos', 'head'), may hold values from -6 to 6
- doc_start: int32 [8192], P('pos'), may hold values from 0 to 8191, as said below
- block_bits: int32 [512], P(('pos', 'head')), may hold values 0 or 1
Outputs:
- attended: bfloat16 [2, 8192, 4096], P(None, 'pos', 'head')
- grad_queries: bfloat16 [2, 8192, 4096], P(None, 'pos', 'head')
- grad_keys_values: bfloat16 [2, 2, 8192, 512], P(None, None, 'pos', 'head')
Inputs may be any that keep to these rules, and one draw needn't show every extreme that they name: doc_start[i] is the first position of the document holding position i; documents are contiguous runs of 1 to 2048 positions, and one has exactly 2048; the last position begins a document of its own.
All inputs are finite; a program needn't handle non-finite values. No bound on the sum of `block_bits` on one device may be relied on, other than what follows from the above.
Results may differ from a plain program's by a relative error of at most 0.025.
Values may be sent and summed in bfloat16 or wider, within the bound.
No kernel may reach another device: no remote copies, remote signals or barrier semaphores. Data moves between devices by JAX's collectives and lax.ppermute only.
A program may use at most 64 MiB of HBM per device.

v0:
```python
import math

import jax
import jax.numpy as jnp
from jax import lax
from jax.sharding import PartitionSpec as P

BLOCK = 16
QUERY_HEADS = 32
KEY_VALUE_HEADS = 4
HEAD_SIZE = 128


NEGATIVE = -1e30


def shifted(array, axis, by):
    count = lax.axis_size(axis)
    pairs = [(i, i + by) for i in range(count) if 0 <= i + by < count]
    return lax.ppermute(array, axis, pairs)


def tile_scores(query_rows, key_rows, factor):
    return (
        jnp.einsum("rgqd,kgd->gqrk", query_rows, key_rows, preferred_element_type=jnp.float32)
        * factor
    )


def local(queries, keys_values, d_out, doc_start, block_bits):
    row_block = queries.shape[1]
    kv_heads = keys_values.shape[3] // HEAD_SIZE
    query_group = QUERY_HEADS // KEY_VALUE_HEADS
    factor = 1.0 / math.sqrt(HEAD_SIZE)
    reach = lax.axis_size("pos") // 4
    here = lax.axis_index("pos")
    bits = lax.all_gather(block_bits, "head", axis=0, tiled=True)
    q_all = queries.reshape(2 * row_block, kv_heads, query_group, HEAD_SIZE)
    q_noisy = q_all[row_block:]
    keep = jnp.repeat(bits, BLOCK).astype(jnp.bfloat16)
    cot_all = jnp.concatenate([d_out[0], d_out[1] * keep[:, None]], 0).reshape(
        2 * row_block, kv_heads, query_group, HEAD_SIZE
    )
    cot_noisy = cot_all[row_block:]
    offsets = jnp.arange(row_block, dtype=jnp.int32)
    q_blk = (here * row_block + offsets) // BLOCK
    row_start = jnp.concatenate([doc_start, doc_start])
    same_local = doc_start[:, None] == doc_start[None, :]
    own_clean = jnp.concatenate(
        [
            same_local & (q_blk[None, :] <= q_blk[:, None]),
            same_local & (q_blk[None, :] < q_blk[:, None]),
        ],
        0,
    )
    own_noisy = same_local & (q_blk[None, :] == q_blk[:, None])
    clean_kv = keys_values[:, 0]
    noisy_kv = keys_values[:, 1]

    def pass_on(moving, unused):
        moved = shifted(moving, "pos", 1)
        return (moved, moved)

    unused_last, remote = lax.scan(pass_on, clean_kv, None, length=reach)
    step_ids = jnp.arange(1, reach + 1, dtype=jnp.int32)

    def remote_mask(distance):
        key_pos = (here - distance) * row_block + offsets
        visible = key_pos[None, :] >= row_start[:, None]
        live = doc_start[0] <= (here - distance) * row_block + row_block - 1
        return (visible, live)

    def stats(query_block_rows, tile, visible):
        scores = tile_scores(
            query_block_rows, tile[0].reshape(row_block, kv_heads, HEAD_SIZE), factor
        )
        masked = jnp.where(visible, scores, NEGATIVE)
        best = jnp.max(masked, -1)
        summed = jnp.sum(jnp.where(visible, jnp.exp(masked - best[..., None]), 0.0), -1)
        return (best, summed)

    def merge_stats(carry, best, summed):
        top, total = carry
        merged = jnp.maximum(top, best)
        return (merged, total * jnp.exp(top - merged) + summed * jnp.exp(best - merged))

    carry = (
        jnp.full((kv_heads, query_group, 2 * row_block), NEGATIVE, jnp.float32),
        jnp.zeros((kv_heads, query_group, 2 * row_block), jnp.float32),
    )
    best, summed = stats(q_all, clean_kv, own_clean)
    carry = merge_stats(carry, best, summed)

    def stats_step(carry, inputs):
        tile, distance = inputs
        visible, live = remote_mask(distance)
        best, summed = stats(q_all, tile, visible)
        return (merge_stats(carry, best, summed), None)

    carry, unused_stats = lax.scan(stats_step, carry, (remote, step_ids))
    best, summed = stats(q_noisy, noisy_kv, own_noisy)
    best = jnp.concatenate(
        [jnp.full((kv_heads, query_group, row_block), NEGATIVE, jnp.float32), best], -1
    )
    summed = jnp.concatenate(
        [jnp.zeros((kv_heads, query_group, row_block), jnp.float32), summed], -1
    )
    top, total = merge_stats(carry, best, summed)
    lse = top + jnp.log(total)

    def tile_weights(query_block_rows, tile, visible, lse_rows):
        scores = tile_scores(
            query_block_rows, tile[0].reshape(row_block, kv_heads, HEAD_SIZE), factor
        )
        weights = jnp.where(
            visible, jnp.exp(jnp.where(visible, scores - lse_rows[..., None], NEGATIVE)), 0.0
        )
        return (weights, weights.astype(jnp.bfloat16))

    def out_tile(query_block_rows, tile, visible, lse_rows):
        weights, weights_low = tile_weights(query_block_rows, tile, visible, lse_rows)
        return jnp.einsum(
            "gqrk,kgd->rgqd",
            weights_low,
            tile[1].reshape(row_block, kv_heads, HEAD_SIZE),
            preferred_element_type=jnp.float32,
        )

    def zero_rows(count):
        return jnp.zeros((count, kv_heads, query_group, HEAD_SIZE), jnp.float32)

    out_all = out_tile(q_all, clean_kv, own_clean, lse)

    def out_step(total_out, inputs):
        tile, distance = inputs
        visible, live = remote_mask(distance)
        piece = out_tile(q_all, tile, visible, lse)
        return (total_out + piece, None)

    out_all, unused_out = lax.scan(out_step, out_all, (remote, step_ids))
    out_noisy = out_tile(q_noisy, noisy_kv, own_noisy, lse[..., row_block:])
    out_all = out_all + jnp.concatenate([zero_rows(row_block), out_noisy], 0)
    attended = out_all.astype(jnp.bfloat16)
    delta = jnp.sum(cot_all.astype(jnp.float32) * attended.astype(jnp.float32), -1).transpose(
        1, 2, 0
    )

    def grad_tile(query_block_rows, cotangent_rows, tile, visible, lse_rows, delta_rows):
        key_rows = tile[0].reshape(row_block, kv_heads, HEAD_SIZE)
        value_rows = tile[1].reshape(row_block, kv_heads, HEAD_SIZE)
        weights, weights_low = tile_weights(query_block_rows, tile, visible, lse_rows)
        dprob = jnp.einsum(
            "rgqd,kgd->gqrk", cotangent_rows, value_rows, preferred_element_type=jnp.float32
        )
        dscore = (weights * (dprob - delta_rows[..., None]) * factor).astype(jnp.bfloat16)
        grad_q = jnp.einsum("gqrk,kgd->rgqd", dscore, key_rows, preferred_element_type=jnp.float32)
        key_gradient = jnp.einsum(
            "gqrk,rgqd->kgd", dscore, query_block_rows, preferred_element_type=jnp.float32
        )
        value_gradient = jnp.einsum(
            "gqrk,rgqd->kgd", weights_low, cotangent_rows, preferred_element_type=jnp.float32
        )
        return (
            grad_q,
            jnp.stack([key_gradient, value_gradient]).reshape(2, row_block, kv_heads * HEAD_SIZE),
        )

    grad_q_all, own_term = grad_tile(q_all, cot_all, clean_kv, own_clean, lse, delta)

    def grad_step(total_q, inputs):
        tile, distance = inputs
        visible, live = remote_mask(distance)
        grad_q, grad_kv = grad_tile(q_all, cot_all, tile, visible, lse, delta)
        return (total_q + grad_q, grad_kv)

    grad_q_all, remote_terms = lax.scan(grad_step, grad_q_all, (remote, step_ids))
    grad_q_noisy, noisy_term = grad_tile(
        q_noisy, cot_noisy, noisy_kv, own_noisy, lse[..., row_block:], delta[..., row_block:]
    )
    grad_q_all = grad_q_all + jnp.concatenate([zero_rows(row_block), grad_q_noisy], 0)
    clean_terms = jnp.concatenate([own_term[None], remote_terms], 0)

    def pass_back(running, term):
        return (shifted(running, "pos", -1) + term, None)

    clean_total, unused_back = lax.scan(pass_back, clean_terms[reach], clean_terms[:reach][::-1])
    grad_keys_values = jnp.stack([clean_total, noisy_term], 1).astype(jnp.bfloat16)
    return (
        attended.reshape(2, row_block, -1),
        grad_q_all.astype(jnp.bfloat16).reshape(2, row_block, -1),
        grad_keys_values,
    )


def solution(mesh):
    in_specs = (
        P(None, "pos", "head"),
        P(None, None, "pos", "head"),
        P(None, "pos", "head"),
        P("pos"),
        P(("pos", "head")),
    )
    out_specs = (P(None, "pos", "head"), P(None, "pos", "head"), P(None, None, "pos", "head"))
    return jax.shard_map(local, mesh=mesh, in_specs=in_specs, out_specs=out_specs, check_vma=False)
```

profile of v0, /device:TPU:64, one launch (start us, length us, event | category | flops | bytes accessed | tf_op | source)
XLA Modules:
  0.0 749.9 jit_solution(17431168767134118005)
XLA Ops:
  25.2 193.1 %while.59 = (s32[]{:T(128)}, bf16[2,128,256]{2,1,0:T(8,128)(2,1)S(1)}, bf16[16,2,128,256]{2,3,1,0:T(8,128)(2,1)}, s32[]{:T(128)}) while((s32[]{:T(128)}, bf16[2,128,256]{2,1,0:T(8,128)(2,1)S(1)}, bf16[16,2,128,256]{2,3,1,0:T(8,128)(2,1)}, s32[]{:T(128)}) %tuple.115), condition=%wide.region_3.4_spmd, body=%wide.region_2.3_spmd.sunk | while | flops 2 | bytes 1310825 | solution.py:64
  25.2 3.4 collective-permute-start
  28.6 8.3 %collective-permute-done = bf16[2,128,256]{2,1,0:T(8,128)(2,1)S(1)} collective-permute-done((bf16[2,128,256]{2,1,0:T(8,128)(2,1)S(1)}, bf16[2,128,256]{2,1,0:T(8,128)(2,1)S(1)}, u32[]{:S(2)}, u32[]{:S(2)}) %collective-permute-start) | collective-permute-done | bytes 131104 | tf_op jit(solution)/shard_map/while/body/eval_jaxpr/ppermute | solution.py:20
  39.6 9.2 %collective-permute-done = bf16[2,128,256]{2,1,0:T(8,128)(2,1)S(1)} collective-permute-done((bf16[2,128,256]{2,1,0:T(8,128)(2,1)S(1)}, bf16[2,128,256]{2,1,0:T(8,128)(2,1)S(1)}, u32[]{:S(2)}, u32[]{:S(2)}) %collective-permute-start) | collective-permute-done | bytes 131104 | tf_op jit(solution)/shard_map/while/body/eval_jaxpr/ppermute | solution.py:20
  51.5 9.2 %collective-permute-done = bf16[2,128,256]{2,1,0:T(8,128)(2,1)S(1)} collective-permute-done((bf16[2,128,256]{2,1,0:T(8,128)(2,1)S(1)}, bf16[2,128,256]{2,1,0:T(8,128)(2,1)S(1)}, u32[]{:S(2)}, u32[]{:S(2)}) %collective-permute-start) | collective-permute-done | bytes 131104 | tf_op jit(solution)/shard_map/while/body/eval_jaxpr/ppermute | solution.py:20
  63.4 9.2 %collective-permute-done = bf16[2,128,256]{2,1,0:T(8,128)(2,1)S(1)} collective-permute-done((bf16[2,128,256]{2,1,0:T(8,128)(2,1)S(1)}, bf16[2,128,256]{2,1,0:T(8,128)(2,1)S(1)}, u32[]{:S(2)}, u32[]{:S(2)}) %collective-permute-start) | collective-permute-done | bytes 131104 | tf_op jit(solution)/shard_map/while/body/eval_jaxpr/ppermute | solution.py:20
  75.3 9.2 %collective-permute-done = bf16[2,128,256]{2,1,0:T(8,128)(2,1)S(1)} collective-permute-done((bf16[2,128,256]{2,1,0:T(8,128)(2,1)S(1)}, bf16[2,128,256]{2,1,0:T(8,128)(2,1)S(1)}, u32[]{:S(2)}, u32[]{:S(2)}) %collective-permute-start) | collective-permute-done | bytes 131104 | tf_op jit(solution)/shard_map/while/body/eval_jaxpr/ppermute | solution.py:20
  87.2 9.2 %collective-permute-done = bf16[2,128,256]{2,1,0:T(8,128)(2,1)S(1)} collective-permute-done((bf16[2,128,256]{2,1,0:T(8,128)(2,1)S(1)}, bf16[2,128,256]{2,1,0:T(8,128)(2,1)S(1)}, u32[]{:S(2)}, u32[]{:S(2)}) %collective-permute-start) | collective-permute-done | bytes 131104 | tf_op jit(solution)/shard_map/while/body/eval_jaxpr/ppermute | solution.py:20
  99.1 9.2 %collective-permute-done = bf16[2,128,256]{2,1,0:T(8,128)(2,1)S(1)} collective-permute-done((bf16[2,128,256]{2,1,0:T(8,128)(2,1)S(1)}, bf16[2,128,256]{2,1,0:T(8,128)(2,1)S(1)}, u32[]{:S(2)}, u32[]{:S(2)}) %collective-permute-start) | collective-permute-done | bytes 131104 | tf_op jit(solution)/shard_map/while/body/eval_jaxpr/ppermute | solution.py:20
  111.0 9.2 %collective-permute-done = bf16[2,128,256]{2,1,0:T(8,128)(2,1)S(1)} collective-permute-done((bf16[2,128,256]{2,1,0:T(8,128)(2,1)S(1)}, bf16[2,128,256]{2,1,0:T(8,128)(2,1)S(1)}, u32[]{:S(2)}, u32[]{:S(2)}) %collective-permute-start) | collective-permute-done | bytes 131104 | tf_op jit(solution)/shard_map/while/body/eval_jaxpr/ppermute | solution.py:20
  122.9 9.5 %collective-permute-done = bf16[2,128,256]{2,1,0:T(8,128)(2,1)S(1)} collective-permute-done((bf16[2,128,256]{2,1,0:T(8,128)(2,1)S(1)}, bf16[2,128,256]{2,1,0:T(8,128)(2,1)S(1)}, u32[]{:S(2)}, u32[]{:S(2)}) %collective-permute-start) | collective-permute-done | bytes 131104 | tf_op jit(solution)/shard_map/while/body/eval_jaxpr/ppermute | solution.py:20
  135.1 10.5 %collective-permute-done = bf16[2,128,256]{2,1,0:T(8,128)(2,1)S(1)} collective-permute-done((bf16[2,128,256]{2,1,0:T(8,128)(2,1)S(1)}, bf16[2,128,256]{2,1,0:T(8,128)(2,1)S(1)}, u32[]{:S(2)}, u32[]{:S(2)}) %collective-permute-start) | collective-permute-done | bytes 131104 | tf_op jit(solution)/shard_map/while/body/eval_jaxpr/ppermute | solution.py:20
  148.4 9.6 %collective-permute-done = bf16[2,128,256]{2,1,0:T(8,128)(2,1)S(1)} collective-permute-done((bf16[2,128,256]{2,1,0:T(8,128)(2,1)S(1)}, bf16[2,128,256]{2,1,0:T(8,128)(2,1)S(1)}, u32[]{:S(2)}, u32[]{:S(2)}) %collective-permute-start) | collective-permute-done | bytes 131104 | tf_op jit(solution)/shard_map/while/body/eval_jaxpr/ppermute | solution.py:20
  160.7 9.2 %collective-permute-done = bf16[2,128,256]{2,1,0:T(8,128)(2,1)S(1)} collective-permute-done((bf16[2,128,256]{2,1,0:T(8,128)(2,1)S(1)}, bf16[2,128,256]{2,1,0:T(8,128)(2,1)S(1)}, u32[]{:S(2)}, u32[]{:S(2)}) %collective-permute-start) | collective-permute-done | bytes 131104 | tf_op jit(solution)/shard_map/while/body/eval_jaxpr/ppermute | solution.py:20
  172.7 9.2 %collective-permute-done = bf16[2,128,256]{2,1,0:T(8,128)(2,1)S(1)} collective-permute-done((bf16[2,128,256]{2,1,0:T(8,128)(2,1)S(1)}, bf16[2,128,256]{2,1,0:T(8,128)(2,1)S(1)}, u32[]{:S(2)}, u32[]{:S(2)}) %collective-permute-start) | collective-permute-done | bytes 131104 | tf_op jit(solution)/shard_map/while/body/eval_jaxpr/ppermute | solution.py:20
  184.5 9.2 %collective-permute-done = bf16[2,128,256]{2,1,0:T(8,128)(2,1)S(1)} collective-permute-done((bf16[2,128,256]{2,1,0:T(8,128)(2,1)S(1)}, bf16[2,128,256]{2,1,0:T(8,128)(2,1)S(1)}, u32[]{:S(2)}, u32[]{:S(2)}) %collective-permute-start) | collective-permute-done | bytes 131104 | tf_op jit(solution)/shard_map/while/body/eval_jaxpr/ppermute | solution.py:20
  196.4 9.2 %collective-permute-done = bf16[2,128,256]{2,1,0:T(8,128)(2,1)S(1)} collective-permute-done((bf16[2,128,256]{2,1,0:T(8,128)(2,1)S(1)}, bf16[2,128,256]{2,1,0:T(8,128)(2,1)S(1)}, u32[]{:S(2)}, u32[]{:S(2)}) %collective-permute-start) | collective-permute-done | bytes 131104 | tf_op jit(solution)/shard_map/while/body/eval_jaxpr/ppermute | solution.py:20
  208.3 9.2 %collective-permute-done = bf16[2,128,256]{2,1,0:T(8,128)(2,1)S(1)} collective-permute-done((bf16[2,128,256]{2,1,0:T(8,128)(2,1)S(1)}, bf16[2,128,256]{2,1,0:T(8,128)(2,1)S(1)}, u32[]{:S(2)}, u32[]{:S(2)}) %collective-permute-start) | collective-permute-done | bytes 131104 | tf_op jit(solution)/shard_map/while/body/eval_jaxpr/ppermute | solution.py:20
  221.6 62.1 %while.61 = (s32[]{:T(128)}, f32[2,8,256]{2,1,0:T(8,128)S(1)}, f32[2,8,256]{2,1,0:T(8,128)S(1)}, s32[16]{0:T(128)}, s32[]{:T(128)}, /*index=5*/s32[256]{0:T(256)...) while((s32[]{:T(128)}, f32[2,8,256]{2,1,0:T(8,128)S(1)}, ...), condition=%wide.region_7.8_spmd.clone, body=%wide.region_4.7_spmd.clone.sunk | while | flops 138461312 | bytes 5687449 | solution.py:100
  294.5 87.7 %while.62 = (s32[]{:T(128)}, f32[256,2,8,128]{0,3,2,1:T(8,128)S(1)}, bf16[16,2,128,256]{2,3,1,0:T(8,128)(2,1)}, s32[16]{0:T(128)}, s32[]{:T(128)}, /*index=5*/s3...) while((s32[]{:T(128)}, ...), condition=%wide.region_11.12_spmd.clone, body=%wide.region_10.11_spmd.clone.sunk | while | flops 271614080 | bytes 5720249 | solution.py:140
  308.3 2.6 bitcast_add_fusion.7
  324.7 2.6 bitcast_add_fusion.7
  330.2 2.6 bitcast_add_fusion.7
  335.7 2.6 bitcast_add_fusion.7
  352.1 2.6 bitcast_add_fusion.7
  357.6 2.6 bitcast_add_fusion.7
  363.1 2.6 bitcast_add_fusion.7
  382.2 3.0 multiply_reduce_fusion
  396.8 3.7 copy.96
  400.4 131.4 %while.63 = (s32[]{:T(128)}, f32[256,2,8,128]{0,3,2,1:T(8,128)S(1)}, f32[16,2,128,256]{2,3,1,0:T(8,128)}, bf16[16,2,128,256]{2,3,1,0:T(8,128)(2,1)}, s32[16]{0:T...) while((s32[]{:T(128)}, ...), condition=%wide.region_14.15_spmd.clone, body=%wide.region_13.14_spmd.clone.sunk | while | flops 676429952 | bytes 23365872 | solution.py:176
  538.5 4.6 pad_maximum_fusion
  543.0 4.6 rev.3
  547.8 201.3 %while.60 = (s32[]{:T(128)}, f32[2,128,256]{2,1,0:T(8,128)S(1)}, f32[16,2,128,256]{2,3,1,0:T(8,128)}, s32[]{:T(128)}) while((s32[]{:T(128)}, f32[2,128,256]{2,1,0:T(8,128)S(1)}, f32[16,2,128,256]{2,3,1,0:T(8,128)}, s32[]{:T(128)}) %tuple.127), condition=%wide.region_16.17_spmd, body=%wide.region_15.16_spmd.sunk | while | flops 65538 | bytes 2883689 | solution.py:186
  550.8 6.4 collective-permute-done.1
  557.3 4.9 collective-permute-start.1
  563.4 4.8 collective-permute-done.1
  568.2 6.6 collective-permute-start.1
  575.9 3.0 collective-permute-done.1
  579.0 8.6 %collective-permute-start.1 = (f32[2,128,256]{2,1,0:T(8,128)S(1)}, f32[2,128,256]{2,1,0:T(8,128)S(1)}, u32[]{:S(2)}, u32[]{:S(2)}) collective-permute-start(f32[2,128,256]{2,1,0:T(8,128)S(1)} %get-tuple-element.766), channel_id=1, source_target_pairs={{2,0},{4,2},{6,4},{8,6},{10,8},{12,10},{14,12},{16,14},{18,16},{20... | collective-permute-start | bytes 786440 | tf_op jit(solution)/shard_map/while/body/eval_jaxpr/ppermute | solution.py:20
  588.7 4.1 collective-permute-done.1
  592.8 8.6 %collective-permute-start.1 = (f32[2,128,256]{2,1,0:T(8,128)S(1)}, f32[2,128,256]{2,1,0:T(8,128)S(1)}, u32[]{:S(2)}, u32[]{:S(2)}) collective-permute-start(f32[2,128,256]{2,1,0:T(8,128)S(1)} %get-tuple-element.766), channel_id=1, source_target_pairs={{2,0},{4,2},{6,4},{8,6},{10,8},{12,10},{14,12},{16,14},{18,16},{20... | collective-permute-start | bytes 786440 | tf_op jit(solution)/shard_map/while/body/eval_jaxpr/ppermute | solution.py:20
  602.6 5.2 collective-permute-done.1
  607.9 8.6 %collective-permute-start.1 = (f32[2,128,256]{2,1,0:T(8,128)S(1)}, f32[2,128,256]{2,1,0:T(8,128)S(1)}, u32[]{:S(2)}, u32[]{:S(2)}) collective-permute-start(f32[2,128,256]{2,1,0:T(8,128)S(1)} %get-tuple-element.766), channel_id=1, source_target_pairs={{2,0},{4,2},{6,4},{8,6},{10,8},{12,10},{14,12},{16,14},{18,16},{20... | collective-permute-start | bytes 786440 | tf_op jit(solution)/shard_map/while/body/eval_jaxpr/ppermute | solution.py:20
  617.6 4.7 collective-permute-done.1
  622.4 8.6 %collective-permute-start.1 = (f32[2,128,256]{2,1,0:T(8,128)S(1)}, f32[2,128,256]{2,1,0:T(8,128)S(1)}, u32[]{:S(2)}, u32[]{:S(2)}) collective-permute-start(f32[2,128,256]{2,1,0:T(8,128)S(1)} %get-tuple-element.766), channel_id=1, source_target_pairs={{2,0},{4,2},{6,4},{8,6},{10,8},{12,10},{14,12},{16,14},{18,16},{20... | collective-permute-start | bytes 786440 | tf_op jit(solution)/shard_map/while/body/eval_jaxpr/ppermute | solution.py:20
  632.1 3.9 collective-permute-done.1
  636.1 8.6 %collective-permute-start.1 = (f32[2,128,256]{2,1,0:T(8,128)S(1)}, f32[2,128,256]{2,1,0:T(8,128)S(1)}, u32[]{:S(2)}, u32[]{:S(2)}) collective-permute-start(f32[2,128,256]{2,1,0:T(8,128)S(1)} %get-tuple-element.766), channel_id=1, source_target_pairs={{2,0},{4,2},{6,4},{8,6},{10,8},{12,10},{14,12},{16,14},{18,16},{20... | collective-permute-start | bytes 786440 | tf_op jit(solution)/shard_map/while/body/eval_jaxpr/ppermute | solution.py:20
  645.8 3.0 collective-permute-done.1
  648.8 8.6 %collective-permute-start.1 = (f32[2,128,256]{2,1,0:T(8,128)S(1)}, f32[2,128,256]{2,1,0:T(8,128)S(1)}, u32[]{:S(2)}, u32[]{:S(2)}) collective-permute-start(f32[2,128,256]{2,1,0:T(8,128)S(1)} %get-tuple-element.766), channel_id=1, source_target_pairs={{2,0},{4,2},{6,4},{8,6},{10,8},{12,10},{14,12},{16,14},{18,16},{20... | collective-permute-start | bytes 786440 | tf_op jit(solution)/shard_map/while/body/eval_jaxpr/ppermute | solution.py:20
  658.6 2.8 collective-permute-done.1
  661.4 8.6 %collective-permute-start.1 = (f32[2,128,256]{2,1,0:T(8,128)S(1)}, f32[2,128,256]{2,1,0:T(8,128)S(1)}, u32[]{:S(2)}, u32[]{:S(2)}) collective-permute-start(f32[2,128,256]{2,1,0:T(8,128)S(1)} %get-tuple-element.766), channel_id=1, source_target_pairs={{2,0},{4,2},{6,4},{8,6},{10,8},{12,10},{14,12},{16,14},{18,16},{20... | collective-permute-start | bytes 786440 | tf_op jit(solution)/shard_map/while/body/eval_jaxpr/ppermute | solution.py:20
  671.1 2.8 collective-permute-done.1
  673.9 8.6 %collective-permute-start.1 = (f32[2,128,256]{2,1,0:T(8,128)S(1)}, f32[2,128,256]{2,1,0:T(8,128)S(1)}, u32[]{:S(2)}, u32[]{:S(2)}) collective-permute-start(f32[2,128,256]{2,1,0:T(8,128)S(1)} %get-tuple-element.766), channel_id=1, source_target_pairs={{2,0},{4,2},{6,4},{8,6},{10,8},{12,10},{14,12},{16,14},{18,16},{20... | collective-permute-start | bytes 786440 | tf_op jit(solution)/shard_map/while/body/eval_jaxpr/ppermute | solution.py:20
  683.6 2.8 collective-permute-done.1
  686.4 8.6 %collective-permute-start.1 = (f32[2,128,256]{2,1,0:T(8,128)S(1)}, f32[2,128,256]{2,1,0:T(8,128)S(1)}, u32[]{:S(2)}, u32[]{:S(2)}) collective-permute-start(f32[2,128,256]{2,1,0:T(8,128)S(1)} %get-tuple-element.766), channel_id=1, source_target_pairs={{2,0},{4,2},{6,4},{8,6},{10,8},{12,10},{14,12},{16,14},{18,16},{20... | collective-permute-start | bytes 786440 | tf_op jit(solution)/shard_map/while/body/eval_jaxpr/ppermute | solution.py:20
  696.2 2.8 collective-permute-done.1
  699.0 8.6 %collective-permute-start.1 = (f32[2,128,256]{2,1,0:T(8,128)S(1)}, f32[2,128,256]{2,1,0:T(8,128)S(1)}, u32[]{:S(2)}, u32[]{:S(2)}) collective-permute-start(f32[2,128,256]{2,1,0:T(8,128)S(1)} %get-tuple-element.766), channel_id=1, source_target_pairs={{2,0},{4,2},{6,4},{8,6},{10,8},{12,10},{14,12},{16,14},{18,16},{20... | collective-permute-start | bytes 786440 | tf_op jit(solution)/shard_map/while/body/eval_jaxpr/ppermute | solution.py:20
  708.7 2.8 collective-permute-done.1
  711.5 8.6 %collective-permute-start.1 = (f32[2,128,256]{2,1,0:T(8,128)S(1)}, f32[2,128,256]{2,1,0:T(8,128)S(1)}, u32[]{:S(2)}, u32[]{:S(2)}) collective-permute-start(f32[2,128,256]{2,1,0:T(8,128)S(1)} %get-tuple-element.766), channel_id=1, source_target_pairs={{2,0},{4,2},{6,4},{8,6},{10,8},{12,10},{14,12},{16,14},{18,16},{20... | collective-permute-start | bytes 786440 | tf_op jit(solution)/shard_map/while/body/eval_jaxpr/ppermute | solution.py:20
  721.3 2.8 collective-permute-done.1
  724.1 8.6 %collective-permute-start.1 = (f32[2,128,256]{2,1,0:T(8,128)S(1)}, f32[2,128,256]{2,1,0:T(8,128)S(1)}, u32[]{:S(2)}, u32[]{:S(2)}) collective-permute-start(f32[2,128,256]{2,1,0:T(8,128)S(1)} %get-tuple-element.766), channel_id=1, source_target_pairs={{2,0},{4,2},{6,4},{8,6},{10,8},{12,10},{14,12},{16,14},{18,16},{20... | collective-permute-start | bytes 786440 | tf_op jit(solution)/shard_map/while/body/eval_jaxpr/ppermute | solution.py:20
  733.8 2.8 collective-permute-done.1
  736.6 8.6 %collective-permute-start.1 = (f32[2,128,256]{2,1,0:T(8,128)S(1)}, f32[2,128,256]{2,1,0:T(8,128)S(1)}, u32[]{:S(2)}, u32[]{:S(2)}) collective-permute-start(f32[2,128,256]{2,1,0:T(8,128)S(1)} %get-tuple-element.766), channel_id=1, source_target_pairs={{2,0},{4,2},{6,4},{8,6},{10,8},{12,10},{14,12},{16,14},{18,16},{20... | collective-permute-start | bytes 786440 | tf_op jit(solution)/shard_map/while/body/eval_jaxpr/ppermute | solution.py:20
  746.3 2.8 collective-permute-done.1
  (616 shorter events, 347.6 us)
Async XLA Ops:
  0.6 13.9 %copy-start.16 = (bf16[2,128,2048]{2,1,0:T(8,128)(2,1)S(1)}, bf16[2,128,2048]{2,1,0:T(8,128)(2,1)}, u32[]{:S(2)}) copy-start(bf16[2,128,2048]{2,1,0:T(8,128)(2,1)} %param.15) | copy-start | bytes 3145732
  7.1 1.6 copy-start.27
  15.5 202.8 %copy-start = (bf16[256,2,8,128]{0,3,2,1:T(8,128)(2,1)}, bf16[256,2,8,128]{0,3,2,1:T(8,128)(2,1)S(1)}, u32[]{:S(2)}) copy-start(bf16[256,2,8,128]{0,3,2,1:T(8,128)(2,1)S(1)} %copy.112) | copy-start | bytes 3145732
  15.6 1.6 copy-start.19
  21.6 1.5 copy-start.10
  21.6 1.8 copy-start.13
  23.4 1.8 copy-start.30
  25.2 11.7 %collective-permute-start = (bf16[2,128,256]{2,1,0:T(8,128)(2,1)S(1)}, bf16[2,128,256]{2,1,0:T(8,128)(2,1)S(1)}, u32[]{:S(2)}, u32[]{:S(2)}) collective-permute-start(bf16[2,128,256]{2,1,0:T(8,128)(2,1)S(1)} %get-tuple-element.643), channel_id=1, source_target_pairs={{0,2},{2,4},{4,6},{6,8},{8,10},{10,12},{12,14},{14,16},{16,18},{18... | collective-permute-start | bytes 393224 | tf_op jit(solution)/shard_map/while/body/eval_jaxpr/ppermute | solution.py:20
  37.7 11.1 %collective-permute-start = (bf16[2,128,256]{2,1,0:T(8,128)(2,1)S(1)}, bf16[2,128,256]{2,1,0:T(8,128)(2,1)S(1)}, u32[]{:S(2)}, u32[]{:S(2)}) collective-permute-start(bf16[2,128,256]{2,1,0:T(8,128)(2,1)S(1)} %get-tuple-element.643), channel_id=1, source_target_pairs={{0,2},{2,4},{4,6},{6,8},{8,10},{10,12},{12,14},{14,16},{16,18},{18... | collective-permute-start | bytes 393224 | tf_op jit(solution)/shard_map/while/body/eval_jaxpr/ppermute | solution.py:20
  49.6 11.1 %collective-permute-start = (bf16[2,128,256]{2,1,0:T(8,128)(2,1)S(1)}, bf16[2,128,256]{2,1,0:T(8,128)(2,1)S(1)}, u32[]{:S(2)}, u32[]{:S(2)}) collective-permute-start(bf16[2,128,256]{2,1,0:T(8,128)(2,1)S(1)} %get-tuple-element.643), channel_id=1, source_target_pairs={{0,2},{2,4},{4,6},{6,8},{8,10},{10,12},{12,14},{14,16},{16,18},{18... | collective-permute-start | bytes 393224 | tf_op jit(solution)/shard_map/while/body/eval_jaxpr/ppermute | solution.py:20
  61.5 11.1 %collective-permute-start = (bf16[2,128,256]{2,1,0:T(8,128)(2,1)S(1)}, bf16[2,128,256]{2,1,0:T(8,128)(2,1)S(1)}, u32[]{:S(2)}, u32[]{:S(2)}) collective-permute-start(bf16[2,128,256]{2,1,0:T(8,128)(2,1)S(1)} %get-tuple-element.643), channel_id=1, source_target_pairs={{0,2},{2,4},{4,6},{6,8},{8,10},{10,12},{12,14},{14,16},{16,18},{18... | collective-permute-start | bytes 393224 | tf_op jit(solution)/shard_map/while/body/eval_jaxpr/ppermute | solution.py:20
  73.4 11.1 %collective-permute-start = (bf16[2,128,256]{2,1,0:T(8,128)(2,1)S(1)}, bf16[2,128,256]{2,1,0:T(8,128)(2,1)S(1)}, u32[]{:S(2)}, u32[]{:S(2)}) collective-permute-start(bf16[2,128,256]{2,1,0:T(8,128)(2,1)S(1)} %get-tuple-element.643), channel_id=1, source_target_pairs={{0,2},{2,4},{4,6},{6,8},{8,10},{10,12},{12,14},{14,16},{16,18},{18... | collective-permute-start | bytes 393224 | tf_op jit(solution)/shard_map/while/body/eval_jaxpr/ppermute | solution.py:20
  85.3 11.1 %collective-permute-start = (bf16[2,128,256]{2,1,0:T(8,128)(2,1)S(1)}, bf16[2,128,256]{2,1,0:T(8,128)(2,1)S(1)}, u32[]{:S(2)}, u32[]{:S(2)}) collective-permute-start(bf16[2,128,256]{2,1,0:T(8,128)(2,1)S(1)} %get-tuple-element.643), channel_id=1, source_target_pairs={{0,2},{2,4},{4,6},{6,8},{8,10},{10,12},{12,14},{14,16},{16,18},{18... | collective-permute-start | bytes 393224 | tf_op jit(solution)/shard_map/while/body/eval_jaxpr/ppermute | solution.py:20
  97.2 11.1 %collective-permute-start = (bf16[2,128,256]{2,1,0:T(8,128)(2,1)S(1)}, bf16[2,128,256]{2,1,0:T(8,128)(2,1)S(1)}, u32[]{:S(2)}, u32[]{:S(2)}) collective-permute-start(bf16[2,128,256]{2,1,0:T(8,128)(2,1)S(1)} %get-tuple-element.643), channel_id=1, source_target_pairs={{0,2},{2,4},{4,6},{6,8},{8,10},{10,12},{12,14},{14,16},{16,18},{18... | collective-permute-start | bytes 393224 | tf_op jit(solution)/shard_map/while/body/eval_jaxpr/ppermute | solution.py:20
  109.1 11.1 %collective-permute-start = (bf16[2,128,256]{2,1,0:T(8,128)(2,1)S(1)}, bf16[2,128,256]{2,1,0:T(8,128)(2,1)S(1)}, u32[]{:S(2)}, u32[]{:S(2)}) collective-permute-start(bf16[2,128,256]{2,1,0:T(8,128)(2,1)S(1)} %get-tuple-element.643), channel_id=1, source_target_pairs={{0,2},{2,4},{4,6},{6,8},{8,10},{10,12},{12,14},{14,16},{16,18},{18... | collective-permute-start | bytes 393224 | tf_op jit(solution)/shard_map/while/body/eval_jaxpr/ppermute | solution.py:20
  121.0 11.4 %collective-permute-start = (bf16[2,128,256]{2,1,0:T(8,128)(2,1)S(1)}, bf16[2,128,256]{2,1,0:T(8,128)(2,1)S(1)}, u32[]{:S(2)}, u32[]{:S(2)}) collective-permute-start(bf16[2,128,256]{2,1,0:T(8,128)(2,1)S(1)} %get-tuple-element.643), channel_id=1, source_target_pairs={{0,2},{2,4},{4,6},{6,8},{8,10},{10,12},{12,14},{14,16},{16,18},{18... | collective-permute-start | bytes 393224 | tf_op jit(solution)/shard_map/while/body/eval_jaxpr/ppermute | solution.py:20
  133.2 12.4 %collective-permute-start = (bf16[2,128,256]{2,1,0:T(8,128)(2,1)S(1)}, bf16[2,128,256]{2,1,0:T(8,128)(2,1)S(1)}, u32[]{:S(2)}, u32[]{:S(2)}) collective-permute-start(bf16[2,128,256]{2,1,0:T(8,128)(2,1)S(1)} %get-tuple-element.643), channel_id=1, source_target_pairs={{0,2},{2,4},{4,6},{6,8},{8,10},{10,12},{12,14},{14,16},{16,18},{18... | collective-permute-start | bytes 393224 | tf_op jit(solution)/shard_map/while/body/eval_jaxpr/ppermute | solution.py:20
  146.4 11.6 %collective-permute-start = (bf16[2,128,256]{2,1,0:T(8,128)(2,1)S(1)}, bf16[2,128,256]{2,1,0:T(8,128)(2,1)S(1)}, u32[]{:S(2)}, u32[]{:S(2)}) collective-permute-start(bf16[2,128,256]{2,1,0:T(8,128)(2,1)S(1)} %get-tuple-element.643), channel_id=1, source_target_pairs={{0,2},{2,4},{4,6},{6,8},{8,10},{10,12},{12,14},{14,16},{16,18},{18... | collective-permute-start | bytes 393224 | tf_op jit(solution)/shard_map/while/body/eval_jaxpr/ppermute | solution.py:20
  158.8 11.1 %collective-permute-start = (bf16[2,128,256]{2,1,0:T(8,128)(2,1)S(1)}, bf16[2,128,256]{2,1,0:T(8,128)(2,1)S(1)}, u32[]{:S(2)}, u32[]{:S(2)}) collective-permute-start(bf16[2,128,256]{2,1,0:T(8,128)(2,1)S(1)} %get-tuple-element.643), channel_id=1, source_target_pairs={{0,2},{2,4},{4,6},{6,8},{8,10},{10,12},{12,14},{14,16},{16,18},{18... | collective-permute-start | bytes 393224 | tf_op jit(solution)/shard_map/while/body/eval_jaxpr/ppermute | solution.py:20
  170.7 11.1 %collective-permute-start = (bf16[2,128,256]{2,1,0:T(8,128)(2,1)S(1)}, bf16[2,128,256]{2,1,0:T(8,128)(2,1)S(1)}, u32[]{:S(2)}, u32[]{:S(2)}) collective-permute-start(bf16[2,128,256]{2,1,0:T(8,128)(2,1)S(1)} %get-tuple-element.643), channel_id=1, source_target_pairs={{0,2},{2,4},{4,6},{6,8},{8,10},{10,12},{12,14},{14,16},{16,18},{18... | collective-permute-start | bytes 393224 | tf_op jit(solution)/shard_map/while/body/eval_jaxpr/ppermute | solution.py:20
  182.6 11.1 %collective-permute-start = (bf16[2,128,256]{2,1,0:T(8,128)(2,1)S(1)}, bf16[2,128,256]{2,1,0:T(8,128)(2,1)S(1)}, u32[]{:S(2)}, u32[]{:S(2)}) collective-permute-start(bf16[2,128,256]{2,1,0:T(8,128)(2,1)S(1)} %get-tuple-element.643), channel_id=1, source_target_pairs={{0,2},{2,4},{4,6},{6,8},{8,10},{10,12},{12,14},{14,16},{16,18},{18... | collective-permute-start | bytes 393224 | tf_op jit(solution)/shard_map/while/body/eval_jaxpr/ppermute | solution.py:20
  194.5 11.1 %collective-permute-start = (bf16[2,128,256]{2,1,0:T(8,128)(2,1)S(1)}, bf16[2,128,256]{2,1,0:T(8,128)(2,1)S(1)}, u32[]{:S(2)}, u32[]{:S(2)}) collective-permute-start(bf16[2,128,256]{2,1,0:T(8,128)(2,1)S(1)} %get-tuple-element.643), channel_id=1, source_target_pairs={{0,2},{2,4},{4,6},{6,8},{8,10},{10,12},{12,14},{14,16},{16,18},{18... | collective-permute-start | bytes 393224 | tf_op jit(solution)/shard_map/while/body/eval_jaxpr/ppermute | solution.py:20
  206.4 11.1 %collective-permute-start = (bf16[2,128,256]{2,1,0:T(8,128)(2,1)S(1)}, bf16[2,128,256]{2,1,0:T(8,128)(2,1)S(1)}, u32[]{:S(2)}, u32[]{:S(2)}) collective-permute-start(bf16[2,128,256]{2,1,0:T(8,128)(2,1)S(1)} %get-tuple-element.643), channel_id=1, source_target_pairs={{0,2},{2,4},{4,6},{6,8},{8,10},{10,12},{12,14},{14,16},{16,18},{18... | collective-permute-start | bytes 393224 | tf_op jit(solution)/shard_map/while/body/eval_jaxpr/ppermute | solution.py:20
  218.3 2.7 copy-start.20
  218.3 3.2 copy-start.28
  219.7 1.3 copy-start.4
  221.6 62.2 %copy-start.31 = (f32[2,8,128]{2,1,0:T(8,128)S(1)}, f32[2,8,128]{2,1,0:T(8,128)}, u32[]{:S(2)}) copy-start(f32[2,8,128]{2,1,0:T(8,128)} %copy-done.30) | copy-start | bytes 24580
  221.6 62.2 %copy-start.32 = (f32[2,8,128]{2,1,0:T(8,128)S(1)}, f32[2,8,128]{2,1,0:T(8,128)}, u32[]{:S(2)}) copy-start(f32[2,8,128]{2,1,0:T(8,128)} %select_reduce_fusion.2) | copy-start | bytes 24580
  283.7 2.7 copy-start.5
  286.4 2.6 copy-start.8
  286.4 2.6 copy-start.24
  289.0 1.5 copy-start.22
  382.2 3.1 copy-start.6
  382.2 3.1 copy-start.12
  382.2 3.1 copy-start.14
  382.2 3.1 copy-start.23
  386.2 2.0 copy-start.1
  405.6 1.2 copy-start.2
  422.1 1.2 copy-start.2
  430.3 1.2 copy-start.2
  438.5 1.2 copy-start.2
  446.7 1.2 copy-start.2
  454.9 1.2 copy-start.2
  471.3 1.2 copy-start.2
  531.8 1.8 copy-start.15
  535.5 3.0 copy-start.21
  535.5 3.0 copy-start.29
  547.8 201.4 %copy-start.26 = (bf16[1,1,128,256]{3,2,1,0:T(8,128)(2,1)S(1)}, bf16[1,1,128,256]{3,2,1,0:T(8,128)(2,1)}, u32[]{:S(2)}) copy-start(bf16[1,1,128,256]{3,2,1,0:T(8,128)(2,1)} %copy.95) | copy-start | bytes 196612
  547.8 9.5 %collective-permute-start.1 = (f32[2,128,256]{2,1,0:T(8,128)S(1)}, f32[2,128,256]{2,1,0:T(8,128)S(1)}, u32[]{:S(2)}, u32[]{:S(2)}) collective-permute-start(f32[2,128,256]{2,1,0:T(8,128)S(1)} %get-tuple-element.766), channel_id=1, source_target_pairs={{2,0},{4,2},{6,4},{8,6},{10,8},{12,10},{14,12},{16,14},{18,16},{20... | collective-permute-start | bytes 786440 | tf_op jit(solution)/shard_map/while/body/eval_jaxpr/ppermute | solution.py:20
  557.3 10.8 %collective-permute-start.1 = (f32[2,128,256]{2,1,0:T(8,128)S(1)}, f32[2,128,256]{2,1,0:T(8,128)S(1)}, u32[]{:S(2)}, u32[]{:S(2)}) collective-permute-start(f32[2,128,256]{2,1,0:T(8,128)S(1)} %get-tuple-element.766), channel_id=1, source_target_pairs={{2,0},{4,2},{6,4},{8,6},{10,8},{12,10},{14,12},{16,14},{18,16},{20... | collective-permute-start | bytes 786440 | tf_op jit(solution)/shard_map/while/body/eval_jaxpr/ppermute | solution.py:20
  568.2 10.7 %collective-permute-start.1 = (f32[2,128,256]{2,1,0:T(8,128)S(1)}, f32[2,128,256]{2,1,0:T(8,128)S(1)}, u32[]{:S(2)}, u32[]{:S(2)}) collective-permute-start(f32[2,128,256]{2,1,0:T(8,128)S(1)} %get-tuple-element.766), channel_id=1, source_target_pairs={{2,0},{4,2},{6,4},{8,6},{10,8},{12,10},{14,12},{16,14},{18,16},{20... | collective-permute-start | bytes 786440 | tf_op jit(solution)/shard_map/while/body/eval_jaxpr/ppermute | solution.py:20
  579.0 13.8 %collective-permute-start.1 = (f32[2,128,256]{2,1,0:T(8,128)S(1)}, f32[2,128,256]{2,1,0:T(8,128)S(1)}, u32[]{:S(2)}, u32[]{:S(2)}) collective-permute-start(f32[2,128,256]{2,1,0:T(8,128)S(1)} %get-tuple-element.766), channel_id=1, source_target_pairs={{2,0},{4,2},{6,4},{8,6},{10,8},{12,10},{14,12},{16,14},{18,16},{20... | collective-permute-start | bytes 786440 | tf_op jit(solution)/shard_map/while/body/eval_jaxpr/ppermute | solution.py:20
  592.8 15.0 %collective-permute-start.1 = (f32[2,128,256]{2,1,0:T(8,128)S(1)}, f32[2,128,256]{2,1,0:T(8,128)S(1)}, u32[]{:S(2)}, u32[]{:S(2)}) collective-permute-start(f32[2,128,256]{2,1,0:T(8,128)S(1)} %get-tuple-element.766), channel_id=1, source_target_pairs={{2,0},{4,2},{6,4},{8,6},{10,8},{12,10},{14,12},{16,14},{18,16},{20... | collective-permute-start | bytes 786440 | tf_op jit(solution)/shard_map/while/body/eval_jaxpr/ppermute | solution.py:20
  607.9 14.5 %collective-permute-start.1 = (f32[2,128,256]{2,1,0:T(8,128)S(1)}, f32[2,128,256]{2,1,0:T(8,128)S(1)}, u32[]{:S(2)}, u32[]{:S(2)}) collective-permute-start(f32[2,128,256]{2,1,0:T(8,128)S(1)} %get-tuple-element.766), channel_id=1, source_target_pairs={{2,0},{4,2},{6,4},{8,6},{10,8},{12,10},{14,12},{16,14},{18,16},{20... | collective-permute-start | bytes 786440 | tf_op jit(solution)/shard_map/while/body/eval_jaxpr/ppermute | solution.py:20
  622.4 13.6 %collective-permute-start.1 = (f32[2,128,256]{2,1,0:T(8,128)S(1)}, f32[2,128,256]{2,1,0:T(8,128)S(1)}, u32[]{:S(2)}, u32[]{:S(2)}) collective-permute-start(f32[2,128,256]{2,1,0:T(8,128)S(1)} %get-tuple-element.766), channel_id=1, source_target_pairs={{2,0},{4,2},{6,4},{8,6},{10,8},{12,10},{14,12},{16,14},{18,16},{20... | collective-permute-start | bytes 786440 | tf_op jit(solution)/shard_map/while/body/eval_jaxpr/ppermute | solution.py:20
  636.1 12.7 %collective-permute-start.1 = (f32[2,128,256]{2,1,0:T(8,128)S(1)}, f32[2,128,256]{2,1,0:T(8,128)S(1)}, u32[]{:S(2)}, u32[]{:S(2)}) collective-permute-start(f32[2,128,256]{2,1,0:T(8,128)S(1)} %get-tuple-element.766), channel_id=1, source_target_pairs={{2,0},{4,2},{6,4},{8,6},{10,8},{12,10},{14,12},{16,14},{18,16},{20... | collective-permute-start | bytes 786440 | tf_op jit(solution)/shard_map/while/body/eval_jaxpr/ppermute | solution.py:20
  648.8 12.5 %collective-permute-start.1 = (f32[2,128,256]{2,1,0:T(8,128)S(1)}, f32[2,128,256]{2,1,0:T(8,128)S(1)}, u32[]{:S(2)}, u32[]{:S(2)}) collective-permute-start(f32[2,128,256]{2,1,0:T(8,128)S(1)} %get-tuple-element.766), channel_id=1, source_target_pairs={{2,0},{4,2},{6,4},{8,6},{10,8},{12,10},{14,12},{16,14},{18,16},{20... | collective-permute-start | bytes 786440 | tf_op jit(solution)/shard_map/while/body/eval_jaxpr/ppermute | solution.py:20
  661.4 12.5 %collective-permute-start.1 = (f32[2,128,256]{2,1,0:T(8,128)S(1)}, f32[2,128,256]{2,1,0:T(8,128)S(1)}, u32[]{:S(2)}, u32[]{:S(2)}) collective-permute-start(f32[2,128,256]{2,1,0:T(8,128)S(1)} %get-tuple-element.766), channel_id=1, source_target_pairs={{2,0},{4,2},{6,4},{8,6},{10,8},{12,10},{14,12},{16,14},{18,16},{20... | collective-permute-start | bytes 786440 | tf_op jit(solution)/shard_map/while/body/eval_jaxpr/ppermute | solution.py:20
  673.9 12.5 %collective-permute-start.1 = (f32[2,128,256]{2,1,0:T(8,128)S(1)}, f32[2,128,256]{2,1,0:T(8,128)S(1)}, u32[]{:S(2)}, u32[]{:S(2)}) collective-permute-start(f32[2,128,256]{2,1,0:T(8,128)S(1)} %get-tuple-element.766), channel_id=1, source_target_pairs={{2,0},{4,2},{6,4},{8,6},{10,8},{12,10},{14,12},{16,14},{18,16},{20... | collective-permute-start | bytes 786440 | tf_op jit(solution)/shard_map/while/body/eval_jaxpr/ppermute | solution.py:20
  686.4 12.5 %collective-permute-start.1 = (f32[2,128,256]{2,1,0:T(8,128)S(1)}, f32[2,128,256]{2,1,0:T(8,128)S(1)}, u32[]{:S(2)}, u32[]{:S(2)}) collective-permute-start(f32[2,128,256]{2,1,0:T(8,128)S(1)} %get-tuple-element.766), channel_id=1, source_target_pairs={{2,0},{4,2},{6,4},{8,6},{10,8},{12,10},{14,12},{16,14},{18,16},{20... | collective-permute-start | bytes 786440 | tf_op jit(solution)/shard_map/while/body/eval_jaxpr/ppermute | solution.py:20
  699.0 12.5 %collective-permute-start.1 = (f32[2,128,256]{2,1,0:T(8,128)S(1)}, f32[2,128,256]{2,1,0:T(8,128)S(1)}, u32[]{:S(2)}, u32[]{:S(2)}) collective-permute-start(f32[2,128,256]{2,1,0:T(8,128)S(1)} %get-tuple-element.766), channel_id=1, source_target_pairs={{2,0},{4,2},{6,4},{8,6},{10,8},{12,10},{14,12},{16,14},{18,16},{20... | collective-permute-start | bytes 786440 | tf_op jit(solution)/shard_map/while/body/eval_jaxpr/ppermute | solution.py:20
  711.5 12.5 %collective-permute-start.1 = (f32[2,128,256]{2,1,0:T(8,128)S(1)}, f32[2,128,256]{2,1,0:T(8,128)S(1)}, u32[]{:S(2)}, u32[]{:S(2)}) collective-permute-start(f32[2,128,256]{2,1,0:T(8,128)S(1)} %get-tuple-element.766), channel_id=1, source_target_pairs={{2,0},{4,2},{6,4},{8,6},{10,8},{12,10},{14,12},{16,14},{18,16},{20... | collective-permute-start | bytes 786440 | tf_op jit(solution)/shard_map/while/body/eval_jaxpr/ppermute | solution.py:20
  724.1 12.5 %collective-permute-start.1 = (f32[2,128,256]{2,1,0:T(8,128)S(1)}, f32[2,128,256]{2,1,0:T(8,128)S(1)}, u32[]{:S(2)}, u32[]{:S(2)}) collective-permute-start(f32[2,128,256]{2,1,0:T(8,128)S(1)} %get-tuple-element.766), channel_id=1, source_target_pairs={{2,0},{4,2},{6,4},{8,6},{10,8},{12,10},{14,12},{16,14},{18,16},{20... | collective-permute-start | bytes 786440 | tf_op jit(solution)/shard_map/while/body/eval_jaxpr/ppermute | solution.py:20
  736.6 12.5 %collective-permute-start.1 = (f32[2,128,256]{2,1,0:T(8,128)S(1)}, f32[2,128,256]{2,1,0:T(8,128)S(1)}, u32[]{:S(2)}, u32[]{:S(2)}) collective-permute-start(f32[2,128,256]{2,1,0:T(8,128)S(1)} %get-tuple-element.766), channel_id=1, source_target_pairs={{2,0},{4,2},{6,4},{8,6},{10,8},{12,10},{14,12},{16,14},{18,16},{20... | collective-permute-start | bytes 786440 | tf_op jit(solution)/shard_map/while/body/eval_jaxpr/ppermute | solution.py:20
  (16 other events, 18.6 us)
where the time goes:
time: 759 us; the launch traced here: 750 us
  waiting for transfers between devices  205 us (27%)
  local copies, waits for them, and re-layouts  180 us (24%)
  starting transfers between devices  158 us (21%)
  matrix products  129 us (17%)
  other arithmetic  40.5 us (5%)
  loops' own time  34.3 us (5%)
    ppermute x32, waiting for transfers between devices, shifted(): return lax.ppermute(array, axis, pairs)  205 us
    ppermute x32, starting transfers between devices, shifted(): return lax.ppermute(array, axis, pairs)  158 us
    dynamic_slice x48, local copies, waits for them, and re-layouts, local(): carry, unused_stats = lax.scan(stats_step, carry, (remote, step_ids))  56.2 us
    dot_general x18, matrix products, out_tile(): jnp.einsum('gqrk,kgd->rgqd', weights_low, tile[1].reshape(row_block, kv_h...  45.6 us
    dot_general x34, matrix products, tile_scores(): jnp.einsum('rgqd,kgd->gqrk', query_rows, key_rows, preferred_element_type...  41.5 us
    dynamic_slice x32, local copies, waits for them, and re-layouts, local(): lax.scan(pass_back, clean_terms[reach], clean_terms[:reach][::-1])  17.6 us
    unnamed x76, local copies, waits for them, and re-layouts  17.4 us
  transfers between devices with their start and end apart: 32, of which 32 were waited for; matrix products, arithmetic and copies ran while one was open for 2% of the time, Pallas kernels for 0%

commit v1 on v0

v1 whole, which is shorter than its diff:
```python
import functools
import math

import jax
import jax.numpy as jnp
from jax import lax
from jax.experimental import pallas as pl
from jax.experimental.pallas import tpu as pltpu
from jax.sharding import Mesh
from jax.sharding import PartitionSpec as P

BLOCK = 16
QUERY_HEADS = 32
KEY_VALUE_HEADS = 4
HEAD_SIZE = 128
GROUP = QUERY_HEADS // KEY_VALUE_HEADS
REACH = 16
NEGATIVE = -1e30
SCALE = 1.0 / math.sqrt(HEAD_SIZE)
SCALE_LOG2 = SCALE * math.log2(math.e)
TILE = 256

NT = (((1,), (1,)), ((), ()))


def dot(a, b, dims=(((1,), (0,)), ((), ()))):
    return lax.dot_general(a, b, dims, preferred_element_type=jnp.float32)


def fold(x, op):
    return op(x.reshape(x.shape[0] // 8, 8, x.shape[1]), 0)


def kernel(
    rows,
    q_ref,
    do_ref,
    far_ref,
    own_ref,
    bias_ref,
    keep_ref,
    *rest,
):
    att_ref, dq_ref, back_ref, local_ref = rest[-14:-10]
    k_all, v_all, k_t, v_t, s_all, p_all, ds_all, dk_all, dv_all, unused = rest[-10:]
    step = pl.program_id(0)
    keys = k_all.shape[0]
    tiles = keys // TILE

    @pl.when(step == 0)
    def _():
        for slot in range(REACH + 2):
            at = pl.ds(slot * rows, rows)
            if slot < REACH:
                k, v = far_ref[slot, 0], far_ref[slot, 1]
            else:
                k, v = own_ref[0, slot - REACH], own_ref[1, slot - REACH]
            k_all[at, :] = k
            v_all[at, :] = v
            k_t[:, at] = k.T
            v_t[:, at] = v.T
        dk_all[...] = jnp.zeros_like(dk_all)
        dv_all[...] = jnp.zeros_like(dv_all)

    q = q_ref[...].reshape(2 * rows, HEAD_SIZE)
    top = jnp.full((8, 2 * rows), NEGATIVE, jnp.float32)
    for tile in range(tiles):
        at = pl.ds(tile * TILE, TILE)
        s = dot(k_all[at, :], q, NT) + bias_ref[at, :]
        s_all[at, :] = s
        top = jnp.maximum(top, fold(s, jnp.max))
    top = jnp.max(top, 0, keepdims=True)

    total = jnp.zeros((8, 2 * rows), jnp.float32)
    for tile in range(tiles):
        at = pl.ds(tile * TILE, TILE)
        e = jnp.exp2((s_all[at, :] - top) * SCALE_LOG2)
        s_all[at, :] = e
        p_all[at, :] = e.astype(jnp.bfloat16)
        total = total + fold(e, jnp.sum)
    inverse = 1.0 / jnp.sum(total, 0, keepdims=True)

    out_t = dot(v_t[...], p_all[...]) * inverse
    att_ref[...] = out_t.T.astype(jnp.bfloat16).reshape(2, rows, HEAD_SIZE)
    out_t = out_t.astype(jnp.bfloat16).astype(jnp.float32)
    do_t = do_ref[...].reshape(2 * rows, HEAD_SIZE).astype(jnp.float32).T
    g_t = (do_t * (inverse * keep_ref[0:1, :])).astype(jnp.bfloat16)
    delta = jnp.sum(g_t.astype(jnp.float32) * out_t, 0, keepdims=True)

    for tile in range(tiles):
        at = pl.ds(tile * TILE, TILE)
        dp = dot(v_all[at, :], g_t)
        ds_all[at, :] = (s_all[at, :] * (dp - delta)).astype(jnp.bfloat16)
    dq_t = dot(k_t[...], ds_all[...]) * SCALE
    dq_ref[...] = dq_t.T.astype(jnp.bfloat16).reshape(2, rows, HEAD_SIZE)
    for tile in range(tiles):
        at = pl.ds(tile * TILE, TILE)
        dk_all[at, :] += dot(ds_all[at, :], q)
        dv_all[at, :] += dot(p_all[at, :], g_t, NT)

    @pl.when(step == GROUP - 1)
    def _():
        for slot in range(REACH + 2):
            at = pl.ds(slot * rows, rows)
            dk = dk_all[at, :] * SCALE
            dv = dv_all[at, :]
            if slot < REACH:
                back_ref[slot, 0] = dk.astype(jnp.bfloat16)
                back_ref[slot, 1] = dv.astype(jnp.bfloat16)
            else:
                local_ref[0, slot - REACH] = dk
                local_ref[1, slot - REACH] = dv


def attend(group, queries, d_out, far, keys_values, bias, keep, earlier):
    rows = queries.shape[1]
    keys = (REACH + 2) * rows

    def column(step):
        return (0, 0, group * GROUP + step)

    by_head = pl.BlockSpec((2, rows, HEAD_SIZE), column)
    whole = lambda shape: pl.BlockSpec(shape, lambda step: (0,) * len(shape))
    hbm = pl.BlockSpec(memory_space=pl.ANY)
    far_shape = (REACH, 2, rows, HEAD_SIZE)
    local_shape = (2, 2, rows, HEAD_SIZE)
    flops = 6 * 2 * keys * 2 * rows * HEAD_SIZE * GROUP
    return pl.pallas_call(
        functools.partial(kernel, rows),
        grid=(GROUP,),
        in_specs=[
            by_head,
            by_head,
            whole(far_shape),
            pl.BlockSpec(local_shape, lambda step: (0, 0, 0, group)),
            whole((keys, 2 * rows)),
            whole((8, 2 * rows)),
        ]
        + [hbm] * len(earlier),
        out_specs=[by_head, by_head, whole(far_shape), whole(local_shape)],
        out_shape=[
            jax.ShapeDtypeStruct(queries.shape, jnp.bfloat16),
            jax.ShapeDtypeStruct(queries.shape, jnp.bfloat16),
            jax.ShapeDtypeStruct(far_shape, jnp.bfloat16),
            jax.ShapeDtypeStruct(local_shape, jnp.float32),
        ],
        scratch_shapes=[
            pltpu.VMEM((keys, HEAD_SIZE), jnp.bfloat16),
            pltpu.VMEM((keys, HEAD_SIZE), jnp.bfloat16),
            pltpu.VMEM((HEAD_SIZE, keys), jnp.bfloat16),
            pltpu.VMEM((HEAD_SIZE, keys), jnp.bfloat16),
            pltpu.VMEM((keys, 2 * rows), jnp.float32),
            pltpu.VMEM((keys, 2 * rows), jnp.bfloat16),
            pltpu.VMEM((keys, 2 * rows), jnp.bfloat16),
            pltpu.VMEM((keys, HEAD_SIZE), jnp.float32),
            pltpu.VMEM((keys, HEAD_SIZE), jnp.float32),
            pltpu.VMEM((8, 128), jnp.float32),
        ],
        input_output_aliases={6 + i: i for i in range(len(earlier))},
        compiler_params=pltpu.CompilerParams(vmem_limit_bytes=40 * 2**20),
        cost_estimate=pl.CostEstimate(
            flops=2 * flops, bytes_accessed=6 * 2**20, transcendentals=keys * 2 * rows * GROUP
        ),
        name=f"attend_{group}",
    )(queries, d_out, far, keys_values, bias, keep, *earlier)


def masks(doc_start, slab, place, places):
    rows = doc_start.shape[0]
    offset = jnp.arange(rows, dtype=jnp.int32)
    starts = jnp.concatenate([doc_start, doc_start])
    slot = jnp.arange(REACH, dtype=jnp.int32)
    base = rows * (places * slab + slot - jnp.where(slot >= place, places, 0))
    key_pos = base[:, None] + offset[None, :]
    far = key_pos[:, :, None] >= starts[None, None, :]
    same = doc_start[:, None] == starts[None, :]
    k_blk = (offset // BLOCK)[:, None]
    q_blk = jnp.concatenate([offset // BLOCK] * 2)[None, :]
    noisy = (jnp.arange(2 * rows, dtype=jnp.int32) >= rows)[None, :]
    own_clean = same & (k_blk + noisy.astype(jnp.int32) <= q_blk)
    own_noisy = same & noisy & (k_blk == q_blk)
    allowed = jnp.concatenate([far, own_clean[None], own_noisy[None]], 0)
    return jnp.where(allowed, 0.0, NEGATIVE).astype(jnp.float32).reshape(-1, 2 * rows)


def local(queries, keys_values, d_out, doc_start, block_bits):
    rows = queries.shape[1]
    slabs, places = lax.axis_size("slab"), lax.axis_size("place")
    slab, place, head = (lax.axis_index(a) for a in ("slab", "place", "head"))
    kv_heads = keys_values.shape[3] // HEAD_SIZE
    later = [(i, i + 1) for i in range(slabs - 1)]
    sooner = [(i + 1, i) for i in range(slabs - 1)]
    slot = jnp.arange(places, dtype=jnp.int32)[:, None, None, None]
    after = slot > place

    far = []
    for group in range(kv_heads):
        own = keys_values[:, 0, :, group * HEAD_SIZE : (group + 1) * HEAD_SIZE]
        before = lax.ppermute(own, "slab", later)
        send = jnp.where(after, own[None], before[None])
        far.append(lax.all_to_all(send, "place", 0, 0))

    other = lax.ppermute(block_bits, "head", [(0, 1), (1, 0)])
    bits = jnp.where(
        head == 0,
        jnp.concatenate([block_bits, other]),
        jnp.concatenate([other, block_bits]),
    )
    keep = jnp.concatenate([jnp.ones((rows,), jnp.int32), jnp.repeat(bits, BLOCK)])
    keep = jnp.broadcast_to(keep.astype(jnp.float32)[None, :], (8, 2 * rows))
    bias = masks(doc_start, slab, place, places)

    earlier = ()
    totals, noisy = [], []
    for group in range(kv_heads):
        att, dq, back, mine = attend(
            group, queries, d_out, far[group], keys_values, bias, keep, earlier
        )
        earlier = (att, dq)
        terms = lax.all_to_all(back, "place", 0, 0).astype(jnp.float32)
        here = jnp.sum(jnp.where(after, terms, 0.0), 0)
        there = jnp.sum(jnp.where(after, 0.0, terms), 0).astype(jnp.bfloat16)
        arrived = lax.ppermute(there, "slab", sooner)
        totals.append(mine[:, 0] + here + arrived.astype(jnp.float32))
        noisy.append(mine[:, 1])
    grad = jnp.stack([jnp.concatenate(totals, -1), jnp.concatenate(noisy, -1)], 1)
    return att, dq, grad.astype(jnp.bfloat16)


def solution(mesh):
    shards, heads = mesh.devices.shape
    cut = Mesh(mesh.devices.reshape(shards // REACH, REACH, heads), ("slab", "place", "head"))
    pos = ("slab", "place")
    in_specs = (
        P(None, pos, "head"),
        P(None, None, pos, "head"),
        P(None, pos, "head"),
        P(pos),
        P((*pos, "head")),
    )
    out_specs = (P(None, pos, "head"), P(None, pos, "head"), P(None, None, pos, "head"))
    return jax.shard_map(local, mesh=cut, in_specs=in_specs, out_specs=out_specs, check_vma=False)
```

time: 759 us -> 145 us (0.19); the launches traced: 750 us -> 144 us
  local copies, waits for them, and re-layouts: 180 us -> 9.96 us
  waiting for transfers between devices: 205 us -> 36.8 us
  starting transfers between devices: 158 us -> 24.8 us
  matrix products: 129 us -> 0 us
  Pallas kernels: 0 us -> 45.2 us
  other arithmetic: 40.5 us -> 4.21 us
  loops' own time: 34.3 us -> 0 us
  blocking collectives: 1.81 us -> 22.3 us
    ppermute x32 -> x5, waiting for transfers between devices: 205 us -> 6.98 us  [the longest x2 4.2 us: local(): arrived = lax.ppermute(there, 'slab', sooner)]
    ppermute x32 -> x5, starting transfers between devices: 158 us -> 9.77 us  [the longest x2 5.45 us: local(): before = lax.ppermute(own, 'slab', later)]
    dot_general x124 -> x0, matrix products: 129 us -> none  [the longest x18 45.6 us: out_tile(): jnp.einsum('gqrk,kgd->rgqd', weights_low, tile[1].reshape(row_block, kv_h...]
    dynamic_slice x80 -> x0, local copies, waits for them, and re-layouts: 73.8 us -> none  [the longest x48 56.2 us: local(): carry, unused_stats = lax.scan(stats_step, carry, (remote, step_ids))]
    slice x56 -> x0, local copies, waits for them, and re-layouts: 49.2 us -> none  [the longest x16 14.2 us: grad_tile(): value_rows = tile[1].reshape(row_block, kv_heads, HEAD_SIZE)]
    pallas_call x0 -> x2, Pallas kernels: none -> 45.2 us  [attend(): pl.pallas_call(functools.partial(kernel, rows), grid=(GROUP,), in_specs=[...]
    another operation x5 -> x0, loops' own time: 34.3 us -> none  [the longest x1 11.5 us: local(): lax.scan(grad_step, grad_q_all, (remote, step_ids))]
    all_to_all x0 -> x3, waiting for transfers between devices: none -> 29.8 us  [the longest x2 15.4 us: local(): far.append(lax.all_to_all(send, 'place', 0, 0))]
  transfers between devices with their start and end apart: 32 -> 8, of which waited for: 32 -> 5; matrix products, arithmetic and copies ran while one was open for 2% -> 4% of each run, Pallas kernels for 0% -> 15%
where the time goes in v1:
time: 145 us; the launch traced here: 144 us
  Pallas kernels  45.2 us (31%)
  waiting for transfers between devices  36.8 us (25%)
  starting transfers between devices  24.8 us (17%)
  blocking collectives  22.3 us (15%)
  local copies, waits for them, and re-layouts  9.96 us (7%)
  other arithmetic  4.21 us (3%)
    pallas_call x2, Pallas kernels, attend(): pl.pallas_call(functools.partial(kernel, rows), grid=(GROUP,), in_specs=[...  45.2 us
    all_to_all x1, blocking collectives, local(): terms = lax.all_to_all(back, 'place', 0, 0).astype(jnp.float32)  22.3 us
    all_to_all x2, waiting for transfers between devices, local(): far.append(lax.all_to_all(send, 'place', 0, 0))  15.4 us
    all_to_all x1, waiting for transfers between devices, local(): terms = lax.all_to_all(back, 'place', 0, 0).astype(jnp.float32)  14.4 us
    all_to_all x2, starting transfers between devices, local(): far.append(lax.all_to_all(send, 'place', 0, 0))  11.4 us
    unnamed x22, local copies, waits for them, and re-layouts  8.89 us
    ppermute x2, starting transfers between devices, local(): before = lax.ppermute(own, 'slab', later)  5.45 us
    ppermute x2, starting transfers between devices, local(): arrived = lax.ppermute(there, 'slab', sooner)  4.23 us
  transfers between devices with their start and end apart: 8, of which 5 were waited for; matrix products, arithmetic and copies ran while one was open for 4% of the time, Pallas kernels for 15%

profile of v1, /device:TPU:64, one launch (start us, length us, event | category | flops | bytes accessed | tf_op | source)
XLA Modules:
  0.0 144.2 jit_solution(2404722635619291044)
XLA Ops:
  0.6 0.1 collective-permute-start.1
  0.7 0.9 slice_bitcast_fusion.2
  1.6 3.5 %collective-permute-start.2 = (bf16[2,128,128]{2,1,0:T(8,128)(2,1)S(1)}, bf16[2,128,128]{2,1,0:T(8,128)(2,1)S(1)}, u32[]{:S(2)}, u32[]{:S(2)}) collective-permute-start(bf16[2,128,128]{2,1,0:T(8,128)(2,1)S(1)} %get-tuple-element.28), channel_id=1, source_target_pairs={{0,32},{32,64},{64,96},{1,33},{33,65},{65,97},{2,34},{34,66},{66,9... | collective-permute-start | bytes 196616 | tf_op jit(solution)/shard_map/ppermute | solution.py:199
  5.2 1.9 %collective-permute-start = (bf16[2,128,128]{2,1,0:T(8,128)(2,1)S(1)}, bf16[2,128,128]{2,1,0:T(8,128)(2,1)S(1)}, u32[]{:S(2)}, u32[]{:S(2)}) collective-permute-start(bf16[2,128,128]{2,1,0:T(8,128)(2,1)S(1)} %get-tuple-element.29), channel_id=1, source_target_pairs={{0,32},{32,64},{64,96},{1,33},{33,65},{65,97},{2,34},{34,66},{66,9... | collective-permute-start | bytes 196616 | tf_op jit(solution)/shard_map/ppermute | solution.py:199
  7.1 0.7 constant_dynamic-update-slice_fusion.1
  7.8 0.7 constant_dynamic-update-slice_fusion
  8.4 0.1 iota_add_fusion
  8.5 0.0 copy-start.8
  8.5 0.0 collective-permute-done.2
  8.5 2.8 %collective-permute-done = bf16[2,128,128]{2,1,0:T(8,128)(2,1)S(1)} collective-permute-done((bf16[2,128,128]{2,1,0:T(8,128)(2,1)S(1)}, bf16[2,128,128]{2,1,0:T(8,128)(2,1)S(1)}, u32[]{:S(2)}, u32[]{:S(2)}) %collective-permute-start) | collective-permute-done | bytes 65568 | tf_op jit(solution)/shard_map/ppermute | solution.py:199
  11.3 1.6 %broadcast_select_fusion = (bf16[16,2,128,128]{3,2,1,0:T(8,128)(2,1)}, bf16[16,2,128,128]{3,2,1,0:T(8,128)(2,1)}) fusion(pred[16]{0:T(512)(128)(4,1)S(1)} %iota_compare_fusion.1, bf16[2,128,128]{2,1,0:T(8,128)(2,1)S(1)} %collective-permute-done.2, bf16[2,128,128]{2,1,0:T(8,128)(2,1)S(1)} %get-tuple-element.28, ...), kind=kLoop, calls=%fused_computation.10 | loop fusion | flops 1048576 | bytes 2359312 | tf_op jit(solution)/shard_map/jit(_where)/select_n | solution.py:200
  12.9 7.0 %all-to-all-start.1 = ((bf16[16,2,128,128]{3,2,1,0:T(8,128)(2,1)}), bf16[16,2,128,128]{3,2,1,0:T(8,128)(2,1)S(1)}, u32[]{:S(2)}, u32[]{:S(2)}) async-start(bf16[16,2,128,128]{3,2,1,0:T(8,128)(2,1)} %get-tuple-element.32), calls=%async_computation.1 | async-start | bytes 2097152 | tf_op jit(solution)/shard_map/all_to_all | solution.py:201
  19.9 0.0 copy-start.9
  20.0 0.0 copy-done.8
  20.0 0.1 compare_and_fusion.1
  20.1 0.5 broadcast_compare_fusion
  20.6 0.3 add_select_fusion
  20.9 0.0 collective-permute-done.1
  20.9 0.0 copy-done.9
  20.9 0.1 broadcast_select_fusion.2
  21.0 0.1 broadcast_in_dim.115
  21.1 0.1 reshape.294
  21.2 15.4 %all-to-all-done.1.far_ref = bf16[16,2,128,128]{3,2,1,0:T(8,128)(2,1)S(1)} async-done(((bf16[16,2,128,128]{3,2,1,0:T(8,128)(2,1)}), bf16[16,2,128,128]{3,2,1,0:T(8,128)(2,1)S(1)}, u32[]{:S(2)}, u32[]{:S(2)}) %all-to-all-start.1) | async-done | bytes 1048608 | tf_op jit(solution)/shard_map/all_to_all | solution.py:201
  36.5 4.3 %all-to-all-start = ((bf16[16,2,128,128]{3,2,1,0:T(8,128)(2,1)}), bf16[16,2,128,128]{3,2,1,0:T(8,128)(2,1)}, u32[]{:S(2)}, u32[]{:S(2)}) async-start(bf16[16,2,128,128]{3,2,1,0:T(8,128)(2,1)} %get-tuple-element.33), calls=%async_computation | async-start | bytes 2097152 | tf_op jit(solution)/shard_map/all_to_all | solution.py:201
  40.9 0.0 copy-start.2
  40.9 0.9 copy-done.2
  41.8 0.0 copy-start.4
  41.8 1.2 copy-done.4
  43.1 0.0 copy-start.6
  43.1 1.2 copy-done.6
  44.3 22.2 %attend_0.1 = (bf16[2,128,2048]{2,1,0:T(8,128)(2,1)}, bf16[2,128,2048]{2,1,0:T(8,128)(2,1)}, bf16[16,2,128,128]{3,2,1,0:T(8,128)(2,1)}, f32[2,2,128,128]{3,2,1,0:T(8,128)S(1)}) custom-call(bf16[2,128,2048]{2,1,0:T(8,128)(2,1)S(1)} %copy-done.4, bf16[2,128,2048]{2,1,0:T(8,128)(2,1)S(1)} %copy-done.6, bf16[16,2,128,128]{3,2,1,0:T(8,128)(2,1)S(1)} %all-to-all-done.1.far_ref, ...), custom_call_target="tpu_custom_call" | custom-call | flops 14495514624 | bytes 6291456 | tf_op jit(solution)/shard_map/attend_0/pallas_call | solution.py:128
  66.5 0.0 copy-start
  66.5 0.7 copy-done
  67.2 0.0 all-to-all-done.far_ref
  67.2 0.0 copy-start.3
  67.2 0.9 copy-done.3
  68.1 0.0 copy-start.5
  68.1 1.2 copy-done.5
  69.4 0.0 copy-start.7
  69.4 1.2 copy-done.7
  70.6 23.0 %attend_1.1 = (bf16[2,128,2048]{2,1,0:T(8,128)(2,1)}, bf16[2,128,2048]{2,1,0:T(8,128)(2,1)}, bf16[16,2,128,128]{3,2,1,0:T(8,128)(2,1)S(1)}, f32[2,2,128,128]{3,2,1,0:T(8,128)S(1)}) custom-call(bf16[2,128,2048]{2,1,0:T(8,128)(2,1)S(1)} %copy-done.5, bf16[2,128,2048]{2,1,0:T(8,128)(2,1)S(1)} %copy-done.7, ...), custom_call_target="tpu_custom_call", output_to_operand_aliasing={{0}: (6, {}), {1}: (7, {})} | custom-call | flops 14495514624 | bytes 6291456 | tf_op jit(solution)/shard_map/attend_1/pallas_call | solution.py:128
  93.6 0.0 copy-start.1
  93.6 22.3 %all_to_all.20 = bf16[16,2,128,128]{3,2,1,0:T(8,128)(2,1)S(1)} all-to-all(bf16[16,2,128,128]{3,2,1,0:T(8,128)(2,1)S(1)} %get-tuple-element.18), channel_id=1, replica_groups=mesh['slab'=4,'place'=16,'head'=2] {'place'}, dimensions={0} | all-to-all | bytes 2097152 | tf_op jit(solution)/shard_map/all_to_all | solution.py:220
  115.9 3.7 %all-to-all-start.2 = ((bf16[16,2,128,128]{3,2,1,0:T(8,128)(2,1)}), bf16[16,2,128,128]{3,2,1,0:T(8,128)(2,1)S(1)}, u32[]{:S(2)}, u32[]{:S(2)}) async-start(bf16[16,2,128,128]{3,2,1,0:T(8,128)(2,1)} %get-tuple-element.16), calls=%async_computation.2 | async-start | bytes 2097152 | tf_op jit(solution)/shard_map/all_to_all | solution.py:220
  119.6 0.0 copy-done.1
  119.6 14.4 %all-to-all-done.2 = bf16[16,2,128,128]{3,2,1,0:T(8,128)(2,1)S(1)} async-done(((bf16[16,2,128,128]{3,2,1,0:T(8,128)(2,1)}), bf16[16,2,128,128]{3,2,1,0:T(8,128)(2,1)S(1)}, u32[]{:S(2)}, u32[]{:S(2)}) %all-to-all-start.2) | async-done | bytes 1048608 | tf_op jit(solution)/shard_map/all_to_all | solution.py:220
  134.1 0.8 fusion.1
  134.9 2.3 %collective-permute-start.3 = (bf16[2,128,128]{2,1,0:T(8,128)(2,1)S(1)}, bf16[2,128,128]{2,1,0:T(8,128)(2,1)S(1)}, u32[]{:S(2)}, u32[]{:S(2)}) collective-permute-start(bf16[2,128,128]{2,1,0:T(8,128)(2,1)S(1)} %get-tuple-element.22), channel_id=1, source_target_pairs={{32,0},{64,32},{96,64},{33,1},{65,33},{97,65},{34,2},{66,34},{98,6... | collective-permute-start | bytes 196616 | tf_op jit(solution)/shard_map/ppermute | solution.py:223
  137.2 1.9 %collective-permute-start.4 = (bf16[2,128,128]{2,1,0:T(8,128)(2,1)S(1)}, bf16[2,128,128]{2,1,0:T(8,128)(2,1)S(1)}, u32[]{:S(2)}, u32[]{:S(2)}) collective-permute-start(bf16[2,128,128]{2,1,0:T(8,128)(2,1)S(1)} %get-tuple-element.27), channel_id=1, source_target_pairs={{32,0},{64,32},{96,64},{33,1},{65,33},{97,65},{34,2},{66,34},{98,6... | collective-permute-start | bytes 196616 | tf_op jit(solution)/shard_map/ppermute | solution.py:223
  139.1 1.9 %collective-permute-done.3 = bf16[2,128,128]{2,1,0:T(8,128)(2,1)S(1)} collective-permute-done((bf16[2,128,128]{2,1,0:T(8,128)(2,1)S(1)}, bf16[2,128,128]{2,1,0:T(8,128)(2,1)S(1)}, u32[]{:S(2)}, u32[]{:S(2)}) %collective-permute-start.3) | collective-permute-done | bytes 65568 | tf_op jit(solution)/shard_map/ppermute | solution.py:223
  141.1 2.3 %collective-permute-done.4 = bf16[2,128,128]{2,1,0:T(8,128)(2,1)S(1)} collective-permute-done((bf16[2,128,128]{2,1,0:T(8,128)(2,1)S(1)}, bf16[2,128,128]{2,1,0:T(8,128)(2,1)S(1)}, u32[]{:S(2)}, u32[]{:S(2)}) %collective-permute-start.4) | collective-permute-done | bytes 65568 | tf_op jit(solution)/shard_map/ppermute | solution.py:223
  143.5 0.7 copy.13
  (14 shorter events, 0.2 us)
Async XLA Ops:
  0.6 20.3 %collective-permute-start.1 = (s32[4]{0:T(128)}, s32[4]{0:T(128)S(1)}, u32[]{:S(2)}, u32[]{:S(2)}) collective-permute-start(s32[4]{0:T(128)} %param.9), channel_id=1, source_target_pairs={{0,1},{1,0},{2,3},{3,2},{4,5},{5,4},{6,7},{7,6},{8,9},{9,8},{10,11... | collective-permute-start | bytes 56 | tf_op jit(solution)/shard_map/ppermute | solution.py:203
  1.6 6.9 %collective-permute-start.2 = (bf16[2,128,128]{2,1,0:T(8,128)(2,1)S(1)}, bf16[2,128,128]{2,1,0:T(8,128)(2,1)S(1)}, u32[]{:S(2)}, u32[]{:S(2)}) collective-permute-start(bf16[2,128,128]{2,1,0:T(8,128)(2,1)S(1)} %get-tuple-element.28), channel_id=1, source_target_pairs={{0,32},{32,64},{64,96},{1,33},{33,65},{65,97},{2,34},{34,66},{66,9... | collective-permute-start | bytes 196616 | tf_op jit(solution)/shard_map/ppermute | solution.py:199
  5.2 6.2 %collective-permute-start = (bf16[2,128,128]{2,1,0:T(8,128)(2,1)S(1)}, bf16[2,128,128]{2,1,0:T(8,128)(2,1)S(1)}, u32[]{:S(2)}, u32[]{:S(2)}) collective-permute-start(bf16[2,128,128]{2,1,0:T(8,128)(2,1)S(1)} %get-tuple-element.29), channel_id=1, source_target_pairs={{0,32},{32,64},{64,96},{1,33},{33,65},{65,97},{2,34},{34,66},{66,9... | collective-permute-start | bytes 196616 | tf_op jit(solution)/shard_map/ppermute | solution.py:199
  8.5 11.4 %copy-start.8 = (s32[128]{0:T(128)S(1)}, s32[128]{0:T(128)}, u32[]{:S(2)}) copy-start(s32[128]{0:T(128)} %param.8) | copy-start | bytes 1540
  12.9 23.6 %all-to-all-start.1 = ((bf16[16,2,128,128]{3,2,1,0:T(8,128)(2,1)}), bf16[16,2,128,128]{3,2,1,0:T(8,128)(2,1)S(1)}, u32[]{:S(2)}, u32[]{:S(2)}) async-start(bf16[16,2,128,128]{3,2,1,0:T(8,128)(2,1)} %get-tuple-element.32), calls=%async_computation.1 | async-start | bytes 2097152 | tf_op jit(solution)/shard_map/all_to_all | solution.py:201
  19.9 1.0 copy-start.9
  36.5 30.7 %all-to-all-start = ((bf16[16,2,128,128]{3,2,1,0:T(8,128)(2,1)}), bf16[16,2,128,128]{3,2,1,0:T(8,128)(2,1)}, u32[]{:S(2)}, u32[]{:S(2)}) async-start(bf16[16,2,128,128]{3,2,1,0:T(8,128)(2,1)} %get-tuple-element.33), calls=%async_computation | async-start | bytes 2097152 | tf_op jit(solution)/shard_map/all_to_all | solution.py:201
  40.9 1.0 copy-start.2
  41.8 1.2 copy-start.4
  43.1 1.2 copy-start.6
  66.5 0.7 copy-start
  67.2 1.0 copy-start.3
  68.1 1.2 copy-start.5
  69.4 1.2 copy-start.7
  93.6 26.0 %copy-start.1 = (f32[2,2,128,128]{3,2,1,0:T(8,128)S(1)}, f32[2,2,128,128]{3,2,1,0:T(8,128)}, u32[]{:S(2)}) copy-start(f32[2,2,128,128]{3,2,1,0:T(8,128)} %copy-done) | copy-start | bytes 786436
  115.9 18.1 %all-to-all-start.2 = ((bf16[16,2,128,128]{3,2,1,0:T(8,128)(2,1)}), bf16[16,2,128,128]{3,2,1,0:T(8,128)(2,1)S(1)}, u32[]{:S(2)}, u32[]{:S(2)}) async-start(bf16[16,2,128,128]{3,2,1,0:T(8,128)(2,1)} %get-tuple-element.16), calls=%async_computation.2 | async-start | bytes 2097152 | tf_op jit(solution)/shard_map/all_to_all | solution.py:220
  134.9 6.2 %collective-permute-start.3 = (bf16[2,128,128]{2,1,0:T(8,128)(2,1)S(1)}, bf16[2,128,128]{2,1,0:T(8,128)(2,1)S(1)}, u32[]{:S(2)}, u32[]{:S(2)}) collective-permute-start(bf16[2,128,128]{2,1,0:T(8,128)(2,1)S(1)} %get-tuple-element.22), channel_id=1, source_target_pairs={{32,0},{64,32},{96,64},{33,1},{65,33},{97,65},{34,2},{66,34},{98,6... | collective-permute-start | bytes 196616 | tf_op jit(solution)/shard_map/ppermute | solution.py:223
  137.2 6.2 %collective-permute-start.4 = (bf16[2,128,128]{2,1,0:T(8,128)(2,1)S(1)}, bf16[2,128,128]{2,1,0:T(8,128)(2,1)S(1)}, u32[]{:S(2)}, u32[]{:S(2)}) collective-permute-start(bf16[2,128,128]{2,1,0:T(8,128)(2,1)S(1)} %get-tuple-element.27), channel_id=1, source_target_pairs={{32,0},{64,32},{96,64},{33,1},{65,33},{97,65},{34,2},{66,34},{98,6... | collective-permute-start | bytes 196616 | tf_op jit(solution)/shard_map/ppermute | solution.py:223

commit v2 on v1

v2 whole, which is shorter than its diff:
```python
import functools
import math

import jax
import jax.numpy as jnp
from jax import lax
from jax.experimental import pallas as pl
from jax.experimental.pallas import tpu as pltpu
from jax.sharding import Mesh
from jax.sharding import PartitionSpec as P

BLOCK = 16
QUERY_HEADS = 32
KEY_VALUE_HEADS = 4
HEAD_SIZE = 128
GROUP = QUERY_HEADS // KEY_VALUE_HEADS
REACH = 16
NEGATIVE = -1e30
SCALE = 1.0 / math.sqrt(HEAD_SIZE)
SCALE_LOG2 = SCALE * math.log2(math.e)
TILE = 256
SLOTS = 3
VMEM_LIMIT = 60 * 2**20

NT = (((1,), (1,)), ((), ()))


def dot(a, b, dims=(((1,), (0,)), ((), ()))):
    return lax.dot_general(a, b, dims, preferred_element_type=jnp.float32)


def fold(x, op):
    return op(x.reshape(x.shape[0] // 8, 8, x.shape[1]), 0)


def kernel(
    rows,
    group,
    q_ref,
    do_ref,
    far_ref,
    own_ref,
    base_ref,
    starts_ref,
    near_ref,
    keep_ref,
    *rest,
):
    att_ref, dq_ref, back_ref, local_ref = rest[-27:-23]
    k_all, v_all, k_t, v_t, bias_all, s_all, p_all, g_all, delta_all, ds_all = rest[-23:-13]
    dk_all, dv_all, q_all, do_all, att_all, dq_all, back_all, local_all = rest[-13:-5]
    arrive, leave, arrive_far, arrive_own, leave_back = rest[-5:]
    keys = k_t.shape[1]
    per = TILE // rows
    tiles = [pl.ds(at, TILE) for at in range(0, keys, TILE)]
    own_columns = pl.ds(group * HEAD_SIZE, HEAD_SIZE)

    def tile_of(held, at):
        return held[pl.ds(at.start // rows, per)].reshape(TILE, HEAD_SIZE)

    def fetch_keys(i, held):
        return [
            pltpu.make_async_copy(far_ref.at[:, i], held.at[pl.ds(0, REACH)], arrive_far.at[i]),
            pltpu.make_async_copy(
                own_ref.at[i, :, :, own_columns], held.at[pl.ds(REACH, 2)], arrive_own.at[i]
            ),
        ]

    def send_back(at):
        slot = at.start // rows
        if slot < REACH:
            source, target = back_all.at[pl.ds(slot, per)], back_ref.at[pl.ds(slot, per)]
        else:
            source, target = local_all, local_ref
        return pltpu.make_async_copy(source, target, leave_back.at[slot // per])

    def columns(head):
        return pl.ds((group * GROUP + head) * HEAD_SIZE, HEAD_SIZE)

    def fetches(head):
        return [
            pltpu.make_async_copy(
                source.at[:, :, columns(head)], held.at[head], arrive.at[head, i]
            )
            for i, (source, held) in enumerate(((q_ref, q_all), (do_ref, do_all)))
        ]

    def send(held, target, head, i):
        return pltpu.make_async_copy(
            held.at[head], target.at[:, :, columns(head)], leave.at[head, i]
        )

    def rows_of(held, head):
        return held[head].reshape(2 * rows, HEAD_SIZE)

    def scores(head):
        for fetch in fetches(head):
            fetch.wait()
        q = rows_of(q_all, head)
        q_t = q.T
        top = jnp.full((8, 2 * rows), NEGATIVE, jnp.float32)
        for at in tiles:
            s = dot(tile_of(k_all, at), q_t) + bias_all[at, :]
            s_all[head % 2, at, :] = s
            top = jnp.maximum(top, fold(s, jnp.max))
            yield
        state[head] = jnp.max(top, 0, keepdims=True)

    def weights(head):
        top = state[head]
        total = jnp.zeros((8, 2 * rows), jnp.float32)
        for at in tiles:
            e = jnp.exp2((s_all[head % 2, at, :] - top) * SCALE_LOG2)
            p_all[head % SLOTS, at, :] = e.astype(jnp.bfloat16)
            total = total + fold(e, jnp.sum)
            yield
        state[head] = 1.0 / jnp.sum(total, 0, keepdims=True)

    def output(head):
        inverse = state[head]
        out_t = dot(v_t[...], p_all[head % SLOTS]) * inverse
        yield
        att_all[head] = out_t.T.astype(jnp.bfloat16).reshape(2, rows, HEAD_SIZE)
        send(att_all, att_ref, head, 0).start()
        yield
        out_t = out_t.astype(jnp.bfloat16).astype(jnp.float32)
        do_t = rows_of(do_all, head).astype(jnp.float32).T
        yield
        g_t = (do_t * (inverse * keep_ref[0:1, :])).astype(jnp.bfloat16)
        g_all[head % 2] = g_t
        delta = jnp.sum(g_t.astype(jnp.float32) * out_t, 0, keepdims=True)
        delta_all[head % 2] = jnp.broadcast_to(delta, (8, 2 * rows))
        yield

    def score_grads(head):
        g_t = g_all[head % 2]
        delta = delta_all[head % 2, 0:1, :]
        for at in tiles:
            dp = dot(tile_of(v_all, at), g_t)
            p = p_all[head % SLOTS, at, :].astype(jnp.float32)
            ds_all[head % 2, at, :] = (p * (dp - delta)).astype(jnp.bfloat16)
            yield

    def key_grads(head):
        q = rows_of(q_all, head)
        g = g_all[head % 2].T
        for at in tiles:
            dk = dot(ds_all[head % 2, at, :], q)
            dv = dot(p_all[head % SLOTS, at, :], g)
            if head > 0:
                dk = dk_all[at, :] + dk
                dv = dv_all[at, :] + dv
            if head < GROUP - 1:
                dk_all[at, :] = dk
                dv_all[at, :] = dv
            else:
                slot = at.start // rows
                for i, total in enumerate((dk * SCALE, dv)):
                    total = total.reshape(per, rows, HEAD_SIZE)
                    if slot < REACH:
                        back_all[pl.ds(slot, per), i] = total.astype(jnp.bfloat16)
                    else:
                        local_all[i] = total
                send_back(at).start()
            yield

    def query_grads(head):
        dq_t = dot(k_t[...], ds_all[head % 2]) * SCALE
        yield
        dq_all[head] = dq_t.T.astype(jnp.bfloat16).reshape(2, rows, HEAD_SIZE)
        send(dq_all, dq_ref, head, 1).start()
        yield

    def together(*parts):
        parts = list(parts)
        while parts:
            parts = [part for part in parts if next(part, part) is not part]

    def flip():
        for slot in range(REACH + 2):
            at = pl.ds(slot * rows, rows)
            k_t[:, at] = k_all[slot].T
            v_t[:, at] = v_all[slot].T
            if slot % per:
                yield

    for i, held in enumerate((k_all, v_all)):
        for fetch in fetch_keys(i, held):
            fetch.start()
        for fetch in fetches(i):
            fetch.start()
    for head in range(2, GROUP):
        for fetch in fetches(head):
            fetch.start()
    key = lax.broadcasted_iota(jnp.int32, (rows, 2 * rows), 0)
    starts = starts_ref[0:1, :]
    for slot in range(REACH):
        visible = key + base_ref[slot] >= starts
        bias_all[pl.ds(slot * rows, rows), :] = jnp.where(visible, 0.0, NEGATIVE)
    bias_all[pl.ds(REACH * rows, 2 * rows), :] = near_ref[...]
    for i, held in enumerate((k_all, v_all)):
        for fetch in fetch_keys(i, held):
            fetch.wait()

    state = {}
    for turn in range(-3, GROUP):
        ready = lambda head: 0 <= head < GROUP
        parts = []
        if ready(turn + 1):
            parts.append(output(turn + 1))
        if ready(turn):
            parts.append(score_grads(turn))
        if ready(turn + 3):
            parts.append(scores(turn + 3))
        if ready(turn - 1):
            parts.append(query_grads(turn - 1))
        if turn == -3:
            parts.append(flip())
        together(*parts)
        parts = []
        if ready(turn):
            parts.append(key_grads(turn))
        if ready(turn + 2):
            parts.append(weights(turn + 2))
        together(*parts)
    together(query_grads(GROUP - 1))

    for at in tiles:
        send_back(at).wait()
    for head in range(GROUP):
        send(att_all, att_ref, head, 0).wait()
        send(dq_all, dq_ref, head, 1).wait()


def attend(group, queries, d_out, far, keys_values, base, starts, near, keep, earlier):
    rows = queries.shape[1]
    keys = (REACH + 2) * rows
    whole = lambda shape: pl.BlockSpec(shape, lambda step: (0,) * len(shape))
    hbm = pl.BlockSpec(memory_space=pltpu.HBM)
    far_shape = (REACH, 2, rows, HEAD_SIZE)
    local_shape = (2, 2, rows, HEAD_SIZE)
    held = pltpu.VMEM((GROUP, 2, rows, HEAD_SIZE), jnp.bfloat16)
    flops = 6 * 2 * keys * 2 * rows * HEAD_SIZE * GROUP
    return pl.pallas_call(
        functools.partial(kernel, rows, group),
        grid=(1,),
        in_specs=[
            hbm,
            hbm,
            hbm,
            hbm,
            pl.BlockSpec(memory_space=pltpu.SMEM),
            whole((8, 2 * rows)),
            whole((2 * rows, 2 * rows)),
            whole((8, 2 * rows)),
        ]
        + [hbm] * len(earlier),
        out_specs=[hbm, hbm, hbm, hbm],
        out_shape=[
            jax.ShapeDtypeStruct(queries.shape, jnp.bfloat16),
            jax.ShapeDtypeStruct(queries.shape, jnp.bfloat16),
            jax.ShapeDtypeStruct(far_shape, jnp.bfloat16),
            jax.ShapeDtypeStruct(local_shape, jnp.float32),
        ],
        scratch_shapes=[
            pltpu.VMEM((REACH + 2, rows, HEAD_SIZE), jnp.bfloat16),
            pltpu.VMEM((REACH + 2, rows, HEAD_SIZE), jnp.bfloat16),
            pltpu.VMEM((HEAD_SIZE, keys), jnp.bfloat16),
            pltpu.VMEM((HEAD_SIZE, keys), jnp.bfloat16),
            pltpu.VMEM((keys, 2 * rows), jnp.float32),
            pltpu.VMEM((2, keys, 2 * rows), jnp.float32),
            pltpu.VMEM((SLOTS, keys, 2 * rows), jnp.bfloat16),
            pltpu.VMEM((2, HEAD_SIZE, 2 * rows), jnp.bfloat16),
            pltpu.VMEM((2, 8, 2 * rows), jnp.float32),
            pltpu.VMEM((2, keys, 2 * rows), jnp.bfloat16),
            pltpu.VMEM((keys, HEAD_SIZE), jnp.float32),
            pltpu.VMEM((keys, HEAD_SIZE), jnp.float32),
            held,
            held,
            held,
            held,
            pltpu.VMEM(far_shape, jnp.bfloat16),
            pltpu.VMEM(local_shape, jnp.float32),
            pltpu.SemaphoreType.DMA((GROUP, 2)),
            pltpu.SemaphoreType.DMA((GROUP, 2)),
            pltpu.SemaphoreType.DMA((2,)),
            pltpu.SemaphoreType.DMA((2,)),
            pltpu.SemaphoreType.DMA((keys // TILE,)),
        ],
        input_output_aliases={8 + i: i for i in range(len(earlier))},
        compiler_params=pltpu.CompilerParams(vmem_limit_bytes=VMEM_LIMIT),
        cost_estimate=pl.CostEstimate(
            flops=2 * flops, bytes_accessed=6 * 2**20, transcendentals=keys * 2 * rows * GROUP
        ),
        name=f"attend_{group}",
    )(queries, d_out, far, keys_values, base, starts, near, keep, *earlier)


def masks(doc_start, slab, place, places):
    rows = doc_start.shape[0]
    offset = jnp.arange(rows, dtype=jnp.int32)
    starts = jnp.concatenate([doc_start, doc_start])[None, :]
    slot = jnp.arange(REACH, dtype=jnp.int32)
    base = rows * (places * slab + slot - jnp.where(slot >= place, places, 0))
    same = doc_start[:, None] == starts
    k_blk = (offset // BLOCK)[:, None]
    q_blk = jnp.concatenate([offset // BLOCK] * 2)[None, :]
    noisy = (jnp.arange(2 * rows, dtype=jnp.int32) >= rows)[None, :]
    own_clean = same & (k_blk + noisy.astype(jnp.int32) <= q_blk)
    own_noisy = same & noisy & (k_blk == q_blk)
    near = jnp.where(jnp.concatenate([own_clean, own_noisy], 0), 0.0, NEGATIVE)
    return base, jnp.broadcast_to(starts, (8, 2 * rows)), near.astype(jnp.float32)


def local(queries, keys_values, d_out, doc_start, block_bits):
    rows = queries.shape[1]
    slabs, places = lax.axis_size("slab"), lax.axis_size("place")
    slab, place, head = (lax.axis_index(a) for a in ("slab", "place", "head"))
    kv_heads = keys_values.shape[3] // HEAD_SIZE
    later = [(i, i + 1) for i in range(slabs - 1)]
    sooner = [(i + 1, i) for i in range(slabs - 1)]
    slot = jnp.arange(places, dtype=jnp.int32)[:, None, None, None]
    after = slot > place

    own = keys_values[:, 0]
    before = lax.ppermute(own, "slab", later)
    far = []
    for group in range(kv_heads):
        part = slice(group * HEAD_SIZE, (group + 1) * HEAD_SIZE)
        send = jnp.where(after, own[None, :, :, part], before[None, :, :, part])
        far.append(lax.all_to_all(send, "place", 0, 0))

    other = lax.ppermute(block_bits, "head", [(0, 1), (1, 0)])
    bits = jnp.where(
        head == 0,
        jnp.concatenate([block_bits, other]),
        jnp.concatenate([other, block_bits]),
    )
    keep = jnp.concatenate([jnp.ones((rows,), jnp.int32), jnp.repeat(bits, BLOCK)])
    keep = jnp.broadcast_to(keep.astype(jnp.float32)[None, :], (8, 2 * rows))
    base, starts, near = masks(doc_start, slab, place, places)

    earlier = ()
    totals, noisy = [], []
    for group in range(kv_heads):
        att, dq, back, mine = attend(
            group, queries, d_out, far[group], keys_values, base, starts, near, keep, earlier
        )
        earlier = (att, dq)
        if totals:
            back, totals[-1] = lax.optimization_barrier((back, totals[-1]))
        terms = lax.all_to_all(back, "place", 0, 0)
        totals.append(terms)
        noisy.append(mine)
    for group, (terms, mine) in enumerate(zip(totals, noisy)):
        terms = terms.astype(jnp.float32)
        here = jnp.sum(jnp.where(after, terms, 0.0), 0)
        there = jnp.sum(jnp.where(after, 0.0, terms), 0).astype(jnp.bfloat16)
        arrived = lax.ppermute(there, "slab", sooner)
        totals[group] = mine[:, 0] + here + arrived.astype(jnp.float32)
        noisy[group] = mine[:, 1]
    grad = jnp.stack([jnp.concatenate(totals, -1), jnp.concatenate(noisy, -1)], 1)
    return att, dq, grad.astype(jnp.bfloat16)


def solution(mesh):
    shards, heads = mesh.devices.shape
    cut = Mesh(mesh.devices.reshape(shards // REACH, REACH, heads), ("slab", "place", "head"))
    pos = ("slab", "place")
    in_specs = (
        P(None, pos, "head"),
        P(None, None, pos, "head"),
        P(None, pos, "head"),
        P(pos),
        P((*pos, "head")),
    )
    out_specs = (P(None, pos, "head"), P(None, pos, "head"), P(None, None, pos, "head"))
    return jax.shard_map(local, mesh=cut, in_specs=in_specs, out_specs=out_specs, check_vma=False)
```

time: 145 us -> 121 us (0.83)
  blocking collectives: 22.3 us -> 0 us
  starting transfers between devices: 24.8 us -> 32.8 us
  Pallas kernels: 45.2 us -> 37.9 us
  local copies, waits for them, and re-layouts: 9.96 us -> 5.02 us
  waiting for transfers between devices: 36.8 us -> 39.4 us
    all_to_all x1 -> x0, blocking collectives: 22.3 us -> none  [local(): terms = lax.all_to_all(back, 'place', 0, 0).astype(jnp.float32)]
    all_to_all x1 -> x2, starting transfers between devices: 3.65 us -> 14.5 us  [local(): terms = lax.all_to_all(back, 'place', 0, 0)]
    pallas_call x2, Pallas kernels: 45.2 us -> 37.9 us  [attend(): pl.pallas_call(functools.partial(kernel, rows, group), grid=(1,), in_spec...]
    unnamed x22 -> x14, local copies, waits for them, and re-layouts: 8.89 us -> 2.68 us
    ppermute x2 -> x1, starting transfers between devices: 5.45 us -> 3.53 us  [local(): before = lax.ppermute(own, 'slab', later)]
    all_to_all x1 -> x2, waiting for transfers between devices: 14.4 us -> 15.3 us  [local(): terms = lax.all_to_all(back, 'place', 0, 0)]
    ppermute x2 -> x1, waiting for transfers between devices: 2.78 us -> 3.61 us  [local(): before = lax.ppermute(own, 'slab', later)]
  transfers between devices with their start and end apart: 8 -> 8, of which waited for: 5 -> 5; matrix products, arithmetic and copies ran while one was open for 4% -> 5% of each run, Pallas kernels for 15% -> 32%
where the time goes in v2:
time: 121 us; the launch traced here: 120 us
  waiting for transfers between devices  39.4 us (33%)
  Pallas kernels  37.9 us (31%)
  starting transfers between devices  32.8 us (27%)
  local copies, waits for them, and re-layouts  5.02 us (4%)
  other arithmetic  3.99 us (3%)
    pallas_call x2, Pallas kernels, attend(): pl.pallas_call(functools.partial(kernel, rows, group), grid=(1,), in_spec...  37.9 us
    all_to_all x2, waiting for transfers between devices, local(): far.append(lax.all_to_all(send, 'place', 0, 0))  16.3 us
    all_to_all x2, waiting for transfers between devices, local(): terms = lax.all_to_all(back, 'place', 0, 0)  15.3 us
    all_to_all x2, starting transfers between devices, local(): terms = lax.all_to_all(back, 'place', 0, 0)  14.5 us
    all_to_all x2, starting transfers between devices, local(): far.append(lax.all_to_all(send, 'place', 0, 0))  10.8 us
    ppermute x2, waiting for transfers between devices, local(): arrived = lax.ppermute(there, 'slab', sooner)  4.2 us
    ppermute x2, starting transfers between devices, local(): arrived = lax.ppermute(there, 'slab', sooner)  3.94 us
    ppermute x1, waiting for transfers between devices, local(): before = lax.ppermute(own, 'slab', later)  3.61 us
  transfers between devices with their start and end apart: 8, of which 5 were waited for; matrix products, arithmetic and copies ran while one was open for 5% of the time, Pallas kernels for 32%

profile of v2, /device:TPU:64, one launch (start us, length us, event | category | flops | bytes accessed | tf_op | source)
XLA Modules:
  0.0 120.1 jit_solution(18023492603092279776)
XLA Ops:
  0.6 0.1 collective-permute-start.1
  0.7 0.9 slice_bitcast_fusion.2
  1.6 3.5 %collective-permute-start = (bf16[2,128,256]{2,1,0:T(8,128)(2,1)S(1)}, bf16[2,128,256]{2,1,0:T(8,128)(2,1)S(1)}, u32[]{:S(2)}, u32[]{:S(2)}) collective-permute-start(bf16[2,128,256]{2,1,0:T(8,128)(2,1)S(1)} %slice_bitcast_fusion.2), channel_id=1, source_target_pairs={{0,32},{32,64},{64,96},{1,33},{33,65},{65,97},{2,34},{34,66},{66,9... | collective-permute-start | bytes 393224 | tf_op jit(solution)/shard_map/ppermute | solution.py:326
  5.3 0.6 fusion.14.base_ref
  5.8 3.6 %collective-permute-done = bf16[2,128,256]{2,1,0:T(8,128)(2,1)S(1)} collective-permute-done((bf16[2,128,256]{2,1,0:T(8,128)(2,1)S(1)}, bf16[2,128,256]{2,1,0:T(8,128)(2,1)S(1)}, u32[]{:S(2)}, u32[]{:S(2)}) %collective-permute-start) | collective-permute-done | bytes 131104 | tf_op jit(solution)/shard_map/ppermute | solution.py:326
  9.5 1.6 %broadcast_select_fusion = (bf16[16,2,128,128]{3,2,1,0:T(8,128)(2,1)}, bf16[16,2,128,128]{3,2,1,0:T(8,128)(2,1)}) fusion(pred[16]{0:T(512)(128)(4,1)S(1)} %iota_compare_fusion.1, bf16[2,128,128]{2,1,0:T(8,128)(2,1)S(1)} %get-tuple-element.34, bf16[2,128,128]{2,1,0:T(8,128)(2,1)S(1)} %get-tuple-element.32, bf16[2,128,128]{2,1,0:T(8,128)(2,1)S(1)} %get-tuple-element.35, ...), kind=kLoop, calls=%fused_computation.8 | loop fusion | flops 1048576 | bytes 2359312 | tf_op jit(solution)/shard_map/jit(_where)/select_n | solution.py:330
  11.0 0.0 copy-start.4
  11.0 0.0 copy-start.5
  11.0 7.2 %all-to-all-start.1 = ((bf16[16,2,128,128]{3,2,1,0:T(8,128)(2,1)}), bf16[16,2,128,128]{3,2,1,0:T(8,128)(2,1)S(1)}, u32[]{:S(2)}, u32[]{:S(2)}) async-start(bf16[16,2,128,128]{3,2,1,0:T(8,128)(2,1)} %get-tuple-element.38), calls=%async_computation.1 | async-start | bytes 2097152 | tf_op jit(solution)/shard_map/all_to_all | solution.py:331
  18.2 0.0 copy-done.4
  18.3 0.1 compare_and_fusion.1
  18.4 0.7 add_select_fusion.near_ref
  19.1 0.0 collective-permute-done.1
  19.1 0.0 copy-done.5
  19.1 0.1 broadcast_select_fusion.2
  19.2 0.1 broadcast_in_dim.112
  19.3 0.1 reshape.43
  19.4 16.3 %all-to-all-done.1.far_ref = bf16[16,2,128,128]{3,2,1,0:T(8,128)(2,1)S(1)} async-done(((bf16[16,2,128,128]{3,2,1,0:T(8,128)(2,1)}), bf16[16,2,128,128]{3,2,1,0:T(8,128)(2,1)S(1)}, u32[]{:S(2)}, u32[]{:S(2)}) %all-to-all-start.1) | async-done | bytes 1048608 | tf_op jit(solution)/shard_map/all_to_all | solution.py:331
  35.7 0.0 copy-start
  35.7 1.0 copy-done
  36.7 3.7 %all-to-all-start = ((bf16[16,2,128,128]{3,2,1,0:T(8,128)(2,1)}), bf16[16,2,128,128]{3,2,1,0:T(8,128)(2,1)S(1)}, u32[]{:S(2)}, u32[]{:S(2)}) async-start(bf16[16,2,128,128]{3,2,1,0:T(8,128)(2,1)} %get-tuple-element.39), calls=%async_computation | async-start | bytes 2097152 | tf_op jit(solution)/shard_map/all_to_all | solution.py:331
  40.3 0.6 broadcast_in_dim.109.starts_ref
  40.9 0.6 broadcast_in_dim.113.keep_ref
  41.5 18.9 %attend_0.1 = (bf16[2,128,2048]{2,1,0:T(8,128)(2,1)}, bf16[2,128,2048]{2,1,0:T(8,128)(2,1)}, bf16[16,2,128,128]{3,2,1,0:T(8,128)(2,1)}, f32[2,2,128,128]{3,2,1,0:T(8,128)}) custom-call(bf16[2,128,2048]{2,1,0:T(8,128)(2,1)} %q_ref.3, bf16[2,128,2048]{2,1,0:T(8,128)(2,1)} %do_ref.3, bf16[16,2,128,128]{3,2,1,0:T(8,128)(2,1)} %copy-done, ...), custom_call_target="tpu_custom_call" | custom-call | flops 14495514624 | bytes 6291456 | tf_op jit(solution)/shard_map/attend_0/pallas_call | solution.py:244
  60.4 0.0 all-to-all-done.far_ref
  60.5 0.0 copy-start.1
  60.5 1.0 copy-done.1
  61.4 7.1 %all-to-all-start.2 = ((bf16[16,2,128,128]{3,2,1,0:T(8,128)(2,1)}), bf16[16,2,128,128]{3,2,1,0:T(8,128)(2,1)S(1)}, u32[]{:S(2)}, u32[]{:S(2)}) async-start(bf16[16,2,128,128]{3,2,1,0:T(8,128)(2,1)} %get-tuple-element.19), calls=%async_computation.2 | async-start | bytes 2097152 | tf_op jit(solution)/shard_map/all_to_all | solution.py:352
  68.6 19.0 %attend_1.1 = (bf16[2,128,2048]{2,1,0:T(8,128)(2,1)}, bf16[2,128,2048]{2,1,0:T(8,128)(2,1)}, bf16[16,2,128,128]{3,2,1,0:T(8,128)(2,1)}, f32[2,2,128,128]{3,2,1,0:T(8,128)}) custom-call(bf16[2,128,2048]{2,1,0:T(8,128)(2,1)} %q_ref.3, bf16[2,128,2048]{2,1,0:T(8,128)(2,1)} %do_ref.3, ...), custom_call_target="tpu_custom_call", output_to_operand_aliasing={{0}: (8, {}), {1}: (9, {})} | custom-call | flops 14495514624 | bytes 6291456 | tf_op jit(solution)/shard_map/attend_1/pallas_call | solution.py:244
  87.5 0.0 all-to-all-done.2
  87.5 0.0 copy-start.3
  87.6 0.0 copy-start.2
  87.6 7.3 %all-to-all-start.3 = ((bf16[16,2,128,128]{3,2,1,0:T(8,128)(2,1)}), bf16[16,2,128,128]{3,2,1,0:T(8,128)(2,1)S(1)}, u32[]{:S(2)}, u32[]{:S(2)}) async-start(bf16[16,2,128,128]{3,2,1,0:T(8,128)(2,1)} %get-tuple-element.22), calls=%async_computation.3 | async-start | bytes 2097152 | tf_op jit(solution)/shard_map/all_to_all | solution.py:352
  94.9 0.0 copy-done.3
  94.9 0.0 copy-done.2
  95.0 15.3 %all-to-all-done.3 = bf16[16,2,128,128]{3,2,1,0:T(8,128)(2,1)S(1)} async-done(((bf16[16,2,128,128]{3,2,1,0:T(8,128)(2,1)}), bf16[16,2,128,128]{3,2,1,0:T(8,128)(2,1)S(1)}, u32[]{:S(2)}, u32[]{:S(2)}) %all-to-all-start.3) | async-done | bytes 1048608 | tf_op jit(solution)/shard_map/all_to_all | solution.py:352
  110.3 0.8 fusion.1
  111.0 2.0 %collective-permute-start.2 = (bf16[2,128,128]{2,1,0:T(8,128)(2,1)S(1)}, bf16[2,128,128]{2,1,0:T(8,128)(2,1)S(1)}, u32[]{:S(2)}, u32[]{:S(2)}) collective-permute-start(bf16[2,128,128]{2,1,0:T(8,128)(2,1)S(1)} %get-tuple-element.26), channel_id=1, source_target_pairs={{32,0},{64,32},{96,64},{33,1},{65,33},{97,65},{34,2},{66,34},{98,6... | collective-permute-start | bytes 196616 | tf_op jit(solution)/shard_map/ppermute | solution.py:359
  113.1 1.9 %collective-permute-start.3 = (bf16[2,128,128]{2,1,0:T(8,128)(2,1)S(1)}, bf16[2,128,128]{2,1,0:T(8,128)(2,1)S(1)}, u32[]{:S(2)}, u32[]{:S(2)}) collective-permute-start(bf16[2,128,128]{2,1,0:T(8,128)(2,1)S(1)} %get-tuple-element.31), channel_id=1, source_target_pairs={{32,0},{64,32},{96,64},{33,1},{65,33},{97,65},{34,2},{66,34},{98,6... | collective-permute-start | bytes 196616 | tf_op jit(solution)/shard_map/ppermute | solution.py:359
  115.0 2.2 %collective-permute-done.2 = bf16[2,128,128]{2,1,0:T(8,128)(2,1)S(1)} collective-permute-done((bf16[2,128,128]{2,1,0:T(8,128)(2,1)S(1)}, bf16[2,128,128]{2,1,0:T(8,128)(2,1)S(1)}, u32[]{:S(2)}, u32[]{:S(2)}) %collective-permute-start.2) | collective-permute-done | bytes 65568 | tf_op jit(solution)/shard_map/ppermute | solution.py:359
  117.2 2.0 %collective-permute-done.3 = bf16[2,128,128]{2,1,0:T(8,128)(2,1)S(1)} collective-permute-done((bf16[2,128,128]{2,1,0:T(8,128)(2,1)S(1)}, bf16[2,128,128]{2,1,0:T(8,128)(2,1)S(1)}, u32[]{:S(2)}, u32[]{:S(2)}) %collective-permute-start.3) | collective-permute-done | bytes 65568 | tf_op jit(solution)/shard_map/ppermute | solution.py:359
  119.3 0.7 copy.13
  (17 shorter events, 0.3 us)
Async XLA Ops:
  0.6 18.5 %collective-permute-start.1 = (s32[4]{0:T(128)}, s32[4]{0:T(128)S(1)}, u32[]{:S(2)}, u32[]{:S(2)}) collective-permute-start(s32[4]{0:T(128)} %param.9), channel_id=1, source_target_pairs={{0,1},{1,0},{2,3},{3,2},{4,5},{5,4},{6,7},{7,6},{8,9},{9,8},{10,11... | collective-permute-start | bytes 56 | tf_op jit(solution)/shard_map/ppermute | solution.py:333
  1.6 7.8 %collective-permute-start = (bf16[2,128,256]{2,1,0:T(8,128)(2,1)S(1)}, bf16[2,128,256]{2,1,0:T(8,128)(2,1)S(1)}, u32[]{:S(2)}, u32[]{:S(2)}) collective-permute-start(bf16[2,128,256]{2,1,0:T(8,128)(2,1)S(1)} %slice_bitcast_fusion.2), channel_id=1, source_target_pairs={{0,32},{32,64},{64,96},{1,33},{33,65},{65,97},{2,34},{34,66},{66,9... | collective-permute-start | bytes 393224 | tf_op jit(solution)/shard_map/ppermute | solution.py:326
  11.0 7.2 %copy-start.4 = (s32[128]{0:T(128)S(1)}, s32[128]{0:T(128)}, u32[]{:S(2)}) copy-start(s32[128]{0:T(128)} %param.8) | copy-start | bytes 1540
  11.0 8.1 %copy-start.5 = (s32[4]{0:T(128)S(1)}, s32[4]{0:T(128)}, u32[]{:S(2)}) copy-start(s32[4]{0:T(128)} %param.9) | copy-start | bytes 52
  11.0 24.7 %all-to-all-start.1 = ((bf16[16,2,128,128]{3,2,1,0:T(8,128)(2,1)}), bf16[16,2,128,128]{3,2,1,0:T(8,128)(2,1)S(1)}, u32[]{:S(2)}, u32[]{:S(2)}) async-start(bf16[16,2,128,128]{3,2,1,0:T(8,128)(2,1)} %get-tuple-element.38), calls=%async_computation.1 | async-start | bytes 2097152 | tf_op jit(solution)/shard_map/all_to_all | solution.py:331
  35.7 1.0 copy-start
  36.7 23.8 %all-to-all-start = ((bf16[16,2,128,128]{3,2,1,0:T(8,128)(2,1)}), bf16[16,2,128,128]{3,2,1,0:T(8,128)(2,1)S(1)}, u32[]{:S(2)}, u32[]{:S(2)}) async-start(bf16[16,2,128,128]{3,2,1,0:T(8,128)(2,1)} %get-tuple-element.39), calls=%async_computation | async-start | bytes 2097152 | tf_op jit(solution)/shard_map/all_to_all | solution.py:331
  60.5 1.0 copy-start.1
  61.4 26.1 %all-to-all-start.2 = ((bf16[16,2,128,128]{3,2,1,0:T(8,128)(2,1)}), bf16[16,2,128,128]{3,2,1,0:T(8,128)(2,1)S(1)}, u32[]{:S(2)}, u32[]{:S(2)}) async-start(bf16[16,2,128,128]{3,2,1,0:T(8,128)(2,1)} %get-tuple-element.19), calls=%async_computation.2 | async-start | bytes 2097152 | tf_op jit(solution)/shard_map/all_to_all | solution.py:352
  87.5 7.4 %copy-start.3 = (f32[2,2,128,128]{3,2,1,0:T(8,128)S(1)}, f32[2,2,128,128]{3,2,1,0:T(8,128)}, u32[]{:S(2)}) copy-start(f32[2,2,128,128]{3,2,1,0:T(8,128)} %get-tuple-element.21) | copy-start | bytes 786436
  87.6 7.4 %copy-start.2 = (f32[2,2,128,128]{3,2,1,0:T(8,128)S(1)}, f32[2,2,128,128]{3,2,1,0:T(8,128)}, u32[]{:S(2)}) copy-start(f32[2,2,128,128]{3,2,1,0:T(8,128)} %get-tuple-element.17) | copy-start | bytes 786436
  87.6 22.7 %all-to-all-start.3 = ((bf16[16,2,128,128]{3,2,1,0:T(8,128)(2,1)}), bf16[16,2,128,128]{3,2,1,0:T(8,128)(2,1)S(1)}, u32[]{:S(2)}, u32[]{:S(2)}) async-start(bf16[16,2,128,128]{3,2,1,0:T(8,128)(2,1)} %get-tuple-element.22), calls=%async_computation.3 | async-start | bytes 2097152 | tf_op jit(solution)/shard_map/all_to_all | solution.py:352
  111.0 6.2 %collective-permute-start.2 = (bf16[2,128,128]{2,1,0:T(8,128)(2,1)S(1)}, bf16[2,128,128]{2,1,0:T(8,128)(2,1)S(1)}, u32[]{:S(2)}, u32[]{:S(2)}) collective-permute-start(bf16[2,128,128]{2,1,0:T(8,128)(2,1)S(1)} %get-tuple-element.26), channel_id=1, source_target_pairs={{32,0},{64,32},{96,64},{33,1},{65,33},{97,65},{34,2},{66,34},{98,6... | collective-permute-start | bytes 196616 | tf_op jit(solution)/shard_map/ppermute | solution.py:359
  113.1 6.2 %collective-permute-start.3 = (bf16[2,128,128]{2,1,0:T(8,128)(2,1)S(1)}, bf16[2,128,128]{2,1,0:T(8,128)(2,1)S(1)}, u32[]{:S(2)}, u32[]{:S(2)}) collective-permute-start(bf16[2,128,128]{2,1,0:T(8,128)(2,1)S(1)} %get-tuple-element.31), channel_id=1, source_target_pairs={{32,0},{64,32},{96,64},{33,1},{65,33},{97,65},{34,2},{66,34},{98,6... | collective-permute-start | bytes 196616 | tf_op jit(solution)/shard_map/ppermute | solution.py:359

commit v3 on v2

--- a/solution.py
+++ b/solution.py
@@ -20,7 +20,7 @@
 SCALE_LOG2 = SCALE * math.log2(math.e)
 TILE = 256
 SLOTS = 3
-VMEM_LIMIT = 60 * 2**20
+VMEM_LIMIT = 50 * 2**20
 
 NT = (((1,), (1,)), ((), ()))
 
@@ -126,7 +126,7 @@
         out_t = out_t.astype(jnp.bfloat16).astype(jnp.float32)
         do_t = rows_of(do_all, head).astype(jnp.float32).T
         yield
-        g_t = (do_t * (inverse * keep_ref[0:1, :])).astype(jnp.bfloat16)
+        g_t = (do_t * (inverse * keep_ref[...])).astype(jnp.bfloat16)
         g_all[head % 2] = g_t
         delta = jnp.sum(g_t.astype(jnp.float32) * out_t, 0, keepdims=True)
         delta_all[head % 2] = jnp.broadcast_to(delta, (8, 2 * rows))
@@ -193,7 +193,7 @@
         for fetch in fetches(head):
             fetch.start()
     key = lax.broadcasted_iota(jnp.int32, (rows, 2 * rows), 0)
-    starts = starts_ref[0:1, :]
+    starts = starts_ref[...]
     for slot in range(REACH):
         visible = key + base_ref[slot] >= starts
         bias_all[pl.ds(slot * rows, rows), :] = jnp.where(visible, 0.0, NEGATIVE)
@@ -236,7 +236,7 @@
     rows = queries.shape[1]
     keys = (REACH + 2) * rows
     whole = lambda shape: pl.BlockSpec(shape, lambda step: (0,) * len(shape))
-    hbm = pl.BlockSpec(memory_space=pltpu.HBM)
+    hbm = pl.BlockSpec(memory_space=pl.ANY)
     far_shape = (REACH, 2, rows, HEAD_SIZE)
     local_shape = (2, 2, rows, HEAD_SIZE)
     held = pltpu.VMEM((GROUP, 2, rows, HEAD_SIZE), jnp.bfloat16)
@@ -250,9 +250,9 @@
             hbm,
             hbm,
             pl.BlockSpec(memory_space=pltpu.SMEM),
-            whole((8, 2 * rows)),
+            whole((1, 2 * rows)),
             whole((2 * rows, 2 * rows)),
-            whole((8, 2 * rows)),
+            whole((1, 2 * rows)),
         ]
         + [hbm] * len(earlier),
         out_specs=[hbm, hbm, hbm, hbm],
@@ -309,7 +309,7 @@
     own_clean = same & (k_blk + noisy.astype(jnp.int32) <= q_blk)
     own_noisy = same & noisy & (k_blk == q_blk)
     near = jnp.where(jnp.concatenate([own_clean, own_noisy], 0), 0.0, NEGATIVE)
-    return base, jnp.broadcast_to(starts, (8, 2 * rows)), near.astype(jnp.float32)
+    return base, starts, near.astype(jnp.float32)
 
 
 def local(queries, keys_values, d_out, doc_start, block_bits):
@@ -337,7 +337,7 @@
         jnp.concatenate([other, block_bits]),
     )
     keep = jnp.concatenate([jnp.ones((rows,), jnp.int32), jnp.repeat(bits, BLOCK)])
-    keep = jnp.broadcast_to(keep.astype(jnp.float32)[None, :], (8, 2 * rows))
+    keep = keep.astype(jnp.float32)[None, :]
     base, starts, near = masks(doc_start, slab, place, places)
 
     earlier = ()
@@ -352,14 +352,15 @@
         terms = lax.all_to_all(back, "place", 0, 0)
         totals.append(terms)
         noisy.append(mine)
-    for group, (terms, mine) in enumerate(zip(totals, noisy)):
+    here, there = [], []
+    for terms in totals:
         terms = terms.astype(jnp.float32)
-        here = jnp.sum(jnp.where(after, terms, 0.0), 0)
-        there = jnp.sum(jnp.where(after, 0.0, terms), 0).astype(jnp.bfloat16)
-        arrived = lax.ppermute(there, "slab", sooner)
-        totals[group] = mine[:, 0] + here + arrived.astype(jnp.float32)
-        noisy[group] = mine[:, 1]
-    grad = jnp.stack([jnp.concatenate(totals, -1), jnp.concatenate(noisy, -1)], 1)
+        here.append(jnp.sum(jnp.where(after, terms, 0.0), 0))
+        there.append(jnp.sum(jnp.where(after, 0.0, terms), 0).astype(jnp.bfloat16))
+    arrived = lax.ppermute(jnp.concatenate(there, -1), "slab", sooner)
+    clean = jnp.concatenate([a + b[:, 0] for a, b in zip(here, noisy)], -1)
+    clean = clean + arrived.astype(jnp.float32)
+    grad = jnp.stack([clean, jnp.concatenate([b[:, 1] for b in noisy], -1)], 1)
     return att, dq, grad.astype(jnp.bfloat16)
 
 

time: 121 us -> 118 us (0.975)
  local copies, waits for them, and re-layouts: 5.02 us -> 2.92 us
    ppermute x2 -> x1, starting transfers between devices: 3.94 us -> 2 us  [local(): arrived = lax.ppermute(jnp.concatenate(there, -1), 'slab', sooner)]
    reduce_sum x1, other arithmetic: 0.78 us -> 2.12 us  [local(): here.append(jnp.sum(jnp.where(after, terms, 0.0), 0))]
    ppermute x2 -> x1, waiting for transfers between devices: 4.2 us -> 4.83 us  [local(): arrived = lax.ppermute(jnp.concatenate(there, -1), 'slab', sooner)]
  transfers between devices with their start and end apart: 8 -> 7, of which waited for: 5 -> 4; matrix products, arithmetic and copies ran while one was open for 5% -> 3% of each run, Pallas kernels for 32% -> 32%
where the time goes in v3:
time: 118 us; the launch traced here: 117 us
  waiting for transfers between devices  40.6 us (34%)
  Pallas kernels  37.1 us (31%)
  starting transfers between devices  31.6 us (27%)
  other arithmetic  4.06 us (3%)
  local copies, waits for them, and re-layouts  2.92 us (2%)
    pallas_call x2, Pallas kernels, attend(): pl.pallas_call(functools.partial(kernel, rows, group), grid=(1,), in_spec...  37.1 us
    all_to_all x2, waiting for transfers between devices, local(): far.append(lax.all_to_all(send, 'place', 0, 0))  17 us
    all_to_all x2, waiting for transfers between devices, local(): terms = lax.all_to_all(back, 'place', 0, 0)  14.6 us
    all_to_all x2, starting transfers between devices, local(): terms = lax.all_to_all(back, 'place', 0, 0)  14.4 us
    all_to_all x2, starting transfers between devices, local(): far.append(lax.all_to_all(send, 'place', 0, 0))  11.6 us
    ppermute x1, waiting for transfers between devices, local(): arrived = lax.ppermute(jnp.concatenate(there, -1), 'slab', sooner)  4.83 us
    ppermute x1, waiting for transfers between devices, local(): before = lax.ppermute(own, 'slab', later)  4.15 us
    ppermute x1, starting transfers between devices, local(): before = lax.ppermute(own, 'slab', later)  3.53 us
  transfers between devices with their start and end apart: 7, of which 4 were waited for; matrix products, arithmetic and copies ran while one was open for 3% of the time, Pallas kernels for 32%

profile of v3, /device:TPU:64, one launch (start us, length us, event | category | flops | bytes accessed | tf_op | source)
XLA Modules:
  0.0 117.1 jit_solution(7290108273552529478)
XLA Ops:
  0.6 0.1 collective-permute-start.1
  0.7 0.9 slice_bitcast_fusion.2
  1.6 3.5 %collective-permute-start = (bf16[2,128,256]{2,1,0:T(8,128)(2,1)S(1)}, bf16[2,128,256]{2,1,0:T(8,128)(2,1)S(1)}, u32[]{:S(2)}, u32[]{:S(2)}) collective-permute-start(bf16[2,128,256]{2,1,0:T(8,128)(2,1)S(1)} %slice_bitcast_fusion.2), channel_id=1, source_target_pairs={{0,32},{32,64},{64,96},{1,33},{33,65},{65,97},{2,34},{34,66},{66,9... | collective-permute-start | bytes 393224 | tf_op jit(solution)/shard_map/ppermute | solution.py:326
  5.3 4.2 %collective-permute-done = bf16[2,128,256]{2,1,0:T(8,128)(2,1)S(1)} collective-permute-done((bf16[2,128,256]{2,1,0:T(8,128)(2,1)S(1)}, bf16[2,128,256]{2,1,0:T(8,128)(2,1)S(1)}, u32[]{:S(2)}, u32[]{:S(2)}) %collective-permute-start) | collective-permute-done | bytes 131104 | tf_op jit(solution)/shard_map/ppermute | solution.py:326
  9.5 1.5 %broadcast_select_fusion = (bf16[16,2,128,128]{3,2,1,0:T(8,128)(2,1)}, bf16[16,2,128,128]{3,2,1,0:T(8,128)(2,1)}) fusion(pred[16]{0:T(512)(128)(4,1)S(1)} %iota_compare_fusion.1, bf16[2,128,128]{2,1,0:T(8,128)(2,1)S(1)} %get-tuple-element.34, bf16[2,128,128]{2,1,0:T(8,128)(2,1)S(1)} %get-tuple-element.32, bf16[2,128,128]{2,1,0:T(8,128)(2,1)S(1)} %get-tuple-element.35, ...), kind=kLoop, calls=%fused_computation.8 | loop fusion | flops 1048576 | bytes 2359312 | tf_op jit(solution)/shard_map/jit(_where)/select_n | solution.py:330
  11.0 0.0 copy-start.4
  11.0 0.0 copy-start.5
  11.0 7.2 %all-to-all-start.1 = ((bf16[16,2,128,128]{3,2,1,0:T(8,128)(2,1)}), bf16[16,2,128,128]{3,2,1,0:T(8,128)(2,1)S(1)}, u32[]{:S(2)}, u32[]{:S(2)}) async-start(bf16[16,2,128,128]{3,2,1,0:T(8,128)(2,1)} %get-tuple-element.38), calls=%async_computation.1 | async-start | bytes 2097152 | tf_op jit(solution)/shard_map/all_to_all | solution.py:331
  18.2 0.0 copy-done.4
  18.2 0.1 compare_and_fusion.1
  18.4 0.0 copy-start.2
  18.4 0.0 collective-permute-done.1
  18.4 0.0 copy-done.5
  18.4 0.1 broadcast_select_fusion.2
  18.5 0.1 broadcast_in_dim.106
  18.6 0.1 reshape.42
  18.7 17.0 %all-to-all-done.1.far_ref = bf16[16,2,128,128]{3,2,1,0:T(8,128)(2,1)S(1)} async-done(((bf16[16,2,128,128]{3,2,1,0:T(8,128)(2,1)}), bf16[16,2,128,128]{3,2,1,0:T(8,128)(2,1)S(1)}, u32[]{:S(2)}, u32[]{:S(2)}) %all-to-all-start.1) | async-done | bytes 1048608 | tf_op jit(solution)/shard_map/all_to_all | solution.py:331
  35.7 0.0 copy-start.3
  35.7 1.0 copy-done.3
  36.7 0.0 copy-start
  36.7 0.0 copy-start.1
  36.7 4.5 %all-to-all-start = ((bf16[16,2,128,128]{3,2,1,0:T(8,128)(2,1)}), bf16[16,2,128,128]{3,2,1,0:T(8,128)(2,1)}, u32[]{:S(2)}, u32[]{:S(2)}) async-start(bf16[16,2,128,128]{3,2,1,0:T(8,128)(2,1)} %get-tuple-element.39), calls=%async_computation | async-start | bytes 2097152 | tf_op jit(solution)/shard_map/all_to_all | solution.py:331
  41.2 0.0 copy-done.2
  41.2 0.0 copy-done
  41.2 0.0 copy-done.1
  41.2 18.5 %attend_0.1 = (bf16[2,128,2048]{2,1,0:T(8,128)(2,1)}, bf16[2,128,2048]{2,1,0:T(8,128)(2,1)}, bf16[16,2,128,128]{3,2,1,0:T(8,128)(2,1)}, f32[2,2,128,128]{3,2,1,0:T(8,128)S(1)}) custom-call(bf16[2,128,2048]{2,1,0:T(8,128)(2,1)S(1)} %copy-done.1, bf16[2,128,2048]{2,1,0:T(8,128)(2,1)S(1)} %copy-done.2, bf16[16,2,128,128]{3,2,1,0:T(8,128)(2,1)} %copy-done.3, ...), custom_call_target="tpu_custom_call" | custom-call | flops 14495514624 | bytes 6291456 | tf_op jit(solution)/shard_map/attend_0/pallas_call | solution.py:244
  59.7 0.0 all-to-all-done.far_ref
  59.7 7.2 %all-to-all-start.2 = ((bf16[16,2,128,128]{3,2,1,0:T(8,128)(2,1)}), bf16[16,2,128,128]{3,2,1,0:T(8,128)(2,1)}, u32[]{:S(2)}, u32[]{:S(2)}) async-start(bf16[16,2,128,128]{3,2,1,0:T(8,128)(2,1)} %get-tuple-element.18), calls=%async_computation.2 | async-start | bytes 2097152 | tf_op jit(solution)/shard_map/all_to_all | solution.py:352
  66.9 18.6 %attend_1.1 = (bf16[2,128,2048]{2,1,0:T(8,128)(2,1)}, bf16[2,128,2048]{2,1,0:T(8,128)(2,1)}, bf16[16,2,128,128]{3,2,1,0:T(8,128)(2,1)}, f32[2,2,128,128]{3,2,1,0:T(8,128)S(1)}) custom-call(bf16[2,128,2048]{2,1,0:T(8,128)(2,1)S(1)} %copy-done.1, bf16[2,128,2048]{2,1,0:T(8,128)(2,1)S(1)} %copy-done.2, ...), custom_call_target="tpu_custom_call", output_to_operand_aliasing={{0}: (8, {}), {1}: (9, {})} | custom-call | flops 14495514624 | bytes 6291456 | tf_op jit(solution)/shard_map/attend_1/pallas_call | solution.py:244
  85.5 0.0 all-to-all-done.2
  85.5 7.2 %all-to-all-start.3 = ((bf16[16,2,128,128]{3,2,1,0:T(8,128)(2,1)}), bf16[16,2,128,128]{3,2,1,0:T(8,128)(2,1)S(1)}, u32[]{:S(2)}, u32[]{:S(2)}) async-start(bf16[16,2,128,128]{3,2,1,0:T(8,128)(2,1)} %get-tuple-element.21), calls=%async_computation.3 | async-start | bytes 2097152 | tf_op jit(solution)/shard_map/all_to_all | solution.py:352
  92.7 14.6 %all-to-all-done.3 = bf16[16,2,128,128]{3,2,1,0:T(8,128)(2,1)S(1)} async-done(((bf16[16,2,128,128]{3,2,1,0:T(8,128)(2,1)}), bf16[16,2,128,128]{3,2,1,0:T(8,128)(2,1)S(1)}, u32[]{:S(2)}, u32[]{:S(2)}) %all-to-all-start.3) | async-done | bytes 1048608 | tf_op jit(solution)/shard_map/all_to_all | solution.py:352
  107.3 2.1 %fusion = (f32[2,128,128]{2,1,0:T(8,128)S(1)}, bf16[2,128,128]{2,1,0:T(8,128)(2,1)S(1)}, bf16[2,128,128]{2,1,0:T(8,128)(2,1)S(1)}, f32[2,128,128]{2,1,0:T(8,128)S(1)}) fusion(bf16[16,2,128,128]{3,2,1,0:T(8,128)(2,1)} %all-to-all-done.2, pred[16]{0:T(512)(128)(4,1)S(1)} %iota_compare_fusion.1, bf16[16,2,128,128]{3,2,1,0:T(8,128)(2,1)S(1)} %all-to-all-done.3), kind=kLoop, calls=%fused_computation.4 | loop fusion | flops 5111808 | bytes 2490384 | tf_op jit(solution)/shard_map/reduce_sum | solution.py:358
  109.5 2.0 %collective-permute-start.2 = (bf16[2,128,256]{2,1,0:T(8,128)(2,1)S(1)}, bf16[2,128,256]{2,1,0:T(8,128)(2,1)S(1)}, u32[]{:S(2)}, u32[]{:S(2)}) collective-permute-start(bf16[2,128,256]{2,1,0:T(8,128)(2,1)S(1)} %pad_maximum_fusion.1), channel_id=1, source_target_pairs={{32,0},{64,32},{96,64},{33,1},{65,33},{97,65},{34,2},{66,34},{98,6... | collective-permute-start | bytes 393224 | tf_op jit(solution)/shard_map/ppermute | solution.py:360
  111.5 4.8 %collective-permute-done.2 = bf16[2,128,256]{2,1,0:T(8,128)(2,1)S(1)} collective-permute-done((bf16[2,128,256]{2,1,0:T(8,128)(2,1)S(1)}, bf16[2,128,256]{2,1,0:T(8,128)(2,1)S(1)}, u32[]{:S(2)}, u32[]{:S(2)}) %collective-permute-start.2) | collective-permute-done | bytes 131104 | tf_op jit(solution)/shard_map/ppermute | solution.py:360
  116.4 0.7 copy.13
  (20 shorter events, 0.3 us)
Async XLA Ops:
  0.6 17.8 %collective-permute-start.1 = (s32[4]{0:T(128)}, s32[4]{0:T(128)S(1)}, u32[]{:S(2)}, u32[]{:S(2)}) collective-permute-start(s32[4]{0:T(128)} %param.9), channel_id=1, source_target_pairs={{0,1},{1,0},{2,3},{3,2},{4,5},{5,4},{6,7},{7,6},{8,9},{9,8},{10,11... | collective-permute-start | bytes 56 | tf_op jit(solution)/shard_map/ppermute | solution.py:333
  1.6 7.8 %collective-permute-start = (bf16[2,128,256]{2,1,0:T(8,128)(2,1)S(1)}, bf16[2,128,256]{2,1,0:T(8,128)(2,1)S(1)}, u32[]{:S(2)}, u32[]{:S(2)}) collective-permute-start(bf16[2,128,256]{2,1,0:T(8,128)(2,1)S(1)} %slice_bitcast_fusion.2), channel_id=1, source_target_pairs={{0,32},{32,64},{64,96},{1,33},{33,65},{65,97},{2,34},{34,66},{66,9... | collective-permute-start | bytes 393224 | tf_op jit(solution)/shard_map/ppermute | solution.py:326
  11.0 7.2 %copy-start.4 = (s32[128]{0:T(128)S(1)}, s32[128]{0:T(128)}, u32[]{:S(2)}) copy-start(s32[128]{0:T(128)} %param.8) | copy-start | bytes 1540
  11.0 7.4 %copy-start.5 = (s32[4]{0:T(128)S(1)}, s32[4]{0:T(128)}, u32[]{:S(2)}) copy-start(s32[4]{0:T(128)} %param.9) | copy-start | bytes 52
  11.0 24.7 %all-to-all-start.1 = ((bf16[16,2,128,128]{3,2,1,0:T(8,128)(2,1)}), bf16[16,2,128,128]{3,2,1,0:T(8,128)(2,1)S(1)}, u32[]{:S(2)}, u32[]{:S(2)}) async-start(bf16[16,2,128,128]{3,2,1,0:T(8,128)(2,1)} %get-tuple-element.38), calls=%async_computation.1 | async-start | bytes 2097152 | tf_op jit(solution)/shard_map/all_to_all | solution.py:331
  18.4 22.8 %copy-start.2 = (bf16[2,128,2048]{2,1,0:T(8,128)(2,1)S(1)}, bf16[2,128,2048]{2,1,0:T(8,128)(2,1)}, u32[]{:S(2)}) copy-start(bf16[2,128,2048]{2,1,0:T(8,128)(2,1)} %do_ref.3) | copy-start | bytes 3145732
  35.7 1.0 copy-start.3
  36.7 4.5 %copy-start = (bf16[2,2,128,256]{3,2,1,0:T(8,128)(2,1)S(1)}, bf16[2,2,128,256]{3,2,1,0:T(8,128)(2,1)}, u32[]{:S(2)}) copy-start(bf16[2,2,128,256]{3,2,1,0:T(8,128)(2,1)} %own_ref.3) | copy-start | bytes 786436
  36.7 4.5 %copy-start.1 = (bf16[2,128,2048]{2,1,0:T(8,128)(2,1)S(1)}, bf16[2,128,2048]{2,1,0:T(8,128)(2,1)}, u32[]{:S(2)}) copy-start(bf16[2,128,2048]{2,1,0:T(8,128)(2,1)} %q_ref.3) | copy-start | bytes 3145732
  36.7 23.0 %all-to-all-start = ((bf16[16,2,128,128]{3,2,1,0:T(8,128)(2,1)}), bf16[16,2,128,128]{3,2,1,0:T(8,128)(2,1)}, u32[]{:S(2)}, u32[]{:S(2)}) async-start(bf16[16,2,128,128]{3,2,1,0:T(8,128)(2,1)} %get-tuple-element.39), calls=%async_computation | async-start | bytes 2097152 | tf_op jit(solution)/shard_map/all_to_all | solution.py:331
  59.7 25.8 %all-to-all-start.2 = ((bf16[16,2,128,128]{3,2,1,0:T(8,128)(2,1)}), bf16[16,2,128,128]{3,2,1,0:T(8,128)(2,1)}, u32[]{:S(2)}, u32[]{:S(2)}) async-start(bf16[16,2,128,128]{3,2,1,0:T(8,128)(2,1)} %get-tuple-element.18), calls=%async_computation.2 | async-start | bytes 2097152 | tf_op jit(solution)/shard_map/all_to_all | solution.py:352
  85.5 21.8 %all-to-all-start.3 = ((bf16[16,2,128,128]{3,2,1,0:T(8,128)(2,1)}), bf16[16,2,128,128]{3,2,1,0:T(8,128)(2,1)S(1)}, u32[]{:S(2)}, u32[]{:S(2)}) async-start(bf16[16,2,128,128]{3,2,1,0:T(8,128)(2,1)} %get-tuple-element.21), calls=%async_computation.3 | async-start | bytes 2097152 | tf_op jit(solution)/shard_map/all_to_all | solution.py:352
  109.5 6.9 %collective-permute-start.2 = (bf16[2,128,256]{2,1,0:T(8,128)(2,1)S(1)}, bf16[2,128,256]{2,1,0:T(8,128)(2,1)S(1)}, u32[]{:S(2)}, u32[]{:S(2)}) collective-permute-start(bf16[2,128,256]{2,1,0:T(8,128)(2,1)S(1)} %pad_maximum_fusion.1), channel_id=1, source_target_pairs={{32,0},{64,32},{96,64},{33,1},{65,33},{97,65},{34,2},{66,34},{98,6... | collective-permute-start | bytes 393224 | tf_op jit(solution)/shard_map/ppermute | solution.py:360

commit v4 on v3

--- a/solution.py
+++ b/solution.py
@@ -41,6 +41,7 @@
     far_ref,
     own_ref,
     base_ref,
+    which_ref,
     starts_ref,
     near_ref,
     keep_ref,
@@ -59,8 +60,14 @@
         return held[pl.ds(at.start // rows, per)].reshape(TILE, HEAD_SIZE)
 
     def fetch_keys(i, held):
-        return [
-            pltpu.make_async_copy(far_ref.at[:, i], held.at[pl.ds(0, REACH)], arrive_far.at[i]),
+        if len(far_ref.shape) == 4:
+            far = [(far_ref.at[:, i], held.at[pl.ds(0, REACH)], arrive_far.at[i, 0])]
+        else:
+            far = [
+                (far_ref.at[slot, which_ref[slot], i], held.at[slot], arrive_far.at[i, slot])
+                for slot in range(REACH)
+            ]
+        return [pltpu.make_async_copy(*one) for one in far] + [
             pltpu.make_async_copy(
                 own_ref.at[i, :, :, own_columns], held.at[pl.ds(REACH, 2)], arrive_own.at[i]
             ),
@@ -232,7 +239,7 @@
         send(dq_all, dq_ref, head, 1).wait()
 
 
-def attend(group, queries, d_out, far, keys_values, base, starts, near, keep, earlier):
+def attend(group, queries, d_out, far, keys_values, base, which, starts, near, keep, earlier):
     rows = queries.shape[1]
     keys = (REACH + 2) * rows
     whole = lambda shape: pl.BlockSpec(shape, lambda step: (0,) * len(shape))
@@ -249,6 +256,7 @@
             hbm,
             hbm,
             hbm,
+            pl.BlockSpec(memory_space=pltpu.SMEM),
             pl.BlockSpec(memory_space=pltpu.SMEM),
             whole((1, 2 * rows)),
             whole((2 * rows, 2 * rows)),
@@ -283,17 +291,17 @@
             pltpu.VMEM(local_shape, jnp.float32),
             pltpu.SemaphoreType.DMA((GROUP, 2)),
             pltpu.SemaphoreType.DMA((GROUP, 2)),
-            pltpu.SemaphoreType.DMA((2,)),
+            pltpu.SemaphoreType.DMA((2, REACH)),
             pltpu.SemaphoreType.DMA((2,)),
             pltpu.SemaphoreType.DMA((keys // TILE,)),
         ],
-        input_output_aliases={8 + i: i for i in range(len(earlier))},
+        input_output_aliases={9 + i: i for i in range(len(earlier))},
         compiler_params=pltpu.CompilerParams(vmem_limit_bytes=VMEM_LIMIT),
         cost_estimate=pl.CostEstimate(
             flops=2 * flops, bytes_accessed=6 * 2**20, transcendentals=keys * 2 * rows * GROUP
         ),
         name=f"attend_{group}",
-    )(queries, d_out, far, keys_values, base, starts, near, keep, *earlier)
+    )(queries, d_out, far, keys_values, base, which, starts, near, keep, *earlier)
 
 
 def masks(doc_start, slab, place, places):
@@ -301,7 +309,8 @@
     offset = jnp.arange(rows, dtype=jnp.int32)
     starts = jnp.concatenate([doc_start, doc_start])[None, :]
     slot = jnp.arange(REACH, dtype=jnp.int32)
-    base = rows * (places * slab + slot - jnp.where(slot >= place, places, 0))
+    which = (slot >= place).astype(jnp.int32)
+    base = rows * (places * (slab - which) + slot)
     same = doc_start[:, None] == starts
     k_blk = (offset // BLOCK)[:, None]
     q_blk = jnp.concatenate([offset // BLOCK] * 2)[None, :]
@@ -309,7 +318,7 @@
     own_clean = same & (k_blk + noisy.astype(jnp.int32) <= q_blk)
     own_noisy = same & noisy & (k_blk == q_blk)
     near = jnp.where(jnp.concatenate([own_clean, own_noisy], 0), 0.0, NEGATIVE)
-    return base, starts, near.astype(jnp.float32)
+    return base, which, starts, near.astype(jnp.float32)
 
 
 def local(queries, keys_values, d_out, doc_start, block_bits):
@@ -327,8 +336,12 @@
     far = []
     for group in range(kv_heads):
         part = slice(group * HEAD_SIZE, (group + 1) * HEAD_SIZE)
-        send = jnp.where(after, own[None, :, :, part], before[None, :, :, part])
-        far.append(lax.all_to_all(send, "place", 0, 0))
+        if group == 0:
+            send = jnp.where(after, own[None, :, :, part], before[None, :, :, part])
+            far.append(lax.all_to_all(send, "place", 0, 0))
+        else:
+            send = jnp.stack([own[:, :, part], before[:, :, part]])
+            far.append(lax.all_gather(send, "place"))
 
     other = lax.ppermute(block_bits, "head", [(0, 1), (1, 0)])
     bits = jnp.where(
@@ -338,13 +351,13 @@
     )
     keep = jnp.concatenate([jnp.ones((rows,), jnp.int32), jnp.repeat(bits, BLOCK)])
     keep = keep.astype(jnp.float32)[None, :]
-    base, starts, near = masks(doc_start, slab, place, places)
+    base, which, starts, near = masks(doc_start, slab, place, places)
 
     earlier = ()
     totals, noisy = [], []
     for group in range(kv_heads):
         att, dq, back, mine = attend(
-            group, queries, d_out, far[group], keys_values, base, starts, near, keep, earlier
+            group, queries, d_out, far[group], keys_values, base, which, starts, near, keep, earlier
         )
         earlier = (att, dq)
         if totals:

time: 118 us -> 127 us (1.076)
  between operations: 0.92 us -> 14.3 us
  starting transfers between devices: 31.6 us -> 23.3 us
  waiting for transfers between devices: 40.6 us -> 44.9 us
    all_to_all x2 -> x1, starting transfers between devices: 11.6 us -> 7.09 us  [local(): far.append(lax.all_to_all(send, 'place', 0, 0))]
    all_to_all x2, starting transfers between devices: 14.4 us -> 10.5 us  [local(): terms = lax.all_to_all(back, 'place', 0, 0)]
    all_to_all x2 -> x1, waiting for transfers between devices: 17 us -> 19.2 us  [local(): far.append(lax.all_to_all(send, 'place', 0, 0))]
    all_to_all x2, waiting for transfers between devices: 14.6 us -> 16.3 us  [local(): terms = lax.all_to_all(back, 'place', 0, 0)]
  transfers between devices with their start and end apart: 7 -> 7, of which waited for: 4 -> 5; matrix products, arithmetic and copies ran while one was open for 3% -> 1% of each run, Pallas kernels for 32% -> 30%
where the time goes in v4:
time: 127 us; the launch traced here: 126 us
  waiting for transfers between devices  44.9 us (35%)
  Pallas kernels  37.6 us (30%)
  starting transfers between devices  23.3 us (18%)
  between operations  14.3 us (11%)
  other arithmetic  4.23 us (3%)
  local copies, waits for them, and re-layouts  1.93 us (2%)
    pallas_call x2, Pallas kernels, attend(): pl.pallas_call(functools.partial(kernel, rows, group), grid=(1,), in_spec...  37.6 us
    all_to_all x1, waiting for transfers between devices, local(): far.append(lax.all_to_all(send, 'place', 0, 0))  19.2 us
    all_to_all x2, waiting for transfers between devices, local(): terms = lax.all_to_all(back, 'place', 0, 0)  16.3 us
    all_to_all x2, starting transfers between devices, local(): terms = lax.all_to_all(back, 'place', 0, 0)  10.5 us
    all_to_all x1, starting transfers between devices, local(): far.append(lax.all_to_all(send, 'place', 0, 0))  7.09 us
    ppermute x1, waiting for transfers between devices, local(): arrived = lax.ppermute(jnp.concatenate(there, -1), 'slab', sooner)  4.83 us
    ppermute x1, waiting for transfers between devices, local(): before = lax.ppermute(own, 'slab', later)  3.56 us
    ppermute x1, starting transfers between devices, local(): before = lax.ppermute(own, 'slab', later)  3.53 us
  transfers between devices with their start and end apart: 7, of which 5 were waited for; matrix products, arithmetic and copies ran while one was open for 1% of the time, Pallas kernels for 30%

profile of v4, /device:TPU:64, one launch (start us, length us, event | category | flops | bytes accessed | tf_op | source)
XLA Modules:
  0.0 126.2 jit_solution(9297292033924369875)
XLA Ops:
  7.2 0.0 all-gather.3.cloned.1.call-start
  7.2 0.9 slice_bitcast_fusion.2
  8.1 0.0 copy-start.3
  8.1 3.5 %collective-permute-start = (bf16[2,128,256]{2,1,0:T(8,128)(2,1)S(1)}, bf16[2,128,256]{2,1,0:T(8,128)(2,1)S(1)}, u32[]{:S(2)}, u32[]{:S(2)}) collective-permute-start(bf16[2,128,256]{2,1,0:T(8,128)(2,1)S(1)} %slice_bitcast_fusion.2), channel_id=1, source_target_pairs={{0,32},{32,64},{64,96},{1,33},{33,65},{65,97},{2,34},{34,66},{66,9... | collective-permute-start | bytes 393224 | tf_op jit(solution)/shard_map/ppermute | solution.py:335
  11.7 3.6 %collective-permute-done = bf16[2,128,256]{2,1,0:T(8,128)(2,1)S(1)} collective-permute-done((bf16[2,128,256]{2,1,0:T(8,128)(2,1)S(1)}, bf16[2,128,256]{2,1,0:T(8,128)(2,1)S(1)}, u32[]{:S(2)}, u32[]{:S(2)}) %collective-permute-start) | collective-permute-done | bytes 131104 | tf_op jit(solution)/shard_map/ppermute | solution.py:335
  15.3 0.0 copy-start.4
  15.3 0.0 copy-start
  15.3 0.0 copy-start.1
  15.3 0.0 copy-start.2
  15.3 0.7 pad_maximum_fusion.1
  16.0 0.0 all-gather.3.cloned.1.call-update
  16.0 0.1 collective-permute-start.1
  16.2 1.1 broadcast_select_fusion
  17.3 7.1 %all-to-all-start = ((bf16[16,2,128,128]{3,2,1,0:T(8,128)(2,1)}), bf16[16,2,128,128]{3,2,1,0:T(8,128)(2,1)}, u32[]{:S(2)}, u32[]{:S(2)}) async-start(bf16[16,2,128,128]{3,2,1,0:T(8,128)(2,1)} %broadcast_select_fusion), calls=%async_computation | async-start | bytes 2097152 | tf_op jit(solution)/shard_map/all_to_all | solution.py:341
  24.4 0.0 copy-done.3
  24.5 0.1 compare_and_fusion.1
  24.7 0.0 collective-permute-done.1
  24.7 0.0 copy-done.4
  24.7 0.1 broadcast_select_fusion.1
  24.8 0.1 broadcast_in_dim.78
  24.8 0.1 reshape.40
  24.9 19.2 %all-to-all-done.far_ref = bf16[16,2,128,128]{3,2,1,0:T(8,128)(2,1)} async-done(((bf16[16,2,128,128]{3,2,1,0:T(8,128)(2,1)}), bf16[16,2,128,128]{3,2,1,0:T(8,128)(2,1)}, u32[]{:S(2)}, u32[]{:S(2)}) %all-to-all-start) | async-done | bytes 1048608 | tf_op jit(solution)/shard_map/all_to_all | solution.py:341
  44.1 0.0 copy-done
  44.1 0.0 copy-done.1
  44.1 0.0 copy-done.2
  44.1 18.8 %attend_0.1 = (bf16[2,128,2048]{2,1,0:T(8,128)(2,1)}, bf16[2,128,2048]{2,1,0:T(8,128)(2,1)}, bf16[16,2,128,128]{3,2,1,0:T(8,128)(2,1)}, f32[2,2,128,128]{3,2,1,0:T(8,128)S(1)}) custom-call(bf16[2,128,2048]{2,1,0:T(8,128)(2,1)S(1)} %copy-done.1, bf16[2,128,2048]{2,1,0:T(8,128)(2,1)S(1)} %copy-done.2, bf16[16,2,128,128]{3,2,1,0:T(8,128)(2,1)} %all-to-all-done.far_ref, ...), custom_call_target="tpu_custom_call" | custom-call | flops 14495514624 | bytes 6291456 | tf_op jit(solution)/shard_map/attend_0/pallas_call | solution.py:251
  62.9 4.4 %all-to-all-start.1 = ((bf16[16,2,128,128]{3,2,1,0:T(8,128)(2,1)}), bf16[16,2,128,128]{3,2,1,0:T(8,128)(2,1)}, u32[]{:S(2)}, u32[]{:S(2)}) async-start(bf16[16,2,128,128]{3,2,1,0:T(8,128)(2,1)} %get-tuple-element.18), calls=%async_computation.1 | async-start | bytes 2097152 | tf_op jit(solution)/shard_map/all_to_all | solution.py:365
  67.3 1.0 all-gather.3.cloned.1.call-done
  68.2 18.8 %attend_1.1 = (bf16[2,128,2048]{2,1,0:T(8,128)(2,1)}, bf16[2,128,2048]{2,1,0:T(8,128)(2,1)}, bf16[16,2,128,128]{3,2,1,0:T(8,128)(2,1)}, f32[2,2,128,128]{3,2,1,0:T(8,128)S(1)}) custom-call(bf16[2,128,2048]{2,1,0:T(8,128)(2,1)S(1)} %copy-done.1, bf16[2,128,2048]{2,1,0:T(8,128)(2,1)S(1)} %copy-done.2, ...), custom_call_target="tpu_custom_call", output_to_operand_aliasing={{0}: (9, {}), {1}: (10, {})} | custom-call | flops 14495514624 | bytes 6291456 | tf_op jit(solution)/shard_map/attend_1/pallas_call | solution.py:251
  87.1 0.0 all-to-all-done.1
  87.1 6.2 %all-to-all-start.2 = ((bf16[16,2,128,128]{3,2,1,0:T(8,128)(2,1)}), bf16[16,2,128,128]{3,2,1,0:T(8,128)(2,1)S(1)}, u32[]{:S(2)}, u32[]{:S(2)}) async-start(bf16[16,2,128,128]{3,2,1,0:T(8,128)(2,1)} %get-tuple-element.21), calls=%async_computation.2 | async-start | bytes 2097152 | tf_op jit(solution)/shard_map/all_to_all | solution.py:365
  93.3 16.3 %all-to-all-done.2 = bf16[16,2,128,128]{3,2,1,0:T(8,128)(2,1)S(1)} async-done(((bf16[16,2,128,128]{3,2,1,0:T(8,128)(2,1)}), bf16[16,2,128,128]{3,2,1,0:T(8,128)(2,1)S(1)}, u32[]{:S(2)}, u32[]{:S(2)}) %all-to-all-start.2) | async-done | bytes 1048608 | tf_op jit(solution)/shard_map/all_to_all | solution.py:365
  109.6 2.0 %fusion = (f32[2,128,128]{2,1,0:T(8,128)S(1)}, bf16[2,128,128]{2,1,0:T(8,128)(2,1)S(1)}, bf16[2,128,128]{2,1,0:T(8,128)(2,1)S(1)}, f32[2,128,128]{2,1,0:T(8,128)S(1)}) fusion(bf16[16,2,128,128]{3,2,1,0:T(8,128)(2,1)} %all-to-all-done.1, pred[16]{0:T(512)(128)(4,1)S(1)} %iota_compare_fusion.1, bf16[16,2,128,128]{3,2,1,0:T(8,128)(2,1)S(1)} %all-to-all-done.2), kind=kLoop, calls=%fused_computation.4 | loop fusion | flops 5111808 | bytes 2490384 | tf_op jit(solution)/shard_map/reduce_sum | solution.py:371
  111.7 2.0 %collective-permute-start.2 = (bf16[2,128,256]{2,1,0:T(8,128)(2,1)S(1)}, bf16[2,128,256]{2,1,0:T(8,128)(2,1)S(1)}, u32[]{:S(2)}, u32[]{:S(2)}) collective-permute-start(bf16[2,128,256]{2,1,0:T(8,128)(2,1)S(1)} %pad_maximum_fusion.2), channel_id=1, source_target_pairs={{32,0},{64,32},{96,64},{33,1},{65,33},{97,65},{34,2},{66,34},{98,6... | collective-permute-start | bytes 393224 | tf_op jit(solution)/shard_map/ppermute | solution.py:373
  113.7 4.8 %collective-permute-done.2 = bf16[2,128,256]{2,1,0:T(8,128)(2,1)S(1)} collective-permute-done((bf16[2,128,256]{2,1,0:T(8,128)(2,1)S(1)}, bf16[2,128,256]{2,1,0:T(8,128)(2,1)S(1)}, u32[]{:S(2)}, u32[]{:S(2)}) %collective-permute-start.2) | collective-permute-done | bytes 131104 | tf_op jit(solution)/shard_map/ppermute | solution.py:373
  118.6 0.7 copy.18
  (21 shorter events, 0.3 us)
Async XLA Ops:
  7.2 61.1 %all-gather.3.cloned.1.call-start = ((), (), s32[]{:S(2)}) async-start(), calls=%async_computation.3 | async-start | bytes 2228224 | tf_op jit(solution)/shard_map/all_gather | solution.py:344
  8.1 16.3 %copy-start.3 = (s32[128]{0:T(128)S(1)}, s32[128]{0:T(128)}, u32[]{:S(2)}) copy-start(s32[128]{0:T(128)} %param.8) | copy-start | bytes 1540
  8.1 7.1 %collective-permute-start = (bf16[2,128,256]{2,1,0:T(8,128)(2,1)S(1)}, bf16[2,128,256]{2,1,0:T(8,128)(2,1)S(1)}, u32[]{:S(2)}, u32[]{:S(2)}) collective-permute-start(bf16[2,128,256]{2,1,0:T(8,128)(2,1)S(1)} %slice_bitcast_fusion.2), channel_id=1, source_target_pairs={{0,32},{32,64},{64,96},{1,33},{33,65},{65,97},{2,34},{34,66},{66,9... | collective-permute-start | bytes 393224 | tf_op jit(solution)/shard_map/ppermute | solution.py:335
  15.3 9.4 %copy-start.4 = (s32[4]{0:T(128)S(1)}, s32[4]{0:T(128)}, u32[]{:S(2)}) copy-start(s32[4]{0:T(128)} %param.9) | copy-start | bytes 52
  15.3 28.8 %copy-start = (bf16[2,2,128,256]{3,2,1,0:T(8,128)(2,1)S(1)}, bf16[2,2,128,256]{3,2,1,0:T(8,128)(2,1)}, u32[]{:S(2)}) copy-start(bf16[2,2,128,256]{3,2,1,0:T(8,128)(2,1)} %own_ref.3) | copy-start | bytes 786436
  15.3 28.8 %copy-start.1 = (bf16[2,128,2048]{2,1,0:T(8,128)(2,1)S(1)}, bf16[2,128,2048]{2,1,0:T(8,128)(2,1)}, u32[]{:S(2)}) copy-start(bf16[2,128,2048]{2,1,0:T(8,128)(2,1)} %q_ref.3) | copy-start | bytes 3145732
  15.3 28.8 %copy-start.2 = (bf16[2,128,2048]{2,1,0:T(8,128)(2,1)S(1)}, bf16[2,128,2048]{2,1,0:T(8,128)(2,1)}, u32[]{:S(2)}) copy-start(bf16[2,128,2048]{2,1,0:T(8,128)(2,1)} %do_ref.3) | copy-start | bytes 3145732
  16.0 8.6 %collective-permute-start.1 = (s32[4]{0:T(128)}, s32[4]{0:T(128)S(1)}, u32[]{:S(2)}, u32[]{:S(2)}) collective-permute-start(s32[4]{0:T(128)} %param.9), channel_id=1, source_target_pairs={{0,1},{1,0},{2,3},{3,2},{4,5},{5,4},{6,7},{7,6},{8,9},{9,8},{10,11... | collective-permute-start | bytes 56 | tf_op jit(solution)/shard_map/ppermute | solution.py:346
  17.3 26.8 %all-to-all-start = ((bf16[16,2,128,128]{3,2,1,0:T(8,128)(2,1)}), bf16[16,2,128,128]{3,2,1,0:T(8,128)(2,1)}, u32[]{:S(2)}, u32[]{:S(2)}) async-start(bf16[16,2,128,128]{3,2,1,0:T(8,128)(2,1)} %broadcast_select_fusion), calls=%async_computation | async-start | bytes 2097152 | tf_op jit(solution)/shard_map/all_to_all | solution.py:341
  62.9 24.1 %all-to-all-start.1 = ((bf16[16,2,128,128]{3,2,1,0:T(8,128)(2,1)}), bf16[16,2,128,128]{3,2,1,0:T(8,128)(2,1)}, u32[]{:S(2)}, u32[]{:S(2)}) async-start(bf16[16,2,128,128]{3,2,1,0:T(8,128)(2,1)} %get-tuple-element.18), calls=%async_computation.1 | async-start | bytes 2097152 | tf_op jit(solution)/shard_map/all_to_all | solution.py:365
  87.1 22.5 %all-to-all-start.2 = ((bf16[16,2,128,128]{3,2,1,0:T(8,128)(2,1)}), bf16[16,2,128,128]{3,2,1,0:T(8,128)(2,1)S(1)}, u32[]{:S(2)}, u32[]{:S(2)}) async-start(bf16[16,2,128,128]{3,2,1,0:T(8,128)(2,1)} %get-tuple-element.21), calls=%async_computation.2 | async-start | bytes 2097152 | tf_op jit(solution)/shard_map/all_to_all | solution.py:365
  111.7 6.9 %collective-permute-start.2 = (bf16[2,128,256]{2,1,0:T(8,128)(2,1)S(1)}, bf16[2,128,256]{2,1,0:T(8,128)(2,1)S(1)}, u32[]{:S(2)}, u32[]{:S(2)}) collective-permute-start(bf16[2,128,256]{2,1,0:T(8,128)(2,1)S(1)} %pad_maximum_fusion.2), channel_id=1, source_target_pairs={{32,0},{64,32},{96,64},{33,1},{65,33},{97,65},{34,2},{66,34},{98,6... | collective-permute-start | bytes 393224 | tf_op jit(solution)/shard_map/ppermute | solution.py:373
Sparse Core Ops, SparseCore 0:
  16.2 52.0 all-gather.2

commit v5 on v3

--- a/solution.py
+++ b/solution.py
@@ -355,8 +355,14 @@
     here, there = [], []
     for terms in totals:
         terms = terms.astype(jnp.float32)
-        here.append(jnp.sum(jnp.where(after, terms, 0.0), 0))
-        there.append(jnp.sum(jnp.where(after, 0.0, terms), 0).astype(jnp.bfloat16))
+        sums = (
+            jnp.sum(jnp.where(after, terms, 0.0), 0),
+            jnp.sum(jnp.where(after, 0.0, terms), 0).astype(jnp.bfloat16),
+        )
+        if len(here) < kv_heads - 1:
+            sums = lax.optimization_barrier(sums)
+        here.append(sums[0])
+        there.append(sums[1])
     arrived = lax.ppermute(jnp.concatenate(there, -1), "slab", sooner)
     clean = jnp.concatenate([a + b[:, 0] for a, b in zip(here, noisy)], -1)
     clean = clean + arrived.astype(jnp.float32)

time: 118 us -> 118 us (level)
  no operation moved by 1% of the time
where the time goes in v5:
time: 118 us; the launch traced here: 117 us
  waiting for transfers between devices  40.6 us (34%)
  Pallas kernels  37.1 us (31%)
  starting transfers between devices  31.6 us (27%)
  other arithmetic  4.07 us (3%)
  local copies, waits for them, and re-layouts  2.92 us (2%)
    pallas_call x2, Pallas kernels, attend(): pl.pallas_call(functools.partial(kernel, rows, group), grid=(1,), in_spec...  37.1 us
    all_to_all x2, waiting for transfers between devices, local(): far.append(lax.all_to_all(send, 'place', 0, 0))  17 us
    all_to_all x2, waiting for transfers between devices, local(): terms = lax.all_to_all(back, 'place', 0, 0)  14.6 us
    all_to_all x2, starting transfers between devices, local(): terms = lax.all_to_all(back, 'place', 0, 0)  14.4 us
    all_to_all x2, starting transfers between devices, local(): far.append(lax.all_to_all(send, 'place', 0, 0))  11.6 us
    ppermute x1, waiting for transfers between devices, local(): arrived = lax.ppermute(jnp.concatenate(there, -1), 'slab', sooner)  4.83 us
    ppermute x1, waiting for transfers between devices, local(): before = lax.ppermute(own, 'slab', later)  4.15 us
    ppermute x1, starting transfers between devices, local(): before = lax.ppermute(own, 'slab', later)  3.53 us
  transfers between devices with their start and end apart: 7, of which 4 were waited for; matrix products, arithmetic and copies ran while one was open for 3% of the time, Pallas kernels for 32%

profile of v5, /device:TPU:64, one launch (start us, length us, event | category | flops | bytes accessed | tf_op | source)
XLA Modules:
  0.0 117.2 jit_solution(8465322854007232023)
XLA Ops:
  0.6 0.1 collective-permute-start.1
  0.7 0.9 slice_bitcast_fusion.2
  1.6 3.5 %collective-permute-start = (bf16[2,128,256]{2,1,0:T(8,128)(2,1)S(1)}, bf16[2,128,256]{2,1,0:T(8,128)(2,1)S(1)}, u32[]{:S(2)}, u32[]{:S(2)}) collective-permute-start(bf16[2,128,256]{2,1,0:T(8,128)(2,1)S(1)} %slice_bitcast_fusion.2), channel_id=1, source_target_pairs={{0,32},{32,64},{64,96},{1,33},{33,65},{65,97},{2,34},{34,66},{66,9... | collective-permute-start | bytes 393224 | tf_op jit(solution)/shard_map/ppermute | solution.py:326
  5.3 4.2 %collective-permute-done = bf16[2,128,256]{2,1,0:T(8,128)(2,1)S(1)} collective-permute-done((bf16[2,128,256]{2,1,0:T(8,128)(2,1)S(1)}, bf16[2,128,256]{2,1,0:T(8,128)(2,1)S(1)}, u32[]{:S(2)}, u32[]{:S(2)}) %collective-permute-start) | collective-permute-done | bytes 131104 | tf_op jit(solution)/shard_map/ppermute | solution.py:326
  9.5 1.5 %broadcast_select_fusion = (bf16[16,2,128,128]{3,2,1,0:T(8,128)(2,1)}, bf16[16,2,128,128]{3,2,1,0:T(8,128)(2,1)}) fusion(pred[16]{0:T(512)(128)(4,1)S(1)} %iota_compare_fusion.1, bf16[2,128,128]{2,1,0:T(8,128)(2,1)S(1)} %get-tuple-element.38, bf16[2,128,128]{2,1,0:T(8,128)(2,1)S(1)} %get-tuple-element.36, bf16[2,128,128]{2,1,0:T(8,128)(2,1)S(1)} %get-tuple-element.39, ...), kind=kLoop, calls=%fused_computation.8 | loop fusion | flops 1048576 | bytes 2359312 | tf_op jit(solution)/shard_map/jit(_where)/select_n | solution.py:330
  11.0 0.0 copy-start.4
  11.0 0.0 copy-start.5
  11.0 7.2 %all-to-all-start.1 = ((bf16[16,2,128,128]{3,2,1,0:T(8,128)(2,1)}), bf16[16,2,128,128]{3,2,1,0:T(8,128)(2,1)S(1)}, u32[]{:S(2)}, u32[]{:S(2)}) async-start(bf16[16,2,128,128]{3,2,1,0:T(8,128)(2,1)} %get-tuple-element.42), calls=%async_computation.1 | async-start | bytes 2097152 | tf_op jit(solution)/shard_map/all_to_all | solution.py:331
  18.2 0.0 copy-done.4
  18.2 0.1 compare_and_fusion.1
  18.4 0.0 copy-start.2
  18.4 0.0 collective-permute-done.1
  18.4 0.0 copy-done.5
  18.4 0.1 broadcast_select_fusion.2
  18.5 0.1 broadcast_in_dim.106
  18.6 0.1 reshape.42
  18.7 17.0 %all-to-all-done.1.far_ref = bf16[16,2,128,128]{3,2,1,0:T(8,128)(2,1)S(1)} async-done(((bf16[16,2,128,128]{3,2,1,0:T(8,128)(2,1)}), bf16[16,2,128,128]{3,2,1,0:T(8,128)(2,1)S(1)}, u32[]{:S(2)}, u32[]{:S(2)}) %all-to-all-start.1) | async-done | bytes 1048608 | tf_op jit(solution)/shard_map/all_to_all | solution.py:331
  35.7 0.0 copy-start.3
  35.7 1.0 copy-done.3
  36.7 0.0 copy-start
  36.7 0.0 copy-start.1
  36.7 4.5 %all-to-all-start = ((bf16[16,2,128,128]{3,2,1,0:T(8,128)(2,1)}), bf16[16,2,128,128]{3,2,1,0:T(8,128)(2,1)}, u32[]{:S(2)}, u32[]{:S(2)}) async-start(bf16[16,2,128,128]{3,2,1,0:T(8,128)(2,1)} %get-tuple-element.43), calls=%async_computation | async-start | bytes 2097152 | tf_op jit(solution)/shard_map/all_to_all | solution.py:331
  41.2 0.0 copy-done.2
  41.2 0.0 copy-done
  41.2 0.0 copy-done.1
  41.2 18.5 %attend_0.1 = (bf16[2,128,2048]{2,1,0:T(8,128)(2,1)}, bf16[2,128,2048]{2,1,0:T(8,128)(2,1)}, bf16[16,2,128,128]{3,2,1,0:T(8,128)(2,1)}, f32[2,2,128,128]{3,2,1,0:T(8,128)S(1)}) custom-call(bf16[2,128,2048]{2,1,0:T(8,128)(2,1)S(1)} %copy-done.1, bf16[2,128,2048]{2,1,0:T(8,128)(2,1)S(1)} %copy-done.2, bf16[16,2,128,128]{3,2,1,0:T(8,128)(2,1)} %copy-done.3, ...), custom_call_target="tpu_custom_call" | custom-call | flops 14495514624 | bytes 6291456 | tf_op jit(solution)/shard_map/attend_0/pallas_call | solution.py:244
  59.7 0.0 all-to-all-done.far_ref
  59.7 7.2 %all-to-all-start.2 = ((bf16[16,2,128,128]{3,2,1,0:T(8,128)(2,1)}), bf16[16,2,128,128]{3,2,1,0:T(8,128)(2,1)}, u32[]{:S(2)}, u32[]{:S(2)}) async-start(bf16[16,2,128,128]{3,2,1,0:T(8,128)(2,1)} %get-tuple-element.20), calls=%async_computation.2 | async-start | bytes 2097152 | tf_op jit(solution)/shard_map/all_to_all | solution.py:352
  66.9 18.6 %attend_1.1 = (bf16[2,128,2048]{2,1,0:T(8,128)(2,1)}, bf16[2,128,2048]{2,1,0:T(8,128)(2,1)}, bf16[16,2,128,128]{3,2,1,0:T(8,128)(2,1)}, f32[2,2,128,128]{3,2,1,0:T(8,128)S(1)}) custom-call(bf16[2,128,2048]{2,1,0:T(8,128)(2,1)S(1)} %copy-done.1, bf16[2,128,2048]{2,1,0:T(8,128)(2,1)S(1)} %copy-done.2, ...), custom_call_target="tpu_custom_call", output_to_operand_aliasing={{0}: (8, {}), {1}: (9, {})} | custom-call | flops 14495514624 | bytes 6291456 | tf_op jit(solution)/shard_map/attend_1/pallas_call | solution.py:244
  85.5 0.0 all-to-all-done.2
  85.5 7.2 %all-to-all-start.3 = ((bf16[16,2,128,128]{3,2,1,0:T(8,128)(2,1)}), bf16[16,2,128,128]{3,2,1,0:T(8,128)(2,1)S(1)}, u32[]{:S(2)}, u32[]{:S(2)}) async-start(bf16[16,2,128,128]{3,2,1,0:T(8,128)(2,1)} %get-tuple-element.24), calls=%async_computation.3 | async-start | bytes 2097152 | tf_op jit(solution)/shard_map/all_to_all | solution.py:352
  92.7 14.6 %all-to-all-done.3 = bf16[16,2,128,128]{3,2,1,0:T(8,128)(2,1)S(1)} async-done(((bf16[16,2,128,128]{3,2,1,0:T(8,128)(2,1)}), bf16[16,2,128,128]{3,2,1,0:T(8,128)(2,1)S(1)}, u32[]{:S(2)}, u32[]{:S(2)}) %all-to-all-start.3) | async-done | bytes 1048608 | tf_op jit(solution)/shard_map/all_to_all | solution.py:352
  107.3 2.1 %fusion.2 = (f32[2,128,128]{2,1,0:T(8,128)S(1)}, bf16[2,128,128]{2,1,0:T(8,128)(2,1)S(1)}, f32[2,128,128]{2,1,0:T(8,128)S(1)}, bf16[2,128,128]{2,1,0:T(8,128)(2,1)S(1)}) fusion(bf16[16,2,128,128]{3,2,1,0:T(8,128)(2,1)S(1)} %all-to-all-done.3, pred[16]{0:T(512)(128)(4,1)S(1)} %iota_compare_fusion.1, bf16[16,2,128,128]{3,2,1,0:T(8,128)(2,1)} %all-to-all-done.2), kind=kLoop, calls=%fused_computation.6 | loop fusion | flops 5111808 | bytes 2490384 | tf_op jit(solution)/shard_map/reduce_sum | solution.py:359
  109.5 2.0 %collective-permute-start.2 = (bf16[2,128,256]{2,1,0:T(8,128)(2,1)S(1)}, bf16[2,128,256]{2,1,0:T(8,128)(2,1)S(1)}, u32[]{:S(2)}, u32[]{:S(2)}) collective-permute-start(bf16[2,128,256]{2,1,0:T(8,128)(2,1)S(1)} %pad_maximum_fusion.1), channel_id=1, source_target_pairs={{32,0},{64,32},{96,64},{33,1},{65,33},{97,65},{34,2},{66,34},{98,6... | collective-permute-start | bytes 393224 | tf_op jit(solution)/shard_map/ppermute | solution.py:366
  111.5 4.8 %collective-permute-done.2 = bf16[2,128,256]{2,1,0:T(8,128)(2,1)S(1)} collective-permute-done((bf16[2,128,256]{2,1,0:T(8,128)(2,1)S(1)}, bf16[2,128,256]{2,1,0:T(8,128)(2,1)S(1)}, u32[]{:S(2)}, u32[]{:S(2)}) %collective-permute-start.2) | collective-permute-done | bytes 131104 | tf_op jit(solution)/shard_map/ppermute | solution.py:366
  116.4 0.7 copy.13
  (20 shorter events, 0.3 us)
Async XLA Ops:
  0.6 17.8 %collective-permute-start.1 = (s32[4]{0:T(128)}, s32[4]{0:T(128)S(1)}, u32[]{:S(2)}, u32[]{:S(2)}) collective-permute-start(s32[4]{0:T(128)} %param.9), channel_id=1, source_target_pairs={{0,1},{1,0},{2,3},{3,2},{4,5},{5,4},{6,7},{7,6},{8,9},{9,8},{10,11... | collective-permute-start | bytes 56 | tf_op jit(solution)/shard_map/ppermute | solution.py:333
  1.6 7.8 %collective-permute-start = (bf16[2,128,256]{2,1,0:T(8,128)(2,1)S(1)}, bf16[2,128,256]{2,1,0:T(8,128)(2,1)S(1)}, u32[]{:S(2)}, u32[]{:S(2)}) collective-permute-start(bf16[2,128,256]{2,1,0:T(8,128)(2,1)S(1)} %slice_bitcast_fusion.2), channel_id=1, source_target_pairs={{0,32},{32,64},{64,96},{1,33},{33,65},{65,97},{2,34},{34,66},{66,9... | collective-permute-start | bytes 393224 | tf_op jit(solution)/shard_map/ppermute | solution.py:326
  11.0 7.2 %copy-start.4 = (s32[128]{0:T(128)S(1)}, s32[128]{0:T(128)}, u32[]{:S(2)}) copy-start(s32[128]{0:T(128)} %param.8) | copy-start | bytes 1540
  11.0 7.4 %copy-start.5 = (s32[4]{0:T(128)S(1)}, s32[4]{0:T(128)}, u32[]{:S(2)}) copy-start(s32[4]{0:T(128)} %param.9) | copy-start | bytes 52
  11.0 24.7 %all-to-all-start.1 = ((bf16[16,2,128,128]{3,2,1,0:T(8,128)(2,1)}), bf16[16,2,128,128]{3,2,1,0:T(8,128)(2,1)S(1)}, u32[]{:S(2)}, u32[]{:S(2)}) async-start(bf16[16,2,128,128]{3,2,1,0:T(8,128)(2,1)} %get-tuple-element.42), calls=%async_computation.1 | async-start | bytes 2097152 | tf_op jit(solution)/shard_map/all_to_all | solution.py:331
  18.4 22.8 %copy-start.2 = (bf16[2,128,2048]{2,1,0:T(8,128)(2,1)S(1)}, bf16[2,128,2048]{2,1,0:T(8,128)(2,1)}, u32[]{:S(2)}) copy-start(bf16[2,128,2048]{2,1,0:T(8,128)(2,1)} %do_ref.3) | copy-start | bytes 3145732
  35.7 1.0 copy-start.3
  36.7 4.5 %copy-start = (bf16[2,2,128,256]{3,2,1,0:T(8,128)(2,1)S(1)}, bf16[2,2,128,256]{3,2,1,0:T(8,128)(2,1)}, u32[]{:S(2)}) copy-start(bf16[2,2,128,256]{3,2,1,0:T(8,128)(2,1)} %own_ref.3) | copy-start | bytes 786436
  36.7 4.5 %copy-start.1 = (bf16[2,128,2048]{2,1,0:T(8,128)(2,1)S(1)}, bf16[2,128,2048]{2,1,0:T(8,128)(2,1)}, u32[]{:S(2)}) copy-start(bf16[2,128,2048]{2,1,0:T(8,128)(2,1)} %q_ref.3) | copy-start | bytes 3145732
  36.7 23.0 %all-to-all-start = ((bf16[16,2,128,128]{3,2,1,0:T(8,128)(2,1)}), bf16[16,2,128,128]{3,2,1,0:T(8,128)(2,1)}, u32[]{:S(2)}, u32[]{:S(2)}) async-start(bf16[16,2,128,128]{3,2,1,0:T(8,128)(2,1)} %get-tuple-element.43), calls=%async_computation | async-start | bytes 2097152 | tf_op jit(solution)/shard_map/all_to_all | solution.py:331
  59.7 25.8 %all-to-all-start.2 = ((bf16[16,2,128,128]{3,2,1,0:T(8,128)(2,1)}), bf16[16,2,128,128]{3,2,1,0:T(8,128)(2,1)}, u32[]{:S(2)}, u32[]{:S(2)}) async-start(bf16[16,2,128,128]{3,2,1,0:T(8,128)(2,1)} %get-tuple-element.20), calls=%async_computation.2 | async-start | bytes 2097152 | tf_op jit(solution)/shard_map/all_to_all | solution.py:352
  85.5 21.8 %all-to-all-start.3 = ((bf16[16,2,128,128]{3,2,1,0:T(8,128)(2,1)}), bf16[16,2,128,128]{3,2,1,0:T(8,128)(2,1)S(1)}, u32[]{:S(2)}, u32[]{:S(2)}) async-start(bf16[16,2,128,128]{3,2,1,0:T(8,128)(2,1)} %get-tuple-element.24), calls=%async_computation.3 | async-start | bytes 2097152 | tf_op jit(solution)/shard_map/all_to_all | solution.py:352
  109.5 6.9 %collective-permute-start.2 = (bf16[2,128,256]{2,1,0:T(8,128)(2,1)S(1)}, bf16[2,128,256]{2,1,0:T(8,128)(2,1)S(1)}, u32[]{:S(2)}, u32[]{:S(2)}) collective-permute-start(bf16[2,128,256]{2,1,0:T(8,128)(2,1)S(1)} %pad_maximum_fusion.1), channel_id=1, source_target_pairs={{32,0},{64,32},{96,64},{33,1},{65,33},{97,65},{34,2},{66,34},{98,6... | collective-permute-start | bytes 393224 | tf_op jit(solution)/shard_map/ppermute | solution.py:366

commit v6 on v3

--- a/solution.py
+++ b/solution.py
@@ -20,7 +20,7 @@
 SCALE_LOG2 = SCALE * math.log2(math.e)
 TILE = 256
 SLOTS = 3
-VMEM_LIMIT = 50 * 2**20
+VMEM_LIMIT = 52 * 2**20
 
 NT = (((1,), (1,)), ((), ()))
 
@@ -296,6 +296,38 @@
     )(queries, d_out, far, keys_values, base, starts, near, keep, *earlier)
 
 
+def settle_kernel(place_ref, terms_ref, mine_ref, here_ref, there_ref):
+    for i in range(2):
+        here = mine_ref[i, 0]
+        there = jnp.zeros_like(here)
+        for slot in range(REACH):
+            term = terms_ref[slot, i].astype(jnp.float32)
+            after = (slot > place_ref[0]).astype(jnp.float32)
+            here = here + term * after
+            there = there + term * (1.0 - after)
+        here_ref[i] = here
+        there_ref[i] = there.astype(jnp.bfloat16)
+
+
+def settle(group, place, terms, mine):
+    shape = terms.shape[1:]
+    whole = lambda shape: pl.BlockSpec(shape, lambda: (0,) * len(shape))
+    return pl.pallas_call(
+        settle_kernel,
+        in_specs=[pl.BlockSpec(memory_space=pltpu.SMEM), whole(terms.shape), whole(mine.shape)],
+        out_specs=[whole(shape), whole(shape)],
+        out_shape=[
+            jax.ShapeDtypeStruct(shape, jnp.float32),
+            jax.ShapeDtypeStruct(shape, jnp.bfloat16),
+        ],
+        compiler_params=pltpu.CompilerParams(vmem_limit_bytes=12 * 2**20),
+        cost_estimate=pl.CostEstimate(
+            flops=4 * terms.size, bytes_accessed=2 * terms.size, transcendentals=0
+        ),
+        name=f"settle_{group}",
+    )(place[None], terms, mine)
+
+
 def masks(doc_start, slab, place, places):
     rows = doc_start.shape[0]
     offset = jnp.arange(rows, dtype=jnp.int32)
@@ -353,13 +385,12 @@
         totals.append(terms)
         noisy.append(mine)
     here, there = [], []
-    for terms in totals:
-        terms = terms.astype(jnp.float32)
-        here.append(jnp.sum(jnp.where(after, terms, 0.0), 0))
-        there.append(jnp.sum(jnp.where(after, 0.0, terms), 0).astype(jnp.bfloat16))
+    for group, (terms, mine) in enumerate(zip(totals, noisy)):
+        sums = settle(group, place, terms, mine)
+        here.append(sums[0])
+        there.append(sums[1])
     arrived = lax.ppermute(jnp.concatenate(there, -1), "slab", sooner)
-    clean = jnp.concatenate([a + b[:, 0] for a, b in zip(here, noisy)], -1)
-    clean = clean + arrived.astype(jnp.float32)
+    clean = jnp.concatenate(here, -1) + arrived.astype(jnp.float32)
     grad = jnp.stack([clean, jnp.concatenate([b[:, 1] for b in noisy], -1)], 1)
     return att, dq, grad.astype(jnp.bfloat16)
 

time: 118 us -> 116 us (0.983)
  other arithmetic: 4.06 us -> 1.9 us
    reduce_sum x1 -> x0, other arithmetic: 2.12 us -> none  [local(): here.append(jnp.sum(jnp.where(after, terms, 0.0), 0))]
  transfers between devices with their start and end apart: 7 -> 7, of which waited for: 4 -> 4; matrix products, arithmetic and copies ran while one was open for 3% -> 3% of each run, Pallas kernels for 32% -> 33%
where the time goes in v6:
time: 116 us; the launch traced here: 115 us
  waiting for transfers between devices  39.6 us (34%)
  Pallas kernels  37.9 us (33%)
  starting transfers between devices  31.4 us (27%)
  local copies, waits for them, and re-layouts  3.47 us (3%)
  other arithmetic  1.9 us (2%)
    pallas_call x2, Pallas kernels, attend(): pl.pallas_call(functools.partial(kernel, rows, group), grid=(1,), in_spec...  37.1 us
    all_to_all x2, waiting for transfers between devices, local(): far.append(lax.all_to_all(send, 'place', 0, 0))  16.4 us
    all_to_all x2, starting transfers between devices, local(): terms = lax.all_to_all(back, 'place', 0, 0)  14.3 us
    all_to_all x2, waiting for transfers between devices, local(): terms = lax.all_to_all(back, 'place', 0, 0)  14.3 us
    all_to_all x2, starting transfers between devices, local(): far.append(lax.all_to_all(send, 'place', 0, 0))  11.5 us
    ppermute x1, waiting for transfers between devices, local(): arrived = lax.ppermute(jnp.concatenate(there, -1), 'slab', sooner)  4.79 us
    ppermute x1, waiting for transfers between devices, local(): before = lax.ppermute(own, 'slab', later)  4.15 us
    ppermute x1, starting transfers between devices, local(): before = lax.ppermute(own, 'slab', later)  3.53 us
  transfers between devices with their start and end apart: 7, of which 4 were waited for; matrix products, arithmetic and copies ran while one was open for 3% of the time, Pallas kernels for 33%

profile of v6, /device:TPU:64, one launch (start us, length us, event | category | flops | bytes accessed | tf_op | source)
XLA Modules:
  0.0 115.2 jit_solution(7731326135471903938)
XLA Ops:
  0.6 0.1 collective-permute-start.1
  0.7 0.9 slice_bitcast_fusion
  1.6 3.5 %collective-permute-start = (bf16[2,128,256]{2,1,0:T(8,128)(2,1)S(1)}, bf16[2,128,256]{2,1,0:T(8,128)(2,1)S(1)}, u32[]{:S(2)}, u32[]{:S(2)}) collective-permute-start(bf16[2,128,256]{2,1,0:T(8,128)(2,1)S(1)} %slice_bitcast_fusion), channel_id=1, source_target_pairs={{0,32},{32,64},{64,96},{1,33},{33,65},{65,97},{2,34},{34,66},{66,9... | collective-permute-start | bytes 393224 | tf_op jit(solution)/shard_map/ppermute | solution.py:358
  5.3 4.2 %collective-permute-done = bf16[2,128,256]{2,1,0:T(8,128)(2,1)S(1)} collective-permute-done((bf16[2,128,256]{2,1,0:T(8,128)(2,1)S(1)}, bf16[2,128,256]{2,1,0:T(8,128)(2,1)S(1)}, u32[]{:S(2)}, u32[]{:S(2)}) %collective-permute-start) | collective-permute-done | bytes 131104 | tf_op jit(solution)/shard_map/ppermute | solution.py:358
  9.5 1.5 %broadcast_select_fusion = (bf16[16,2,128,128]{3,2,1,0:T(8,128)(2,1)}, bf16[16,2,128,128]{3,2,1,0:T(8,128)(2,1)}) fusion(pred[16]{0:T(512)(128)(4,1)S(1)} %iota_compare_fusion.1, bf16[2,128,128]{2,1,0:T(8,128)(2,1)S(1)} %get-tuple-element.36, bf16[2,128,128]{2,1,0:T(8,128)(2,1)S(1)} %get-tuple-element.34, bf16[2,128,128]{2,1,0:T(8,128)(2,1)S(1)} %get-tuple-element.37, ...), kind=kLoop, calls=%fused_computation | loop fusion | flops 1048576 | bytes 2359312 | tf_op jit(solution)/shard_map/jit(_where)/select_n | solution.py:362
  11.0 0.0 copy-start.2
  11.0 7.2 %all-to-all-start.1 = ((bf16[16,2,128,128]{3,2,1,0:T(8,128)(2,1)}), bf16[16,2,128,128]{3,2,1,0:T(8,128)(2,1)S(1)}, u32[]{:S(2)}, u32[]{:S(2)}) async-start(bf16[16,2,128,128]{3,2,1,0:T(8,128)(2,1)} %get-tuple-element.40), calls=%async_computation.1 | async-start | bytes 2097152 | tf_op jit(solution)/shard_map/all_to_all | solution.py:363
  18.2 0.0 copy-done.2
  18.2 0.1 compare_and_fusion.1
  18.4 0.0 copy-start.3
  18.4 0.0 collective-permute-done.1
  18.4 0.6 copy-done.3
  19.0 0.1 broadcast_select_fusion.2
  19.1 0.1 broadcast_in_dim.84
  19.2 0.1 reshape.42
  19.3 16.4 %all-to-all-done.1.far_ref = bf16[16,2,128,128]{3,2,1,0:T(8,128)(2,1)S(1)} async-done(((bf16[16,2,128,128]{3,2,1,0:T(8,128)(2,1)}), bf16[16,2,128,128]{3,2,1,0:T(8,128)(2,1)S(1)}, u32[]{:S(2)}, u32[]{:S(2)}) %all-to-all-start.1) | async-done | bytes 1048608 | tf_op jit(solution)/shard_map/all_to_all | solution.py:363
  35.7 0.0 copy-start.1
  35.7 0.0 copy-start
  35.7 1.0 copy-done.1
  36.6 4.3 %all-to-all-start = ((bf16[16,2,128,128]{3,2,1,0:T(8,128)(2,1)}), bf16[16,2,128,128]{3,2,1,0:T(8,128)(2,1)}, u32[]{:S(2)}, u32[]{:S(2)}) async-start(bf16[16,2,128,128]{3,2,1,0:T(8,128)(2,1)} %get-tuple-element.41), calls=%async_computation | async-start | bytes 2097152 | tf_op jit(solution)/shard_map/all_to_all | solution.py:363
  41.0 0.0 copy-done
  41.0 18.5 %attend_0.1 = (bf16[2,128,2048]{2,1,0:T(8,128)(2,1)}, bf16[2,128,2048]{2,1,0:T(8,128)(2,1)}, bf16[16,2,128,128]{3,2,1,0:T(8,128)(2,1)}, f32[2,2,128,128]{3,2,1,0:T(8,128)S(1)}) custom-call(bf16[2,128,2048]{2,1,0:T(8,128)(2,1)} %q_ref.3, bf16[2,128,2048]{2,1,0:T(8,128)(2,1)} %do_ref.3, bf16[16,2,128,128]{3,2,1,0:T(8,128)(2,1)} %copy-done.1, ...), custom_call_target="tpu_custom_call" | custom-call | flops 14495514624 | bytes 6291456 | tf_op jit(solution)/shard_map/attend_0/pallas_call | solution.py:244
  59.5 0.0 all-to-all-done.far_ref
  59.5 7.1 %all-to-all-start.2 = ((bf16[16,2,128,128]{3,2,1,0:T(8,128)(2,1)}), bf16[16,2,128,128]{3,2,1,0:T(8,128)(2,1)S(1)}, u32[]{:S(2)}, u32[]{:S(2)}) async-start(bf16[16,2,128,128]{3,2,1,0:T(8,128)(2,1)} %get-tuple-element.22), calls=%async_computation.2 | async-start | bytes 2097152 | tf_op jit(solution)/shard_map/all_to_all | solution.py:384
  66.6 18.6 %attend_1.1 = (bf16[2,128,2048]{2,1,0:T(8,128)(2,1)}, bf16[2,128,2048]{2,1,0:T(8,128)(2,1)}, bf16[16,2,128,128]{3,2,1,0:T(8,128)(2,1)}, f32[2,2,128,128]{3,2,1,0:T(8,128)S(1)}) custom-call(bf16[2,128,2048]{2,1,0:T(8,128)(2,1)} %q_ref.3, bf16[2,128,2048]{2,1,0:T(8,128)(2,1)} %do_ref.3, ...), custom_call_target="tpu_custom_call", output_to_operand_aliasing={{0}: (8, {}), {1}: (9, {})} | custom-call | flops 14495514624 | bytes 6291456 | tf_op jit(solution)/shard_map/attend_1/pallas_call | solution.py:244
  85.2 0.0 all-to-all-done.2.terms_ref
  85.2 7.2 %all-to-all-start.3 = ((bf16[16,2,128,128]{3,2,1,0:T(8,128)(2,1)}), bf16[16,2,128,128]{3,2,1,0:T(8,128)(2,1)S(1)}, u32[]{:S(2)}, u32[]{:S(2)}) async-start(bf16[16,2,128,128]{3,2,1,0:T(8,128)(2,1)} %get-tuple-element.26), calls=%async_computation.3 | async-start | bytes 2097152 | tf_op jit(solution)/shard_map/all_to_all | solution.py:384
  92.5 0.4 settle_0.1
  92.9 14.3 %all-to-all-done.3.terms_ref = bf16[16,2,128,128]{3,2,1,0:T(8,128)(2,1)S(1)} async-done(((bf16[16,2,128,128]{3,2,1,0:T(8,128)(2,1)}), bf16[16,2,128,128]{3,2,1,0:T(8,128)(2,1)S(1)}, u32[]{:S(2)}, u32[]{:S(2)}) %all-to-all-start.3) | async-done | bytes 1048608 | tf_op jit(solution)/shard_map/all_to_all | solution.py:384
  107.1 0.4 settle_1.1
  107.6 2.0 %collective-permute-start.2 = (bf16[2,128,256]{2,1,0:T(8,128)(2,1)S(1)}, bf16[2,128,256]{2,1,0:T(8,128)(2,1)S(1)}, u32[]{:S(2)}, u32[]{:S(2)}) collective-permute-start(bf16[2,128,256]{2,1,0:T(8,128)(2,1)S(1)} %pad_maximum_fusion.1), channel_id=1, source_target_pairs={{32,0},{64,32},{96,64},{33,1},{65,33},{97,65},{34,2},{66,34},{98,6... | collective-permute-start | bytes 393224 | tf_op jit(solution)/shard_map/ppermute | solution.py:392
  109.7 4.8 %collective-permute-done.2 = bf16[2,128,256]{2,1,0:T(8,128)(2,1)S(1)} collective-permute-done((bf16[2,128,256]{2,1,0:T(8,128)(2,1)S(1)}, bf16[2,128,256]{2,1,0:T(8,128)(2,1)S(1)}, u32[]{:S(2)}, u32[]{:S(2)}) %collective-permute-start.2) | collective-permute-done | bytes 131104 | tf_op jit(solution)/shard_map/ppermute | solution.py:392
  114.5 0.7 copy.12
  (18 shorter events, 0.3 us)
Async XLA Ops:
  0.6 17.8 %collective-permute-start.1 = (s32[4]{0:T(128)}, s32[4]{0:T(128)S(1)}, u32[]{:S(2)}, u32[]{:S(2)}) collective-permute-start(s32[4]{0:T(128)} %param.9), channel_id=1, source_target_pairs={{0,1},{1,0},{2,3},{3,2},{4,5},{5,4},{6,7},{7,6},{8,9},{9,8},{10,11... | collective-permute-start | bytes 56 | tf_op jit(solution)/shard_map/ppermute | solution.py:365
  1.6 7.8 %collective-permute-start = (bf16[2,128,256]{2,1,0:T(8,128)(2,1)S(1)}, bf16[2,128,256]{2,1,0:T(8,128)(2,1)S(1)}, u32[]{:S(2)}, u32[]{:S(2)}) collective-permute-start(bf16[2,128,256]{2,1,0:T(8,128)(2,1)S(1)} %slice_bitcast_fusion), channel_id=1, source_target_pairs={{0,32},{32,64},{64,96},{1,33},{33,65},{65,97},{2,34},{34,66},{66,9... | collective-permute-start | bytes 393224 | tf_op jit(solution)/shard_map/ppermute | solution.py:358
  11.0 7.2 %copy-start.2 = (s32[128]{0:T(128)S(1)}, s32[128]{0:T(128)}, u32[]{:S(2)}) copy-start(s32[128]{0:T(128)} %param.8) | copy-start | bytes 1540
  11.0 24.7 %all-to-all-start.1 = ((bf16[16,2,128,128]{3,2,1,0:T(8,128)(2,1)}), bf16[16,2,128,128]{3,2,1,0:T(8,128)(2,1)S(1)}, u32[]{:S(2)}, u32[]{:S(2)}) async-start(bf16[16,2,128,128]{3,2,1,0:T(8,128)(2,1)} %get-tuple-element.40), calls=%async_computation.1 | async-start | bytes 2097152 | tf_op jit(solution)/shard_map/all_to_all | solution.py:363
  18.4 0.7 copy-start.3
  35.7 1.0 copy-start.1
  35.7 5.3 %copy-start = (bf16[2,2,128,256]{3,2,1,0:T(8,128)(2,1)S(1)}, bf16[2,2,128,256]{3,2,1,0:T(8,128)(2,1)}, u32[]{:S(2)}) copy-start(bf16[2,2,128,256]{3,2,1,0:T(8,128)(2,1)} %own_ref.3) | copy-start | bytes 786436
  36.6 22.9 %all-to-all-start = ((bf16[16,2,128,128]{3,2,1,0:T(8,128)(2,1)}), bf16[16,2,128,128]{3,2,1,0:T(8,128)(2,1)}, u32[]{:S(2)}, u32[]{:S(2)}) async-start(bf16[16,2,128,128]{3,2,1,0:T(8,128)(2,1)} %get-tuple-element.41), calls=%async_computation | async-start | bytes 2097152 | tf_op jit(solution)/shard_map/all_to_all | solution.py:363
  59.5 25.7 %all-to-all-start.2 = ((bf16[16,2,128,128]{3,2,1,0:T(8,128)(2,1)}), bf16[16,2,128,128]{3,2,1,0:T(8,128)(2,1)S(1)}, u32[]{:S(2)}, u32[]{:S(2)}) async-start(bf16[16,2,128,128]{3,2,1,0:T(8,128)(2,1)} %get-tuple-element.22), calls=%async_computation.2 | async-start | bytes 2097152 | tf_op jit(solution)/shard_map/all_to_all | solution.py:384
  85.2 21.9 %all-to-all-start.3 = ((bf16[16,2,128,128]{3,2,1,0:T(8,128)(2,1)}), bf16[16,2,128,128]{3,2,1,0:T(8,128)(2,1)S(1)}, u32[]{:S(2)}, u32[]{:S(2)}) async-start(bf16[16,2,128,128]{3,2,1,0:T(8,128)(2,1)} %get-tuple-element.26), calls=%async_computation.3 | async-start | bytes 2097152 | tf_op jit(solution)/shard_map/all_to_all | solution.py:384
  107.6 6.9 %collective-permute-start.2 = (bf16[2,128,256]{2,1,0:T(8,128)(2,1)S(1)}, bf16[2,128,256]{2,1,0:T(8,128)(2,1)S(1)}, u32[]{:S(2)}, u32[]{:S(2)}) collective-permute-start(bf16[2,128,256]{2,1,0:T(8,128)(2,1)S(1)} %pad_maximum_fusion.1), channel_id=1, source_target_pairs={{32,0},{64,32},{96,64},{33,1},{65,33},{97,65},{34,2},{66,34},{98,6... | collective-permute-start | bytes 393224 | tf_op jit(solution)/shard_map/ppermute | solution.py:392
